TPU v7x, 256 devices: a whole 4x4x8 slice. The times are simulated.
256 devices in a mesh: tm: 32 (over z, x), space: 8 (over y, core).
Axes of the slice: x: 4, y: 4, z: 8, core: 2. Of those that a mesh axis runs over, the one named last changes fastest.
Arguments:
- sources: float32 [64, 4, 1024, 256], P('tm', None, 'space'), may hold values from -36 to 36
- starts: float32 [64, 1024, 256], P('tm', 'space'), may hold values from -24 to 24
- coupling: float32 [1024], P('space'), may hold values from 0.05 to 0.25
- classes: int32 [1024, 2], P('space'), may hold values from 0 to 3
- inverses: float32 [4, 128, 128], replicated, may hold values from 0 to 1
- coarse_rate: float32 [4, 128], replicated, may hold values from 0.002 to 0.5
Outputs:
- states: float32 [64, 4, 1024, 256], P('tm', None, 'space')
All inputs are finite; a program needn't handle non-finite values.
Results may differ from a plain program's by a relative error of at most 0.0003.
Values sent between devices are 32-bit elements; how exact they have to be, the bound alone decides.
No kernel may reach another device: no remote copies, remote signals or barrier semaphores. Data moves between devices by JAX's collectives and lax.ppermute only.
A program may use at most 64 MiB of HBM per device.

v0:
```python
import jax
import jax.numpy as jnp
from jax import lax
from jax.sharding import PartitionSpec as P

LB = 128
STEPS = 4


def with_halo(x, sides, width):
    for axis, dim in sides:
        count, length = (lax.axis_size(axis), x.shape[dim])
        up = [(i, (i + 1) % count) for i in range(count - 1)]
        down = [(j, i) for i, j in up]
        last = lax.slice_in_dim(x, length - width, length, axis=dim)
        first = lax.slice_in_dim(x, 0, width, axis=dim)
        before = lax.ppermute(last, axis, up)
        after = lax.ppermute(first, axis, down)
        x = jnp.concatenate([before, x, after], axis=dim)
    return x


def passed_along(block, axis, distance):
    devices = range(lax.axis_size(axis))
    route = [(i - distance, i) for i in devices if i - distance in devices]
    return lax.ppermute(block, axis, route)


def advance(field, source, coupling, classes, inverses):
    padded = with_halo(field, (("space", 1),), 1)
    rhs = field + coupling[None, :, None] * (padded[:, :-2] + padded[:, 2:]) + source
    group_count, row_count, line_len = rhs.shape
    blocked = rhs.reshape(group_count, row_count, line_len // LB, LB)
    every_class = jnp.einsum("krbj,cij->ckrbi", blocked, inverses, precision=lax.Precision.HIGHEST)
    result = every_class[0]
    for category in range(1, inverses.shape[0]):
        result = jnp.where(classes[None, :, :, None] == category, every_class[category], result)
    return result.reshape(group_count, row_count, line_len)


def shards(sources, starts, coupling, classes, inverses, coarse_rate):
    group_count = starts.shape[0]
    first_device = lax.axis_index("tm") == 0
    rates = jnp.zeros((classes.shape[0], classes.shape[1], LB), jnp.float32)
    for category in range(inverses.shape[0]):
        rates = jnp.where(
            classes[:, :, None] == category, coarse_rate[category][None, None, :], rates
        )
    decay = jnp.exp(-rates).reshape(starts.shape[1], starts.shape[2])
    fine_state = starts
    for substep in range(STEPS - 1):
        fine_state = advance(fine_state, sources[:, substep], coupling, classes, inverses)
    ends = advance(fine_state, sources[:, STEPS - 1], coupling, classes, inverses)
    incoming = passed_along(ends[-1], "tm", 1)
    entry = jnp.where(first_device, starts[0], incoming)
    fine_state = jnp.concatenate([entry[None], ends[:-1]], axis=0)
    for substep in range(STEPS - 1):
        fine_state = advance(fine_state, sources[:, substep], coupling, classes, inverses)
    resid = advance(fine_state, sources[:, STEPS - 1], coupling, classes, inverses) - ends

    def chain_from(carried):
        outputs = []
        for group in range(group_count):
            carried = decay * carried + resid[group]
            outputs.append(carried)
        return jnp.stack(outputs, axis=0)

    zeros_field = jnp.zeros_like(decay)

    def relay_turn(turn_index, carried):
        return passed_along(chain_from(carried)[-1], "tm", 1)

    entering = lax.fori_loop(0, lax.axis_size("tm") - 1, relay_turn, zeros_field)
    errors = chain_from(entering)
    finals = ends + errors
    previous = passed_along(finals[-1], "tm", 1)
    entry = jnp.where(first_device, starts[0], previous)
    fine_state = jnp.concatenate([entry[None], finals[:-1]], axis=0)
    collected = []
    for substep in range(STEPS - 1):
        fine_state = advance(fine_state, sources[:, substep], coupling, classes, inverses)
        collected.append(fine_state)
    collected.append(finals)
    return jnp.stack(collected, axis=1)


def solution(mesh):
    in_specs = (
        P("tm", None, "space", None),
        P("tm", "space", None),
        P("space"),
        P("space", None),
        P(),
        P(),
    )
    out_specs = P("tm", None, "space", None)
    return jax.shard_map(shards, mesh=mesh, in_specs=in_specs, out_specs=out_specs, check_vma=False)
```

profile of v0, /device:TPU:152, one launch (start us, length us, event | category | flops | bytes accessed | tf_op | source)
XLA Modules:
  0.0 475.1 jit_solution(7762681052797429370)
XLA Ops:
  7.2 3.8 collective-permute-done.1
  18.5 3.8 collective-permute-done.3
  25.8 2.4 collective-permute-start.5
  29.7 3.8 collective-permute-done.5
  40.8 3.8 collective-permute-done.7
  46.0 3.4 collective-permute-start.9
  49.4 6.8 %collective-permute-done.9 = f32[128,256]{0,1:T(8,128)S(1)} collective-permute-done((f32[128,256]{0,1:T(8,128)S(1)}, f32[128,256]{0,1:T(8,128)S(1)}, u32[]{:S(2)}, u32[]{:S(2)}) %collective-permute-start.9) | collective-permute-done | bytes 131104 | tf_op jit(solution)/shard_map/ppermute | solution.py:26
  62.2 3.8 collective-permute-done.10
  73.4 3.8 collective-permute-done.12
  80.7 2.6 collective-permute-start.14
  84.6 3.8 collective-permute-done.14
  95.8 3.8 collective-permute-done.16
  101.3 328.2 %while.11 = (s32[]{:T(128)}, f32[128,256]{0,1:T(8,128)S(1)}, f32[2,128,256]{1,2,0:T(8,128)S(1)}, pred[128,2]{0,1:T(4,128)(4,1)S(1)}, pred[128,2]{0,1:T(4,128)(4,...) while((s32[]{:T(128)}, f32[128,256]{0,1:T(8,128)S(1)}, ...), condition=%wide.region_1.2_spmd.clone, body=%wide.region_0.1_spmd.clone.sunk | while | flops 294914 | bytes 1053853 | solution.py:73
  103.5 8.2 %collective-permute-done = f32[128,256]{0,1:T(8,128)S(1)} collective-permute-done((f32[128,256]{0,1:T(8,128)S(1)}, f32[128,256]{0,1:T(8,128)S(1)}, u32[]{:S(2)}, u32[]{:S(2)}) %collective-permute-start) | collective-permute-done | bytes 131104 | tf_op jit(solution)/shard_map/while/body/eval_jaxpr/ppermute | solution.py:26
  113.9 8.2 %collective-permute-done = f32[128,256]{0,1:T(8,128)S(1)} collective-permute-done((f32[128,256]{0,1:T(8,128)S(1)}, f32[128,256]{0,1:T(8,128)S(1)}, u32[]{:S(2)}, u32[]{:S(2)}) %collective-permute-start) | collective-permute-done | bytes 131104 | tf_op jit(solution)/shard_map/while/body/eval_jaxpr/ppermute | solution.py:26
  124.3 8.2 %collective-permute-done = f32[128,256]{0,1:T(8,128)S(1)} collective-permute-done((f32[128,256]{0,1:T(8,128)S(1)}, f32[128,256]{0,1:T(8,128)S(1)}, u32[]{:S(2)}, u32[]{:S(2)}) %collective-permute-start) | collective-permute-done | bytes 131104 | tf_op jit(solution)/shard_map/while/body/eval_jaxpr/ppermute | solution.py:26
  134.7 8.6 %collective-permute-done = f32[128,256]{0,1:T(8,128)S(1)} collective-permute-done((f32[128,256]{0,1:T(8,128)S(1)}, f32[128,256]{0,1:T(8,128)S(1)}, u32[]{:S(2)}, u32[]{:S(2)}) %collective-permute-start) | collective-permute-done | bytes 131104 | tf_op jit(solution)/shard_map/while/body/eval_jaxpr/ppermute | solution.py:26
  145.4 9.6 %collective-permute-done = f32[128,256]{0,1:T(8,128)S(1)} collective-permute-done((f32[128,256]{0,1:T(8,128)S(1)}, f32[128,256]{0,1:T(8,128)S(1)}, u32[]{:S(2)}, u32[]{:S(2)}) %collective-permute-start) | collective-permute-done | bytes 131104 | tf_op jit(solution)/shard_map/while/body/eval_jaxpr/ppermute | solution.py:26
  157.1 8.7 %collective-permute-done = f32[128,256]{0,1:T(8,128)S(1)} collective-permute-done((f32[128,256]{0,1:T(8,128)S(1)}, f32[128,256]{0,1:T(8,128)S(1)}, u32[]{:S(2)}, u32[]{:S(2)}) %collective-permute-start) | collective-permute-done | bytes 131104 | tf_op jit(solution)/shard_map/while/body/eval_jaxpr/ppermute | solution.py:26
  168.0 8.2 %collective-permute-done = f32[128,256]{0,1:T(8,128)S(1)} collective-permute-done((f32[128,256]{0,1:T(8,128)S(1)}, f32[128,256]{0,1:T(8,128)S(1)}, u32[]{:S(2)}, u32[]{:S(2)}) %collective-permute-start) | collective-permute-done | bytes 131104 | tf_op jit(solution)/shard_map/while/body/eval_jaxpr/ppermute | solution.py:26
  178.4 8.2 %collective-permute-done = f32[128,256]{0,1:T(8,128)S(1)} collective-permute-done((f32[128,256]{0,1:T(8,128)S(1)}, f32[128,256]{0,1:T(8,128)S(1)}, u32[]{:S(2)}, u32[]{:S(2)}) %collective-permute-start) | collective-permute-done | bytes 131104 | tf_op jit(solution)/shard_map/while/body/eval_jaxpr/ppermute | solution.py:26
  188.8 8.2 %collective-permute-done = f32[128,256]{0,1:T(8,128)S(1)} collective-permute-done((f32[128,256]{0,1:T(8,128)S(1)}, f32[128,256]{0,1:T(8,128)S(1)}, u32[]{:S(2)}, u32[]{:S(2)}) %collective-permute-start) | collective-permute-done | bytes 131104 | tf_op jit(solution)/shard_map/while/body/eval_jaxpr/ppermute | solution.py:26
  199.2 8.2 %collective-permute-done = f32[128,256]{0,1:T(8,128)S(1)} collective-permute-done((f32[128,256]{0,1:T(8,128)S(1)}, f32[128,256]{0,1:T(8,128)S(1)}, u32[]{:S(2)}, u32[]{:S(2)}) %collective-permute-start) | collective-permute-done | bytes 131104 | tf_op jit(solution)/shard_map/while/body/eval_jaxpr/ppermute | solution.py:26
  209.6 8.2 %collective-permute-done = f32[128,256]{0,1:T(8,128)S(1)} collective-permute-done((f32[128,256]{0,1:T(8,128)S(1)}, f32[128,256]{0,1:T(8,128)S(1)}, u32[]{:S(2)}, u32[]{:S(2)}) %collective-permute-start) | collective-permute-done | bytes 131104 | tf_op jit(solution)/shard_map/while/body/eval_jaxpr/ppermute | solution.py:26
  220.0 8.2 %collective-permute-done = f32[128,256]{0,1:T(8,128)S(1)} collective-permute-done((f32[128,256]{0,1:T(8,128)S(1)}, f32[128,256]{0,1:T(8,128)S(1)}, u32[]{:S(2)}, u32[]{:S(2)}) %collective-permute-start) | collective-permute-done | bytes 131104 | tf_op jit(solution)/shard_map/while/body/eval_jaxpr/ppermute | solution.py:26
  230.4 9.1 %collective-permute-done = f32[128,256]{0,1:T(8,128)S(1)} collective-permute-done((f32[128,256]{0,1:T(8,128)S(1)}, f32[128,256]{0,1:T(8,128)S(1)}, u32[]{:S(2)}, u32[]{:S(2)}) %collective-permute-start) | collective-permute-done | bytes 131104 | tf_op jit(solution)/shard_map/while/body/eval_jaxpr/ppermute | solution.py:26
  241.7 9.0 %collective-permute-done = f32[128,256]{0,1:T(8,128)S(1)} collective-permute-done((f32[128,256]{0,1:T(8,128)S(1)}, f32[128,256]{0,1:T(8,128)S(1)}, u32[]{:S(2)}, u32[]{:S(2)}) %collective-permute-start) | collective-permute-done | bytes 131104 | tf_op jit(solution)/shard_map/while/body/eval_jaxpr/ppermute | solution.py:26
  252.9 8.2 %collective-permute-done = f32[128,256]{0,1:T(8,128)S(1)} collective-permute-done((f32[128,256]{0,1:T(8,128)S(1)}, f32[128,256]{0,1:T(8,128)S(1)}, u32[]{:S(2)}, u32[]{:S(2)}) %collective-permute-start) | collective-permute-done | bytes 131104 | tf_op jit(solution)/shard_map/while/body/eval_jaxpr/ppermute | solution.py:26
  263.3 8.2 %collective-permute-done = f32[128,256]{0,1:T(8,128)S(1)} collective-permute-done((f32[128,256]{0,1:T(8,128)S(1)}, f32[128,256]{0,1:T(8,128)S(1)}, u32[]{:S(2)}, u32[]{:S(2)}) %collective-permute-start) | collective-permute-done | bytes 131104 | tf_op jit(solution)/shard_map/while/body/eval_jaxpr/ppermute | solution.py:26
  273.7 8.2 %collective-permute-done = f32[128,256]{0,1:T(8,128)S(1)} collective-permute-done((f32[128,256]{0,1:T(8,128)S(1)}, f32[128,256]{0,1:T(8,128)S(1)}, u32[]{:S(2)}, u32[]{:S(2)}) %collective-permute-start) | collective-permute-done | bytes 131104 | tf_op jit(solution)/shard_map/while/body/eval_jaxpr/ppermute | solution.py:26
  284.1 8.2 %collective-permute-done = f32[128,256]{0,1:T(8,128)S(1)} collective-permute-done((f32[128,256]{0,1:T(8,128)S(1)}, f32[128,256]{0,1:T(8,128)S(1)}, u32[]{:S(2)}, u32[]{:S(2)}) %collective-permute-start) | collective-permute-done | bytes 131104 | tf_op jit(solution)/shard_map/while/body/eval_jaxpr/ppermute | solution.py:26
  294.5 8.2 %collective-permute-done = f32[128,256]{0,1:T(8,128)S(1)} collective-permute-done((f32[128,256]{0,1:T(8,128)S(1)}, f32[128,256]{0,1:T(8,128)S(1)}, u32[]{:S(2)}, u32[]{:S(2)}) %collective-permute-start) | collective-permute-done | bytes 131104 | tf_op jit(solution)/shard_map/while/body/eval_jaxpr/ppermute | solution.py:26
  304.9 8.2 %collective-permute-done = f32[128,256]{0,1:T(8,128)S(1)} collective-permute-done((f32[128,256]{0,1:T(8,128)S(1)}, f32[128,256]{0,1:T(8,128)S(1)}, u32[]{:S(2)}, u32[]{:S(2)}) %collective-permute-start) | collective-permute-done | bytes 131104 | tf_op jit(solution)/shard_map/while/body/eval_jaxpr/ppermute | solution.py:26
  315.3 8.7 %collective-permute-done = f32[128,256]{0,1:T(8,128)S(1)} collective-permute-done((f32[128,256]{0,1:T(8,128)S(1)}, f32[128,256]{0,1:T(8,128)S(1)}, u32[]{:S(2)}, u32[]{:S(2)}) %collective-permute-start) | collective-permute-done | bytes 131104 | tf_op jit(solution)/shard_map/while/body/eval_jaxpr/ppermute | solution.py:26
  326.1 9.4 %collective-permute-done = f32[128,256]{0,1:T(8,128)S(1)} collective-permute-done((f32[128,256]{0,1:T(8,128)S(1)}, f32[128,256]{0,1:T(8,128)S(1)}, u32[]{:S(2)}, u32[]{:S(2)}) %collective-permute-start) | collective-permute-done | bytes 131104 | tf_op jit(solution)/shard_map/while/body/eval_jaxpr/ppermute | solution.py:26
  337.7 8.6 %collective-permute-done = f32[128,256]{0,1:T(8,128)S(1)} collective-permute-done((f32[128,256]{0,1:T(8,128)S(1)}, f32[128,256]{0,1:T(8,128)S(1)}, u32[]{:S(2)}, u32[]{:S(2)}) %collective-permute-start) | collective-permute-done | bytes 131104 | tf_op jit(solution)/shard_map/while/body/eval_jaxpr/ppermute | solution.py:26
  348.4 8.2 %collective-permute-done = f32[128,256]{0,1:T(8,128)S(1)} collective-permute-done((f32[128,256]{0,1:T(8,128)S(1)}, f32[128,256]{0,1:T(8,128)S(1)}, u32[]{:S(2)}, u32[]{:S(2)}) %collective-permute-start) | collective-permute-done | bytes 131104 | tf_op jit(solution)/shard_map/while/body/eval_jaxpr/ppermute | solution.py:26
  358.8 8.2 %collective-permute-done = f32[128,256]{0,1:T(8,128)S(1)} collective-permute-done((f32[128,256]{0,1:T(8,128)S(1)}, f32[128,256]{0,1:T(8,128)S(1)}, u32[]{:S(2)}, u32[]{:S(2)}) %collective-permute-start) | collective-permute-done | bytes 131104 | tf_op jit(solution)/shard_map/while/body/eval_jaxpr/ppermute | solution.py:26
  369.2 8.2 %collective-permute-done = f32[128,256]{0,1:T(8,128)S(1)} collective-permute-done((f32[128,256]{0,1:T(8,128)S(1)}, f32[128,256]{0,1:T(8,128)S(1)}, u32[]{:S(2)}, u32[]{:S(2)}) %collective-permute-start) | collective-permute-done | bytes 131104 | tf_op jit(solution)/shard_map/while/body/eval_jaxpr/ppermute | solution.py:26
  379.6 8.2 %collective-permute-done = f32[128,256]{0,1:T(8,128)S(1)} collective-permute-done((f32[128,256]{0,1:T(8,128)S(1)}, f32[128,256]{0,1:T(8,128)S(1)}, u32[]{:S(2)}, u32[]{:S(2)}) %collective-permute-start) | collective-permute-done | bytes 131104 | tf_op jit(solution)/shard_map/while/body/eval_jaxpr/ppermute | solution.py:26
  390.0 8.2 %collective-permute-done = f32[128,256]{0,1:T(8,128)S(1)} collective-permute-done((f32[128,256]{0,1:T(8,128)S(1)}, f32[128,256]{0,1:T(8,128)S(1)}, u32[]{:S(2)}, u32[]{:S(2)}) %collective-permute-start) | collective-permute-done | bytes 131104 | tf_op jit(solution)/shard_map/while/body/eval_jaxpr/ppermute | solution.py:26
  400.4 8.2 %collective-permute-done = f32[128,256]{0,1:T(8,128)S(1)} collective-permute-done((f32[128,256]{0,1:T(8,128)S(1)}, f32[128,256]{0,1:T(8,128)S(1)}, u32[]{:S(2)}, u32[]{:S(2)}) %collective-permute-start) | collective-permute-done | bytes 131104 | tf_op jit(solution)/shard_map/while/body/eval_jaxpr/ppermute | solution.py:26
  410.8 8.2 %collective-permute-done = f32[128,256]{0,1:T(8,128)S(1)} collective-permute-done((f32[128,256]{0,1:T(8,128)S(1)}, f32[128,256]{0,1:T(8,128)S(1)}, u32[]{:S(2)}, u32[]{:S(2)}) %collective-permute-start) | collective-permute-done | bytes 131104 | tf_op jit(solution)/shard_map/while/body/eval_jaxpr/ppermute | solution.py:26
  421.2 8.2 %collective-permute-done = f32[128,256]{0,1:T(8,128)S(1)} collective-permute-done((f32[128,256]{0,1:T(8,128)S(1)}, f32[128,256]{0,1:T(8,128)S(1)}, u32[]{:S(2)}, u32[]{:S(2)}) %collective-permute-start) | collective-permute-done | bytes 131104 | tf_op jit(solution)/shard_map/while/body/eval_jaxpr/ppermute | solution.py:26
  431.7 8.3 %collective-permute-done.18 = f32[128,256]{0,1:T(8,128)S(1)} collective-permute-done((f32[128,256]{0,1:T(8,128)S(1)}, f32[128,256]{0,1:T(8,128)S(1)}, u32[]{:S(2)}, u32[]{:S(2)}) %collective-permute-start.18) | collective-permute-done | bytes 131104 | tf_op jit(solution)/shard_map/ppermute | solution.py:26
  445.9 3.8 collective-permute-done.19
  457.1 3.8 collective-permute-done.21
  468.3 3.8 collective-permute-done.23
  (183 shorter events, 146.7 us)
Async XLA Ops:
  0.9 6.3 %collective-permute-start.2 = (f32[2,1,256]{1,2,0:T(8,128)S(1)}, f32[2,1,256]{1,2,0:T(8,128)S(1)}, u32[]{:S(2)}, u32[]{:S(2)}) collective-permute-start(f32[2,1,256]{1,2,0:T(8,128)S(1)} %copy.93), channel_id=1, source_target_pairs={{1,0},{2,1},{3,2},{4,3},{5,4},{6,5},{7,6},{9,8},{10,9},{11,10},{12... | collective-permute-start | bytes 6152 | tf_op jit(solution)/shard_map/ppermute | solution.py:18
  3.2 7.8 %collective-permute-start.1 = (f32[2,1,256]{1,2,0:T(8,128)S(1)}, f32[2,1,256]{1,2,0:T(8,128)S(1)}, u32[]{:S(2)}, u32[]{:S(2)}) collective-permute-start(f32[2,1,256]{1,2,0:T(8,128)S(1)} %copy.91), channel_id=1, source_target_pairs={{0,1},{1,2},{2,3},{3,4},{4,5},{5,6},{6,7},{8,9},{9,10},{10,11},{11... | collective-permute-start | bytes 6152 | tf_op jit(solution)/shard_map/ppermute | solution.py:17
  12.7 5.8 %collective-permute-start.4 = (f32[2,1,256]{1,2,0:T(8,128)S(1)}, f32[2,1,256]{1,2,0:T(8,128)S(1)}, u32[]{:S(2)}, u32[]{:S(2)}) collective-permute-start(f32[2,1,256]{1,2,0:T(8,128)S(1)} %get-tuple-element.157), channel_id=1, source_target_pairs={{1,0},{2,1},{3,2},{4,3},{5,4},{6,5},{7,6},{9,8},{10,9},{11,10},{12... | collective-permute-start | bytes 6152 | tf_op jit(solution)/shard_map/ppermute | solution.py:18
  14.6 7.7 %collective-permute-start.3 = (f32[2,1,256]{1,2,0:T(8,128)S(1)}, f32[2,1,256]{1,2,0:T(8,128)S(1)}, u32[]{:S(2)}, u32[]{:S(2)}) collective-permute-start(f32[2,1,256]{1,2,0:T(8,128)S(1)} %get-tuple-element.156), channel_id=1, source_target_pairs={{0,1},{1,2},{2,3},{3,4},{4,5},{5,6},{6,7},{8,9},{9,10},{10,11},{11... | collective-permute-start | bytes 6152 | tf_op jit(solution)/shard_map/ppermute | solution.py:17
  23.9 5.8 %collective-permute-start.6 = (f32[2,1,256]{1,2,0:T(8,128)S(1)}, f32[2,1,256]{1,2,0:T(8,128)S(1)}, u32[]{:S(2)}, u32[]{:S(2)}) collective-permute-start(f32[2,1,256]{1,2,0:T(8,128)S(1)} %get-tuple-element.155), channel_id=1, source_target_pairs={{1,0},{2,1},{3,2},{4,3},{5,4},{6,5},{7,6},{9,8},{10,9},{11,10},{12... | collective-permute-start | bytes 6152 | tf_op jit(solution)/shard_map/ppermute | solution.py:18
  25.8 7.7 %collective-permute-start.5 = (f32[2,1,256]{1,2,0:T(8,128)S(1)}, f32[2,1,256]{1,2,0:T(8,128)S(1)}, u32[]{:S(2)}, u32[]{:S(2)}) collective-permute-start(f32[2,1,256]{1,2,0:T(8,128)S(1)} %get-tuple-element.154), channel_id=1, source_target_pairs={{0,1},{1,2},{2,3},{3,4},{4,5},{5,6},{6,7},{8,9},{9,10},{10,11},{11... | collective-permute-start | bytes 6152 | tf_op jit(solution)/shard_map/ppermute | solution.py:17
  37.0 7.7 %collective-permute-start.7 = (f32[2,1,256]{1,2,0:T(8,128)S(1)}, f32[2,1,256]{1,2,0:T(8,128)S(1)}, u32[]{:S(2)}, u32[]{:S(2)}) collective-permute-start(f32[2,1,256]{1,2,0:T(8,128)S(1)} %get-tuple-element.152), channel_id=1, source_target_pairs={{0,1},{1,2},{2,3},{3,4},{4,5},{5,6},{6,7},{8,9},{9,10},{10,11},{11... | collective-permute-start | bytes 6152 | tf_op jit(solution)/shard_map/ppermute | solution.py:17
  46.0 10.2 %collective-permute-start.9 = (f32[128,256]{0,1:T(8,128)S(1)}, f32[128,256]{0,1:T(8,128)S(1)}, u32[]{:S(2)}, u32[]{:S(2)}) collective-permute-start(f32[128,256]{0,1:T(8,128)S(1)} %bitcast.482), channel_id=1, source_target_pairs={{0,8},{8,16},{16,24},{24,32},{32,40},{40,48},{48,56},{56,64},{64,7... | collective-permute-start | bytes 393224 | tf_op jit(solution)/shard_map/ppermute | solution.py:26
  58.3 7.7 %collective-permute-start.10 = (f32[2,1,256]{1,2,0:T(8,128)S(1)}, f32[2,1,256]{1,2,0:T(8,128)S(1)}, u32[]{:S(2)}, u32[]{:S(2)}) collective-permute-start(f32[2,1,256]{1,2,0:T(8,128)S(1)} %get-tuple-element.148), channel_id=1, source_target_pairs={{0,1},{1,2},{2,3},{3,4},{4,5},{5,6},{6,7},{8,9},{9,10},{10,11},{11... | collective-permute-start | bytes 6152 | tf_op jit(solution)/shard_map/ppermute | solution.py:17
  67.6 5.8 %collective-permute-start.13 = (f32[2,1,256]{1,2,0:T(8,128)S(1)}, f32[2,1,256]{1,2,0:T(8,128)S(1)}, u32[]{:S(2)}, u32[]{:S(2)}) collective-permute-start(f32[2,1,256]{1,2,0:T(8,128)S(1)} %get-tuple-element.147), channel_id=1, source_target_pairs={{1,0},{2,1},{3,2},{4,3},{5,4},{6,5},{7,6},{9,8},{10,9},{11,10},{12... | collective-permute-start | bytes 6152 | tf_op jit(solution)/shard_map/ppermute | solution.py:18
  69.5 7.7 %collective-permute-start.12 = (f32[2,1,256]{1,2,0:T(8,128)S(1)}, f32[2,1,256]{1,2,0:T(8,128)S(1)}, u32[]{:S(2)}, u32[]{:S(2)}) collective-permute-start(f32[2,1,256]{1,2,0:T(8,128)S(1)} %get-tuple-element.146), channel_id=1, source_target_pairs={{0,1},{1,2},{2,3},{3,4},{4,5},{5,6},{6,7},{8,9},{9,10},{10,11},{11... | collective-permute-start | bytes 6152 | tf_op jit(solution)/shard_map/ppermute | solution.py:17
  80.7 7.7 %collective-permute-start.14 = (f32[2,1,256]{1,2,0:T(8,128)S(1)}, f32[2,1,256]{1,2,0:T(8,128)S(1)}, u32[]{:S(2)}, u32[]{:S(2)}) collective-permute-start(f32[2,1,256]{1,2,0:T(8,128)S(1)} %get-tuple-element.144), channel_id=1, source_target_pairs={{0,1},{1,2},{2,3},{3,4},{4,5},{5,6},{6,7},{8,9},{9,10},{10,11},{11... | collective-permute-start | bytes 6152 | tf_op jit(solution)/shard_map/ppermute | solution.py:17
  91.9 7.7 %collective-permute-start.16 = (f32[2,1,256]{1,2,0:T(8,128)S(1)}, f32[2,1,256]{1,2,0:T(8,128)S(1)}, u32[]{:S(2)}, u32[]{:S(2)}) collective-permute-start(f32[2,1,256]{1,2,0:T(8,128)S(1)} %get-tuple-element.142), channel_id=1, source_target_pairs={{0,1},{1,2},{2,3},{3,4},{4,5},{5,6},{6,7},{8,9},{9,10},{10,11},{11... | collective-permute-start | bytes 6152 | tf_op jit(solution)/shard_map/ppermute | solution.py:17
  101.5 10.2 %collective-permute-start = (f32[128,256]{0,1:T(8,128)S(1)}, f32[128,256]{0,1:T(8,128)S(1)}, u32[]{:S(2)}, u32[]{:S(2)}) collective-permute-start(f32[128,256]{0,1:T(8,128)S(1)} %bitcast_add_fusion.3), channel_id=1, source_target_pairs={{0,8},{8,16},{16,24},{24,32},{32,40},{40,48},{48,56},{56,64},{64,7... | collective-permute-start | bytes 393224 | tf_op jit(solution)/shard_map/while/body/eval_jaxpr/ppermute | solution.py:26
  111.9 10.2 %collective-permute-start = (f32[128,256]{0,1:T(8,128)S(1)}, f32[128,256]{0,1:T(8,128)S(1)}, u32[]{:S(2)}, u32[]{:S(2)}) collective-permute-start(f32[128,256]{0,1:T(8,128)S(1)} %bitcast_add_fusion.3), channel_id=1, source_target_pairs={{0,8},{8,16},{16,24},{24,32},{32,40},{40,48},{48,56},{56,64},{64,7... | collective-permute-start | bytes 393224 | tf_op jit(solution)/shard_map/while/body/eval_jaxpr/ppermute | solution.py:26
  122.3 10.2 %collective-permute-start = (f32[128,256]{0,1:T(8,128)S(1)}, f32[128,256]{0,1:T(8,128)S(1)}, u32[]{:S(2)}, u32[]{:S(2)}) collective-permute-start(f32[128,256]{0,1:T(8,128)S(1)} %bitcast_add_fusion.3), channel_id=1, source_target_pairs={{0,8},{8,16},{16,24},{24,32},{32,40},{40,48},{48,56},{56,64},{64,7... | collective-permute-start | bytes 393224 | tf_op jit(solution)/shard_map/while/body/eval_jaxpr/ppermute | solution.py:26
  132.7 10.5 %collective-permute-start = (f32[128,256]{0,1:T(8,128)S(1)}, f32[128,256]{0,1:T(8,128)S(1)}, u32[]{:S(2)}, u32[]{:S(2)}) collective-permute-start(f32[128,256]{0,1:T(8,128)S(1)} %bitcast_add_fusion.3), channel_id=1, source_target_pairs={{0,8},{8,16},{16,24},{24,32},{32,40},{40,48},{48,56},{56,64},{64,7... | collective-permute-start | bytes 393224 | tf_op jit(solution)/shard_map/while/body/eval_jaxpr/ppermute | solution.py:26
  143.4 11.5 %collective-permute-start = (f32[128,256]{0,1:T(8,128)S(1)}, f32[128,256]{0,1:T(8,128)S(1)}, u32[]{:S(2)}, u32[]{:S(2)}) collective-permute-start(f32[128,256]{0,1:T(8,128)S(1)} %bitcast_add_fusion.3), channel_id=1, source_target_pairs={{0,8},{8,16},{16,24},{24,32},{32,40},{40,48},{48,56},{56,64},{64,7... | collective-permute-start | bytes 393224 | tf_op jit(solution)/shard_map/while/body/eval_jaxpr/ppermute | solution.py:26
  155.2 10.7 %collective-permute-start = (f32[128,256]{0,1:T(8,128)S(1)}, f32[128,256]{0,1:T(8,128)S(1)}, u32[]{:S(2)}, u32[]{:S(2)}) collective-permute-start(f32[128,256]{0,1:T(8,128)S(1)} %bitcast_add_fusion.3), channel_id=1, source_target_pairs={{0,8},{8,16},{16,24},{24,32},{32,40},{40,48},{48,56},{56,64},{64,7... | collective-permute-start | bytes 393224 | tf_op jit(solution)/shard_map/while/body/eval_jaxpr/ppermute | solution.py:26
  166.1 10.2 %collective-permute-start = (f32[128,256]{0,1:T(8,128)S(1)}, f32[128,256]{0,1:T(8,128)S(1)}, u32[]{:S(2)}, u32[]{:S(2)}) collective-permute-start(f32[128,256]{0,1:T(8,128)S(1)} %bitcast_add_fusion.3), channel_id=1, source_target_pairs={{0,8},{8,16},{16,24},{24,32},{32,40},{40,48},{48,56},{56,64},{64,7... | collective-permute-start | bytes 393224 | tf_op jit(solution)/shard_map/while/body/eval_jaxpr/ppermute | solution.py:26
  176.5 10.2 %collective-permute-start = (f32[128,256]{0,1:T(8,128)S(1)}, f32[128,256]{0,1:T(8,128)S(1)}, u32[]{:S(2)}, u32[]{:S(2)}) collective-permute-start(f32[128,256]{0,1:T(8,128)S(1)} %bitcast_add_fusion.3), channel_id=1, source_target_pairs={{0,8},{8,16},{16,24},{24,32},{32,40},{40,48},{48,56},{56,64},{64,7... | collective-permute-start | bytes 393224 | tf_op jit(solution)/shard_map/while/body/eval_jaxpr/ppermute | solution.py:26
  186.9 10.2 %collective-permute-start = (f32[128,256]{0,1:T(8,128)S(1)}, f32[128,256]{0,1:T(8,128)S(1)}, u32[]{:S(2)}, u32[]{:S(2)}) collective-permute-start(f32[128,256]{0,1:T(8,128)S(1)} %bitcast_add_fusion.3), channel_id=1, source_target_pairs={{0,8},{8,16},{16,24},{24,32},{32,40},{40,48},{48,56},{56,64},{64,7... | collective-permute-start | bytes 393224 | tf_op jit(solution)/shard_map/while/body/eval_jaxpr/ppermute | solution.py:26
  197.3 10.2 %collective-permute-start = (f32[128,256]{0,1:T(8,128)S(1)}, f32[128,256]{0,1:T(8,128)S(1)}, u32[]{:S(2)}, u32[]{:S(2)}) collective-permute-start(f32[128,256]{0,1:T(8,128)S(1)} %bitcast_add_fusion.3), channel_id=1, source_target_pairs={{0,8},{8,16},{16,24},{24,32},{32,40},{40,48},{48,56},{56,64},{64,7... | collective-permute-start | bytes 393224 | tf_op jit(solution)/shard_map/while/body/eval_jaxpr/ppermute | solution.py:26
  207.7 10.2 %collective-permute-start = (f32[128,256]{0,1:T(8,128)S(1)}, f32[128,256]{0,1:T(8,128)S(1)}, u32[]{:S(2)}, u32[]{:S(2)}) collective-permute-start(f32[128,256]{0,1:T(8,128)S(1)} %bitcast_add_fusion.3), channel_id=1, source_target_pairs={{0,8},{8,16},{16,24},{24,32},{32,40},{40,48},{48,56},{56,64},{64,7... | collective-permute-start | bytes 393224 | tf_op jit(solution)/shard_map/while/body/eval_jaxpr/ppermute | solution.py:26
  218.1 10.2 %collective-permute-start = (f32[128,256]{0,1:T(8,128)S(1)}, f32[128,256]{0,1:T(8,128)S(1)}, u32[]{:S(2)}, u32[]{:S(2)}) collective-permute-start(f32[128,256]{0,1:T(8,128)S(1)} %bitcast_add_fusion.3), channel_id=1, source_target_pairs={{0,8},{8,16},{16,24},{24,32},{32,40},{40,48},{48,56},{56,64},{64,7... | collective-permute-start | bytes 393224 | tf_op jit(solution)/shard_map/while/body/eval_jaxpr/ppermute | solution.py:26
  228.5 11.0 %collective-permute-start = (f32[128,256]{0,1:T(8,128)S(1)}, f32[128,256]{0,1:T(8,128)S(1)}, u32[]{:S(2)}, u32[]{:S(2)}) collective-permute-start(f32[128,256]{0,1:T(8,128)S(1)} %bitcast_add_fusion.3), channel_id=1, source_target_pairs={{0,8},{8,16},{16,24},{24,32},{32,40},{40,48},{48,56},{56,64},{64,7... | collective-permute-start | bytes 393224 | tf_op jit(solution)/shard_map/while/body/eval_jaxpr/ppermute | solution.py:26
  239.7 11.0 %collective-permute-start = (f32[128,256]{0,1:T(8,128)S(1)}, f32[128,256]{0,1:T(8,128)S(1)}, u32[]{:S(2)}, u32[]{:S(2)}) collective-permute-start(f32[128,256]{0,1:T(8,128)S(1)} %bitcast_add_fusion.3), channel_id=1, source_target_pairs={{0,8},{8,16},{16,24},{24,32},{32,40},{40,48},{48,56},{56,64},{64,7... | collective-permute-start | bytes 393224 | tf_op jit(solution)/shard_map/while/body/eval_jaxpr/ppermute | solution.py:26
  250.9 10.2 %collective-permute-start = (f32[128,256]{0,1:T(8,128)S(1)}, f32[128,256]{0,1:T(8,128)S(1)}, u32[]{:S(2)}, u32[]{:S(2)}) collective-permute-start(f32[128,256]{0,1:T(8,128)S(1)} %bitcast_add_fusion.3), channel_id=1, source_target_pairs={{0,8},{8,16},{16,24},{24,32},{32,40},{40,48},{48,56},{56,64},{64,7... | collective-permute-start | bytes 393224 | tf_op jit(solution)/shard_map/while/body/eval_jaxpr/ppermute | solution.py:26
  261.3 10.2 %collective-permute-start = (f32[128,256]{0,1:T(8,128)S(1)}, f32[128,256]{0,1:T(8,128)S(1)}, u32[]{:S(2)}, u32[]{:S(2)}) collective-permute-start(f32[128,256]{0,1:T(8,128)S(1)} %bitcast_add_fusion.3), channel_id=1, source_target_pairs={{0,8},{8,16},{16,24},{24,32},{32,40},{40,48},{48,56},{56,64},{64,7... | collective-permute-start | bytes 393224 | tf_op jit(solution)/shard_map/while/body/eval_jaxpr/ppermute | solution.py:26
  271.7 10.2 %collective-permute-start = (f32[128,256]{0,1:T(8,128)S(1)}, f32[128,256]{0,1:T(8,128)S(1)}, u32[]{:S(2)}, u32[]{:S(2)}) collective-permute-start(f32[128,256]{0,1:T(8,128)S(1)} %bitcast_add_fusion.3), channel_id=1, source_target_pairs={{0,8},{8,16},{16,24},{24,32},{32,40},{40,48},{48,56},{56,64},{64,7... | collective-permute-start | bytes 393224 | tf_op jit(solution)/shard_map/while/body/eval_jaxpr/ppermute | solution.py:26
  282.1 10.2 %collective-permute-start = (f32[128,256]{0,1:T(8,128)S(1)}, f32[128,256]{0,1:T(8,128)S(1)}, u32[]{:S(2)}, u32[]{:S(2)}) collective-permute-start(f32[128,256]{0,1:T(8,128)S(1)} %bitcast_add_fusion.3), channel_id=1, source_target_pairs={{0,8},{8,16},{16,24},{24,32},{32,40},{40,48},{48,56},{56,64},{64,7... | collective-permute-start | bytes 393224 | tf_op jit(solution)/shard_map/while/body/eval_jaxpr/ppermute | solution.py:26
  292.5 10.2 %collective-permute-start = (f32[128,256]{0,1:T(8,128)S(1)}, f32[128,256]{0,1:T(8,128)S(1)}, u32[]{:S(2)}, u32[]{:S(2)}) collective-permute-start(f32[128,256]{0,1:T(8,128)S(1)} %bitcast_add_fusion.3), channel_id=1, source_target_pairs={{0,8},{8,16},{16,24},{24,32},{32,40},{40,48},{48,56},{56,64},{64,7... | collective-permute-start | bytes 393224 | tf_op jit(solution)/shard_map/while/body/eval_jaxpr/ppermute | solution.py:26
  302.9 10.2 %collective-permute-start = (f32[128,256]{0,1:T(8,128)S(1)}, f32[128,256]{0,1:T(8,128)S(1)}, u32[]{:S(2)}, u32[]{:S(2)}) collective-permute-start(f32[128,256]{0,1:T(8,128)S(1)} %bitcast_add_fusion.3), channel_id=1, source_target_pairs={{0,8},{8,16},{16,24},{24,32},{32,40},{40,48},{48,56},{56,64},{64,7... | collective-permute-start | bytes 393224 | tf_op jit(solution)/shard_map/while/body/eval_jaxpr/ppermute | solution.py:26
  313.3 10.7 %collective-permute-start = (f32[128,256]{0,1:T(8,128)S(1)}, f32[128,256]{0,1:T(8,128)S(1)}, u32[]{:S(2)}, u32[]{:S(2)}) collective-permute-start(f32[128,256]{0,1:T(8,128)S(1)} %bitcast_add_fusion.3), channel_id=1, source_target_pairs={{0,8},{8,16},{16,24},{24,32},{32,40},{40,48},{48,56},{56,64},{64,7... | collective-permute-start | bytes 393224 | tf_op jit(solution)/shard_map/while/body/eval_jaxpr/ppermute | solution.py:26
  324.2 11.4 %collective-permute-start = (f32[128,256]{0,1:T(8,128)S(1)}, f32[128,256]{0,1:T(8,128)S(1)}, u32[]{:S(2)}, u32[]{:S(2)}) collective-permute-start(f32[128,256]{0,1:T(8,128)S(1)} %bitcast_add_fusion.3), channel_id=1, source_target_pairs={{0,8},{8,16},{16,24},{24,32},{32,40},{40,48},{48,56},{56,64},{64,7... | collective-permute-start | bytes 393224 | tf_op jit(solution)/shard_map/while/body/eval_jaxpr/ppermute | solution.py:26
  335.8 10.5 %collective-permute-start = (f32[128,256]{0,1:T(8,128)S(1)}, f32[128,256]{0,1:T(8,128)S(1)}, u32[]{:S(2)}, u32[]{:S(2)}) collective-permute-start(f32[128,256]{0,1:T(8,128)S(1)} %bitcast_add_fusion.3), channel_id=1, source_target_pairs={{0,8},{8,16},{16,24},{24,32},{32,40},{40,48},{48,56},{56,64},{64,7... | collective-permute-start | bytes 393224 | tf_op jit(solution)/shard_map/while/body/eval_jaxpr/ppermute | solution.py:26
  346.5 10.2 %collective-permute-start = (f32[128,256]{0,1:T(8,128)S(1)}, f32[128,256]{0,1:T(8,128)S(1)}, u32[]{:S(2)}, u32[]{:S(2)}) collective-permute-start(f32[128,256]{0,1:T(8,128)S(1)} %bitcast_add_fusion.3), channel_id=1, source_target_pairs={{0,8},{8,16},{16,24},{24,32},{32,40},{40,48},{48,56},{56,64},{64,7... | collective-permute-start | bytes 393224 | tf_op jit(solution)/shard_map/while/body/eval_jaxpr/ppermute | solution.py:26
  356.9 10.2 %collective-permute-start = (f32[128,256]{0,1:T(8,128)S(1)}, f32[128,256]{0,1:T(8,128)S(1)}, u32[]{:S(2)}, u32[]{:S(2)}) collective-permute-start(f32[128,256]{0,1:T(8,128)S(1)} %bitcast_add_fusion.3), channel_id=1, source_target_pairs={{0,8},{8,16},{16,24},{24,32},{32,40},{40,48},{48,56},{56,64},{64,7... | collective-permute-start | bytes 393224 | tf_op jit(solution)/shard_map/while/body/eval_jaxpr/ppermute | solution.py:26
  367.3 10.2 %collective-permute-start = (f32[128,256]{0,1:T(8,128)S(1)}, f32[128,256]{0,1:T(8,128)S(1)}, u32[]{:S(2)}, u32[]{:S(2)}) collective-permute-start(f32[128,256]{0,1:T(8,128)S(1)} %bitcast_add_fusion.3), channel_id=1, source_target_pairs={{0,8},{8,16},{16,24},{24,32},{32,40},{40,48},{48,56},{56,64},{64,7... | collective-permute-start | bytes 393224 | tf_op jit(solution)/shard_map/while/body/eval_jaxpr/ppermute | solution.py:26
  377.7 10.2 %collective-permute-start = (f32[128,256]{0,1:T(8,128)S(1)}, f32[128,256]{0,1:T(8,128)S(1)}, u32[]{:S(2)}, u32[]{:S(2)}) collective-permute-start(f32[128,256]{0,1:T(8,128)S(1)} %bitcast_add_fusion.3), channel_id=1, source_target_pairs={{0,8},{8,16},{16,24},{24,32},{32,40},{40,48},{48,56},{56,64},{64,7... | collective-permute-start | bytes 393224 | tf_op jit(solution)/shard_map/while/body/eval_jaxpr/ppermute | solution.py:26
  388.1 10.2 %collective-permute-start = (f32[128,256]{0,1:T(8,128)S(1)}, f32[128,256]{0,1:T(8,128)S(1)}, u32[]{:S(2)}, u32[]{:S(2)}) collective-permute-start(f32[128,256]{0,1:T(8,128)S(1)} %bitcast_add_fusion.3), channel_id=1, source_target_pairs={{0,8},{8,16},{16,24},{24,32},{32,40},{40,48},{48,56},{56,64},{64,7... | collective-permute-start | bytes 393224 | tf_op jit(solution)/shard_map/while/body/eval_jaxpr/ppermute | solution.py:26
  398.5 10.2 %collective-permute-start = (f32[128,256]{0,1:T(8,128)S(1)}, f32[128,256]{0,1:T(8,128)S(1)}, u32[]{:S(2)}, u32[]{:S(2)}) collective-permute-start(f32[128,256]{0,1:T(8,128)S(1)} %bitcast_add_fusion.3), channel_id=1, source_target_pairs={{0,8},{8,16},{16,24},{24,32},{32,40},{40,48},{48,56},{56,64},{64,7... | collective-permute-start | bytes 393224 | tf_op jit(solution)/shard_map/while/body/eval_jaxpr/ppermute | solution.py:26
  408.9 10.2 %collective-permute-start = (f32[128,256]{0,1:T(8,128)S(1)}, f32[128,256]{0,1:T(8,128)S(1)}, u32[]{:S(2)}, u32[]{:S(2)}) collective-permute-start(f32[128,256]{0,1:T(8,128)S(1)} %bitcast_add_fusion.3), channel_id=1, source_target_pairs={{0,8},{8,16},{16,24},{24,32},{32,40},{40,48},{48,56},{56,64},{64,7... | collective-permute-start | bytes 393224 | tf_op jit(solution)/shard_map/while/body/eval_jaxpr/ppermute | solution.py:26
  419.3 10.2 %collective-permute-start = (f32[128,256]{0,1:T(8,128)S(1)}, f32[128,256]{0,1:T(8,128)S(1)}, u32[]{:S(2)}, u32[]{:S(2)}) collective-permute-start(f32[128,256]{0,1:T(8,128)S(1)} %bitcast_add_fusion.3), channel_id=1, source_target_pairs={{0,8},{8,16},{16,24},{24,32},{32,40},{40,48},{48,56},{56,64},{64,7... | collective-permute-start | bytes 393224 | tf_op jit(solution)/shard_map/while/body/eval_jaxpr/ppermute | solution.py:26
  429.8 10.2 %collective-permute-start.18 = (f32[128,256]{0,1:T(8,128)S(1)}, f32[128,256]{0,1:T(8,128)S(1)}, u32[]{:S(2)}, u32[]{:S(2)}) collective-permute-start(f32[128,256]{0,1:T(8,128)S(1)} %get-tuple-element.140), channel_id=1, source_target_pairs={{0,8},{8,16},{16,24},{24,32},{32,40},{40,48},{48,56},{56,64},{64,7... | collective-permute-start | bytes 393224 | tf_op jit(solution)/shard_map/ppermute | solution.py:26
  442.0 7.7 %collective-permute-start.19 = (f32[2,1,256]{1,2,0:T(8,128)S(1)}, f32[2,1,256]{1,2,0:T(8,128)S(1)}, u32[]{:S(2)}, u32[]{:S(2)}) collective-permute-start(f32[2,1,256]{1,2,0:T(8,128)S(1)} %get-tuple-element.138), channel_id=1, source_target_pairs={{0,1},{1,2},{2,3},{3,4},{4,5},{5,6},{6,7},{8,9},{9,10},{10,11},{11... | collective-permute-start | bytes 6152 | tf_op jit(solution)/shard_map/ppermute | solution.py:17
  453.2 7.7 %collective-permute-start.21 = (f32[2,1,256]{1,2,0:T(8,128)S(1)}, f32[2,1,256]{1,2,0:T(8,128)S(1)}, u32[]{:S(2)}, u32[]{:S(2)}) collective-permute-start(f32[2,1,256]{1,2,0:T(8,128)S(1)} %get-tuple-element.136), channel_id=1, source_target_pairs={{0,1},{1,2},{2,3},{3,4},{4,5},{5,6},{6,7},{8,9},{9,10},{10,11},{11... | collective-permute-start | bytes 6152 | tf_op jit(solution)/shard_map/ppermute | solution.py:17
  464.4 7.7 %collective-permute-start.23 = (f32[2,1,256]{1,2,0:T(8,128)S(1)}, f32[2,1,256]{1,2,0:T(8,128)S(1)}, u32[]{:S(2)}, u32[]{:S(2)}) collective-permute-start(f32[2,1,256]{1,2,0:T(8,128)S(1)} %get-tuple-element.134), channel_id=1, source_target_pairs={{0,1},{1,2},{2,3},{3,4},{4,5},{5,6},{6,7},{8,9},{9,10},{10,11},{11... | collective-permute-start | bytes 6152 | tf_op jit(solution)/shard_map/ppermute | solution.py:17
  (12 other events, 67.7 us)
where the time goes:
time: 477 us; the launch traced here: 475 us
  waiting for transfers between devices  332 us (70%)
  starting transfers between devices  113 us (24%)
  other arithmetic  11.2 us (2%)
  matrix products  11 us (2%)
  local copies, waits for them, and re-layouts  6.41 us (1%)
    ppermute x33, waiting for transfers between devices, passed_along(): return lax.ppermute(block, axis, route)  277 us
    ppermute x33, starting transfers between devices, passed_along(): return lax.ppermute(block, axis, route)  64.9 us
    ppermute x11, waiting for transfers between devices, with_halo(): before = lax.ppermute(last, axis, up)  42 us
    ppermute x11, starting transfers between devices, with_halo(): before = lax.ppermute(last, axis, up)  26.7 us
    ppermute x11, starting transfers between devices, with_halo(): after = lax.ppermute(first, axis, down)  21.3 us
    ppermute x11, waiting for transfers between devices, with_halo(): after = lax.ppermute(first, axis, down)  13.7 us
    dot_general x11, matrix products, advance(): jnp.einsum('krbj,cij->ckrbi', blocked, inverses, precision=lax.Precision....  11 us
  transfers between devices with their start and end apart: 55, of which 54 were waited for; matrix products, arithmetic and copies ran while one was open for 0% of the time, Pallas kernels for 0%

commit v1 on v0

v1 whole, which is shorter than its diff:
```python
import functools

import jax
import jax.numpy as jnp
from jax import lax
from jax.experimental import pallas as pl
from jax.experimental.pallas import tpu as pltpu
from jax.sharding import PartitionSpec as P

LB = 128
PAD = 16
EDGE = 8
VMEM = pl.BlockSpec(memory_space=pltpu.VMEM)
SMEM = pl.BlockSpec(memory_space=pltpu.SMEM)


def class_masks(params):
    even, odd, upper = [], [], []
    for block in range(2):
        category = jnp.broadcast_to(params[:, 1 + block : 2 + block], (params.shape[0], LB))
        high = category > 1.5
        low = category - jnp.where(high, 2.0, 0.0)
        odd.append(jnp.where(low > 0.5, 1.0, 0.0).astype(jnp.bfloat16))
        even.append(jnp.where(low > 0.5, 0.0, 1.0).astype(jnp.bfloat16))
        upper.append(high)
    return even, odd, upper


def cut_masks(masks, first, last):
    return tuple([m[first:last] for m in kind] for kind in masks)


def solve_lines(fields, masks, weights):
    even, odd, upper = masks
    rows = fields[0].shape[0]
    left = []
    for field in fields:
        for block in range(2):
            x = field[:, block * LB : (block + 1) * LB]
            high = x.astype(jnp.bfloat16)
            low = (x - high.astype(jnp.float32)).astype(jnp.bfloat16)
            high_pair = [high * even[block], high * odd[block]]
            low_pair = [low * even[block], low * odd[block]]
            left.append(jnp.concatenate(high_pair + low_pair + high_pair, axis=1))
    product = jnp.dot(jnp.concatenate(left, axis=0), weights, preferred_element_type=jnp.float32)
    results = []
    for index in range(len(fields)):
        blocks = []
        for block in range(2):
            part = product[(2 * index + block) * rows : (2 * index + block + 1) * rows]
            blocks.append(jnp.where(upper[block], part[:, LB:], part[:, :LB]))
        results.append(jnp.concatenate(blocks, axis=1))
    return results


def spread(field, coupling):
    rows = field.shape[0]
    return field + coupling * (pltpu.roll(field, 1, 0) + pltpu.roll(field, rows - 1, 0))


def relax_kernel(
    chunks, first_ref, starts_ref, sources_ref, params_ref, above_ref, below_ref, weights_ref, rates_ref,
    terms_ref, factor_ref, shift_ref, decay_ref, base_ref, last_ref, relaxed_ref,
):
    first = first_ref[0, 0]

    def padded(slab, own):
        return jnp.concatenate([above_ref[slab], own, below_ref[slab]], axis=0)

    params = padded(10, params_ref[...])
    coupling = jnp.broadcast_to(params[:, :1], (params.shape[0], 2 * LB))
    masks = class_masks(params)
    rows = params.shape[0]
    near = slice(EDGE, rows - EDGE)
    own = slice(PAD, rows - PAD)
    near_coupling, near_masks = coupling[near], cut_masks(masks, EDGE, rows - EDGE)
    weights = weights_ref[...]

    starts = [padded(g * 5, starts_ref[g]) for g in range(2)]

    def source(g, m):
        return padded(g * 5 + 1 + m, sources_ref[g, m])

    linear = starts[0][near]
    state = starts
    for m in range(2):
        state = solve_lines([spread(state[g], coupling) + source(g, m) for g in range(2)], masks, weights)
        (linear,) = solve_lines([spread(linear, near_coupling)], near_masks, weights)
        for g in range(2):
            relaxed_ref[g, m] = state[g][own]
    rhs = [(spread(state[g], coupling) + source(g, 2))[near] for g in range(2)]
    *state, linear = solve_lines(rhs + [spread(linear, near_coupling)], near_masks, weights)
    inner = slice(EDGE, rows - EDGE - PAD)
    for g in range(2):
        relaxed_ref[g, 2] = state[g][inner]
    rhs = [spread(state[g], near_coupling) + source(g, 3)[near] for g in range(2)]
    *ends, linear = solve_lines(rhs + [spread(linear, near_coupling)], near_masks, weights)
    linear = jnp.where(first > 0, jnp.zeros_like(linear), linear)

    change = ends[0] - starts[1][near]
    resid, onward = change, ends[1]
    for m in range(4):
        resid, onward = solve_lines(
            [spread(resid, near_coupling), spread(onward, near_coupling)], near_masks, weights
        )

    near_params = params[near]
    rate_blocks = []
    for block in range(2):
        category = jnp.broadcast_to(near_params[:, 1 + block : 2 + block], (near_params.shape[0], LB))
        rate = jnp.broadcast_to(rates_ref[0:1, :], category.shape)
        for c in range(1, 4):
            rate = jnp.where(category > c - 0.5, jnp.broadcast_to(rates_ref[c : c + 1, :], category.shape), rate)
        rate_blocks.append(rate)
    rates = jnp.concatenate(rate_blocks, axis=1)
    decay = jnp.exp(-rates)
    ahead = onward * jnp.exp(rates)
    term = resid + ahead - decay * linear

    tiles = term.shape[0] // 8
    terms_ref[...] = jnp.zeros_like(terms_ref)
    factor_ref[...] = jnp.zeros_like(factor_ref)
    squared = decay * decay
    for block in range(2):
        for t in range(tiles):
            tile = block * tiles + t
            chunk, slot = tile % chunks, tile // chunks
            where = (slice(t * 8, t * 8 + 8), slice(block * LB, (block + 1) * LB))
            terms_ref[chunk, slot * 8 : slot * 8 + 8, :] = term[where]
            factor_ref[chunk, slot * 8 : slot * 8 + 8, :] = squared[where]
    shift_ref[...] = ends[1] - ahead
    decay_ref[...] = decay
    base_ref[0] = jnp.where(first > 0, jnp.zeros_like(linear), starts[0][near])
    base_ref[1] = change - linear
    last_ref[0] = ends[0][inner] - linear[inner]
    last_ref[1] = (ends[1] + resid - decay * linear)[inner]


def scan_kernel(terms_ref, factor_ref, entering_ref):
    factor = factor_ref[...]
    carried = jnp.zeros_like(factor)
    for d in range(terms_ref.shape[0]):
        entering_ref[d] = carried
        carried = factor * carried + terms_ref[d]


def final_kernel(
    chunks, entering_ref, shift_ref, decay_ref, base_ref, last_ref, relaxed_ref, params_ref, above_ref, below_ref,
    weights_ref, states_ref,
):
    decay = decay_ref[...]
    tiles = decay.shape[0] // 8
    blocks = []
    for block in range(2):
        parts = []
        for t in range(tiles):
            tile = block * tiles + t
            chunk, slot = tile % chunks, tile // chunks
            parts.append(entering_ref[chunk, slot * 8 : slot * 8 + 8, :])
        blocks.append(jnp.concatenate(parts, axis=0))
    entering = jnp.concatenate(blocks, axis=1)
    params = jnp.concatenate([above_ref[10][EDGE:], params_ref[...], below_ref[10][:EDGE]], axis=0)
    coupling = jnp.broadcast_to(params[:, :1], (params.shape[0], 2 * LB))
    masks = class_masks(params)
    inner = slice(EDGE, params.shape[0] - EDGE)
    passed = decay * entering
    states_ref[0, 3] = passed[inner] + last_ref[0]
    states_ref[1, 3] = (decay * passed)[inner] + last_ref[1]
    state = [entering + shift_ref[...] - base_ref[0], passed + base_ref[1]]
    weights = weights_ref[...]
    for m in range(3):
        state = solve_lines([spread(s, coupling) for s in state], masks, weights)
        for g in range(2):
            states_ref[g, m] = relaxed_ref[g, m] + state[g][inner]


def shards(sources, starts, coupling, classes, inverses, coarse_rate):
    count, along = lax.axis_size("tm"), lax.axis_size("space")
    lines, line_len = starts.shape[1:]
    near_rows = lines + 2 * EDGE
    f32 = jnp.float32
    first = (lax.axis_index("tm") == 0).astype(jnp.int32).reshape(1, 1)

    params = jnp.concatenate([coupling[:, None], classes.astype(f32)], axis=1)
    params = jnp.pad(params, ((0, 0), (0, line_len - 3)))

    def slabs(rows):
        fields = jnp.concatenate([starts[:, None, rows], sources[:, :, rows]], axis=1)
        fields = fields.reshape(-1, PAD, line_len)
        return jnp.concatenate([fields, params[None, rows]], axis=0)

    with jax.named_scope("halo"):
        up = [(i, i + 1) for i in range(along - 1)]
        down = [(j, i) for i, j in up]
        above = lax.ppermute(slabs(slice(lines - PAD, lines)), "space", up)
        below = lax.ppermute(slabs(slice(0, PAD)), "space", down)

    with jax.named_scope("weights"):
        transposed = inverses.transpose(0, 2, 1)
        table = jnp.concatenate(
            [
                jnp.concatenate([transposed[0], transposed[2]], axis=1),
                jnp.concatenate([transposed[1], transposed[3]], axis=1),
            ],
            axis=0,
        )
        high = lax.reduce_precision(table, 8, 7)
        weights = jnp.concatenate([high, high, table - high], axis=0).astype(jnp.bfloat16)

    per_chunk = 8 * -(-(2 * near_rows // 8) // count)
    chunked = jax.ShapeDtypeStruct((count, per_chunk, LB), f32)
    near = jax.ShapeDtypeStruct((near_rows, line_len), f32)
    params_compiler = pltpu.CompilerParams(vmem_limit_bytes=48 * 1024 * 1024)
    terms, factors, shift, decay, base, last, relaxed = pl.pallas_call(
        functools.partial(relax_kernel, count),
        out_shape=(
            chunked,
            chunked,
            near,
            near,
            jax.ShapeDtypeStruct((2, near_rows, line_len), f32),
            jax.ShapeDtypeStruct((2, lines, line_len), f32),
            jax.ShapeDtypeStruct((2, 3, lines, line_len), f32),
        ),
        in_specs=[SMEM] + [VMEM] * 7,
        out_specs=[VMEM] * 7,
        compiler_params=params_compiler,
        name="relax",
    )(first, starts, sources, params, above, below, weights, coarse_rate)

    with jax.named_scope("onward"):
        shift = lax.ppermute(shift, "tm", [(i, i + 1) for i in range(count - 1)])
    with jax.named_scope("gather_terms"):
        terms = lax.all_to_all(terms, "tm", 0, 0)
    factor = lax.dynamic_index_in_dim(factors, lax.axis_index("tm"), 0, keepdims=False)
    entering = pl.pallas_call(
        scan_kernel,
        out_shape=chunked,
        in_specs=[VMEM] * 2,
        out_specs=VMEM,
        compiler_params=params_compiler,
        name="scan",
    )(terms, factor)
    with jax.named_scope("return_terms"):
        entering = lax.all_to_all(entering, "tm", 0, 0)
    return pl.pallas_call(
        functools.partial(final_kernel, count),
        out_shape=jax.ShapeDtypeStruct((2, 4, lines, line_len), f32),
        in_specs=[VMEM] * 10,
        out_specs=VMEM,
        compiler_params=params_compiler,
        name="final",
    )(entering, shift, decay, base, last, relaxed, params, above, below, weights)


def solution(mesh):
    in_specs = (
        P("tm", None, "space", None),
        P("tm", "space", None),
        P("space"),
        P("space", None),
        P(),
        P(),
    )
    out_specs = P("tm", None, "space", None)
    return jax.shard_map(shards, mesh=mesh, in_specs=in_specs, out_specs=out_specs, check_vma=False)
```

time: 477 us -> 63.1 us (0.13)
  the two profiles are of different devices: /device:TPU:152 before, /device:TPU:8 now
where the time goes in v1:
time: 63.1 us; the launch traced here: 62.7 us
  waiting for transfers between devices  25.8 us (41%)
  starting transfers between devices  22.9 us (36%)
  Pallas kernels  8.2 us (13%)
  local copies, waits for them, and re-layouts  4.79 us (8%)
  other arithmetic  0.8 us (1%)
    all_to_all x1, waiting for transfers between devices, shards(): terms = lax.all_to_all(terms, 'tm', 0, 0)  11.6 us
    all_to_all x1, starting transfers between devices, shards(): terms = lax.all_to_all(terms, 'tm', 0, 0)  10.8 us
    all_to_all x1, waiting for transfers between devices, shards(): entering = lax.all_to_all(entering, 'tm', 0, 0)  6.33 us
    pallas_call x1, Pallas kernels, shards(): pl.pallas_call(functools.partial(relax_kernel, count), out_shape=(chunked...  5.06 us
    ppermute x1, waiting for transfers between devices, shards(): above = lax.ppermute(slabs(slice(lines - PAD, lines)), 'space', up)  4.4 us
    all_to_all x1, starting transfers between devices, shards(): entering = lax.all_to_all(entering, 'tm', 0, 0)  4 us
    ppermute x1, starting transfers between devices, shards(): shift = lax.ppermute(shift, 'tm', [(i, i + 1) for i in range(count - 1)])  3.63 us
    ppermute x1, waiting for transfers between devices, shards(): shift = lax.ppermute(shift, 'tm', [(i, i + 1) for i in range(count - 1)])  3.23 us
  transfers between devices with their start and end apart: 5, of which 5 were waited for; matrix products, arithmetic and copies ran while one was open for 2% of the time, Pallas kernels for 0%

profile of v1, /device:TPU:8, one launch (start us, length us, event | category | flops | bytes accessed | tf_op | source)
XLA Modules:
  0.0 62.7 jit_solution(10134995388191996613)
XLA Ops:
  0.0 0.7 %convert_element_type.4 = f32[128,2]{0,1:T(2,128)S(1)} convert(s32[128,2]{0,1:T(2,128)} %param.9) | non-fusion elementwise | flops 256 | bytes 2048 | tf_op jit(solution)/shard_map/convert_element_type | solution.py:184
  0.7 0.0 copy-start.7
  0.7 0.7 %copy-done.7 = f32[128]{0:T(128)S(1)} copy-done((f32[128]{0:T(128)S(1)}, f32[128]{0:T(128)}, u32[]{:S(2)}) %copy-start.7) | copy-done | bytes 536
  1.3 0.1 copy.12
  1.5 0.8 %slice_bitcast_fusion.4 = (f32[2,1,16,256]{3,2,1,0:T(8,128)S(1)}, f32[2,1,16,256]{3,2,1,0:T(8,128)S(1)}) fusion(f32[2,128,256]{2,1,0:T(8,128)} %starts_ref.1), kind=kLoop, calls=%fused_computation.15 | loop fusion | bytes 131072 | tf_op jit(solution)/shard_map/halo/broadcast_in_dim | solution.py:188
  2.3 1.0 %fusion.3 = (f32[2,4,16,256]{3,2,1,0:T(8,128)S(1)}, f32[2,4,16,256]{3,2,1,0:T(8,128)S(1)}) fusion(f32[2,4,128,256]{3,2,1,0:T(8,128)} %sources_ref.1), kind=kLoop, calls=%fused_computation.21 | loop fusion | bytes 524288 | tf_op jit(solution)/shard_map/halo/slice | solution.py:188
  3.3 0.0 copy-start.6
  3.3 2.1 %collective-permute-start.1 = (f32[11,16,256]{2,1,0:T(8,128)S(1)}, f32[11,16,256]{2,1,0:T(8,128)S(1)}, u32[]{:S(2)}, u32[]{:S(2)}) collective-permute-start(f32[11,16,256]{2,1,0:T(8,128)S(1)} %pad_maximum_fusion.2), channel_id=1, source_target_pairs={{1,0},{2,1},{3,2},{4,3},{5,4},{6,5},{7,6},{9,8},{10,9},{11,10},{12... | collective-permute-start | bytes 540680 | tf_op jit(solution)/shard_map/halo/ppermute | solution.py:196
  5.4 2.4 %collective-permute-start = (f32[11,16,256]{2,1,0:T(8,128)S(1)}, f32[11,16,256]{2,1,0:T(8,128)S(1)}, u32[]{:S(2)}, u32[]{:S(2)}) collective-permute-start(f32[11,16,256]{2,1,0:T(8,128)S(1)} %pad_maximum_fusion.1), channel_id=1, source_target_pairs={{0,1},{1,2},{2,3},{3,4},{4,5},{5,6},{6,7},{8,9},{9,10},{10,11},{11... | collective-permute-start | bytes 540680 | tf_op jit(solution)/shard_map/halo/ppermute | solution.py:195
  7.8 0.0 copy-done.6
  7.8 0.1 copy.15
  8.0 0.0 copy-start
  8.1 0.0 copy-start.1
  8.1 0.0 copy-start.2
  8.1 0.2 collective-permute-done.1.below_ref
  8.4 4.4 %collective-permute-done.above_ref = f32[11,16,256]{2,1,0:T(8,128)S(1)} collective-permute-done((f32[11,16,256]{2,1,0:T(8,128)S(1)}, f32[11,16,256]{2,1,0:T(8,128)S(1)}, u32[]{:S(2)}, u32[]{:S(2)}) %collective-permute-start) | collective-permute-done | bytes 180256 | tf_op jit(solution)/shard_map/halo/ppermute | solution.py:195
  12.8 0.0 copy-done
  12.8 0.0 copy-done.1
  12.8 0.0 copy-done.2
  12.8 5.1 %relax.1 = (f32[32,16,128]{2,1,0:T(8,128)}, f32[32,16,128]{2,1,0:T(8,128)S(1)}, f32[144,256]{1,0:T(8,128)S(1)}, f32[144,256]{1,0:T(8,128)S(1)}, f32[2,144,256]{2...) custom-call(s32[1,1]{1,0:T(1,128)} %bitcast.first_ref, f32[2,128,256]{2,1,0:T(8,128)S(1)} %copy-done.1, ...), custom_call_target="tpu_custom_call" | custom-call | tf_op jit(solution)/shard_map/relax/pallas_call | solution.py:214
  17.8 0.0 copy-start.3
  17.8 0.7 %copy-done.3 = f32[32,16,128]{2,1,0:T(8,128)} copy-done((f32[32,16,128]{2,1,0:T(8,128)}, f32[32,16,128]{2,1,0:T(8,128)S(1)}, u32[]{:S(2)}) %copy-start.3) | copy-done | bytes 262168
  18.5 0.0 copy-start.4
  18.5 0.7 %copy-done.4 = f32[144,256]{1,0:T(8,128)} copy-done((f32[144,256]{1,0:T(8,128)}, f32[144,256]{1,0:T(8,128)S(1)}, u32[]{:S(2)}) %copy-start.4) | copy-done | bytes 147480
  19.2 10.8 %all-to-all-start = ((f32[32,16,128]{2,1,0:T(8,128)}), f32[32,16,128]{2,1,0:T(8,128)S(1)}, u32[]{:S(2)}, u32[]{:S(2)}) async-start(f32[32,16,128]{2,1,0:T(8,128)} %get-tuple-element.12), calls=%async_computation | async-start | bytes 524288 | tf_op jit(solution)/shard_map/gather_terms/all_to_all | solution.py:234
  30.0 0.7 %dynamic-slice_bitcast_fusion.factor_ref = f32[16,128]{1,0:T(8,128)S(1)} fusion(f32[32,16,128]{2,1,0:T(8,128)} %copy-done.3, s32[]{:T(128)S(6)} %select_n.4), kind=kLoop, calls=%fused_computation.19 | loop fusion | bytes 16388 | tf_op jit(solution)/shard_map/jit(dynamic_index_in_dim)/squeeze | solution.py:235
  30.7 11.6 %all-to-all-done.terms_ref = f32[32,16,128]{2,1,0:T(8,128)S(1)} async-done(((f32[32,16,128]{2,1,0:T(8,128)}), f32[32,16,128]{2,1,0:T(8,128)S(1)}, u32[]{:S(2)}, u32[]{:S(2)}) %all-to-all-start) | async-done | bytes 262176 | tf_op jit(solution)/shard_map/gather_terms/all_to_all | solution.py:234
  42.3 0.8 %scan.1 = f32[32,16,128]{2,1,0:T(8,128)} custom-call(f32[32,16,128]{2,1,0:T(8,128)S(1)} %all-to-all-done.terms_ref, f32[16,128]{1,0:T(8,128)S(1)} %dynamic-slice_bitcast_fusion.factor_ref), custom_call_target="tpu_custom_call" | custom-call | tf_op jit(solution)/shard_map/scan/pallas_call | solution.py:236
  43.1 0.0 copy-start.5
  43.1 4.0 %all-to-all-start.1 = ((f32[32,16,128]{2,1,0:T(8,128)}), f32[32,16,128]{2,1,0:T(8,128)S(1)}, u32[]{:S(2)}, u32[]{:S(2)}) async-start(f32[32,16,128]{2,1,0:T(8,128)} %scan.1), calls=%async_computation.1 | async-start | bytes 524288 | tf_op jit(solution)/shard_map/return_terms/all_to_all | solution.py:245
  47.1 0.0 copy-done.5
  47.1 3.6 %collective-permute-start.2 = (f32[144,256]{1,0:T(8,128)S(1)}, f32[144,256]{1,0:T(8,128)S(1)}, u32[]{:S(2)}, u32[]{:S(2)}) collective-permute-start(f32[144,256]{1,0:T(8,128)S(1)} %copy-done.5), channel_id=1, source_target_pairs={{0,8},{8,16},{16,24},{24,32},{32,40},{40,48},{48,56},{56,64},{64,7... | collective-permute-start | bytes 442376 | tf_op jit(solution)/shard_map/onward/ppermute | solution.py:232
  50.7 3.2 %collective-permute-done.2.shift_ref = f32[144,256]{1,0:T(8,128)S(1)} collective-permute-done((f32[144,256]{1,0:T(8,128)S(1)}, f32[144,256]{1,0:T(8,128)S(1)}, u32[]{:S(2)}, u32[]{:S(2)}) %collective-permute-start.2) | collective-permute-done | bytes 147488 | tf_op jit(solution)/shard_map/onward/ppermute | solution.py:232
  54.0 6.3 %all-to-all-done.1.entering_ref = f32[32,16,128]{2,1,0:T(8,128)S(1)} async-done(((f32[32,16,128]{2,1,0:T(8,128)}), f32[32,16,128]{2,1,0:T(8,128)S(1)}, u32[]{:S(2)}, u32[]{:S(2)}) %all-to-all-start.1) | async-done | bytes 262176 | tf_op jit(solution)/shard_map/return_terms/all_to_all | solution.py:245
  60.3 2.4 %final.1 = f32[2,4,128,256]{3,2,1,0:T(8,128)} custom-call(f32[32,16,128]{2,1,0:T(8,128)S(1)} %all-to-all-done.1.entering_ref, f32[144,256]{1,0:T(8,128)S(1)} %collective-permute-done.2.shift_ref, f32[144,256]{1,0:T(8,128)S(1)} %get-tuple-element.15.decay_ref, f32[2,144,256]{2,1,0:T(8,128)S(1)} %get-tuple-element.16.base_ref, ...), custom_call_target="tpu_custom_call" | custom-call | tf_op jit(solution)/shard_map/final/pallas_call | solution.py:246
  (9 shorter events, 0.2 us)
Async XLA Ops:
  0.7 0.7 %copy-start.7 = (f32[128]{0:T(128)S(1)}, f32[128]{0:T(128)}, u32[]{:S(2)}) copy-start(f32[128]{0:T(128)} %param.8) | copy-start | bytes 1540
  3.3 4.5 %copy-start.6 = (f32[4,128,128]{2,1,0:T(8,128)S(1)}, f32[4,128,128]{2,1,0:T(8,128)}, u32[]{:S(2)}) copy-start(f32[4,128,128]{2,1,0:T(8,128)} %param.10) | copy-start | bytes 786436
  3.3 5.1 %collective-permute-start.1 = (f32[11,16,256]{2,1,0:T(8,128)S(1)}, f32[11,16,256]{2,1,0:T(8,128)S(1)}, u32[]{:S(2)}, u32[]{:S(2)}) collective-permute-start(f32[11,16,256]{2,1,0:T(8,128)S(1)} %pad_maximum_fusion.2), channel_id=1, source_target_pairs={{1,0},{2,1},{3,2},{4,3},{5,4},{6,5},{7,6},{9,8},{10,9},{11,10},{12... | collective-permute-start | bytes 540680 | tf_op jit(solution)/shard_map/halo/ppermute | solution.py:196
  5.4 7.4 %collective-permute-start = (f32[11,16,256]{2,1,0:T(8,128)S(1)}, f32[11,16,256]{2,1,0:T(8,128)S(1)}, u32[]{:S(2)}, u32[]{:S(2)}) collective-permute-start(f32[11,16,256]{2,1,0:T(8,128)S(1)} %pad_maximum_fusion.1), channel_id=1, source_target_pairs={{0,1},{1,2},{2,3},{3,4},{4,5},{5,6},{6,7},{8,9},{9,10},{10,11},{11... | collective-permute-start | bytes 540680 | tf_op jit(solution)/shard_map/halo/ppermute | solution.py:195
  8.0 4.8 %copy-start = (f32[2,4,128,256]{3,2,1,0:T(8,128)S(1)}, f32[2,4,128,256]{3,2,1,0:T(8,128)}, u32[]{:S(2)}) copy-start(f32[2,4,128,256]{3,2,1,0:T(8,128)} %sources_ref.1) | copy-start | bytes 3145732
  8.1 4.7 %copy-start.1 = (f32[2,128,256]{2,1,0:T(8,128)S(1)}, f32[2,128,256]{2,1,0:T(8,128)}, u32[]{:S(2)}) copy-start(f32[2,128,256]{2,1,0:T(8,128)} %starts_ref.1) | copy-start | bytes 786436
  8.1 4.7 %copy-start.2 = (f32[4,128]{1,0:T(4,128)S(1)}, f32[4,128]{1,0:T(4,128)}, u32[]{:S(2)}) copy-start(f32[4,128]{1,0:T(4,128)} %rates_ref.1) | copy-start | bytes 6148
  17.8 0.7 %copy-start.3 = (f32[32,16,128]{2,1,0:T(8,128)}, f32[32,16,128]{2,1,0:T(8,128)S(1)}, u32[]{:S(2)}) copy-start(f32[32,16,128]{2,1,0:T(8,128)S(1)} %get-tuple-element.13) | copy-start | bytes 786436
  18.5 0.7 %copy-start.4 = (f32[144,256]{1,0:T(8,128)}, f32[144,256]{1,0:T(8,128)S(1)}, u32[]{:S(2)}) copy-start(f32[144,256]{1,0:T(8,128)S(1)} %get-tuple-element.14) | copy-start | bytes 442372
  19.2 23.1 %all-to-all-start = ((f32[32,16,128]{2,1,0:T(8,128)}), f32[32,16,128]{2,1,0:T(8,128)S(1)}, u32[]{:S(2)}, u32[]{:S(2)}) async-start(f32[32,16,128]{2,1,0:T(8,128)} %get-tuple-element.12), calls=%async_computation | async-start | bytes 524288 | tf_op jit(solution)/shard_map/gather_terms/all_to_all | solution.py:234
  43.1 4.0 %copy-start.5 = (f32[144,256]{1,0:T(8,128)S(1)}, f32[144,256]{1,0:T(8,128)}, u32[]{:S(2)}) copy-start(f32[144,256]{1,0:T(8,128)} %copy-done.4) | copy-start | bytes 442372
  43.1 17.2 %all-to-all-start.1 = ((f32[32,16,128]{2,1,0:T(8,128)}), f32[32,16,128]{2,1,0:T(8,128)S(1)}, u32[]{:S(2)}, u32[]{:S(2)}) async-start(f32[32,16,128]{2,1,0:T(8,128)} %scan.1), calls=%async_computation.1 | async-start | bytes 524288 | tf_op jit(solution)/shard_map/return_terms/all_to_all | solution.py:245
  47.1 6.9 %collective-permute-start.2 = (f32[144,256]{1,0:T(8,128)S(1)}, f32[144,256]{1,0:T(8,128)S(1)}, u32[]{:S(2)}, u32[]{:S(2)}) collective-permute-start(f32[144,256]{1,0:T(8,128)S(1)} %copy-done.5), channel_id=1, source_target_pairs={{0,8},{8,16},{16,24},{24,32},{32,40},{40,48},{48,56},{56,64},{64,7... | collective-permute-start | bytes 442376 | tf_op jit(solution)/shard_map/onward/ppermute | solution.py:232

commit v2 on v0

v2 whole, which is shorter than its diff:
```python
import functools

import jax
import jax.numpy as jnp
from jax import lax
from jax.experimental import pallas as pl
from jax.experimental.pallas import tpu as pltpu
from jax.sharding import PartitionSpec as P

LB = 128
GROUPS = 2
STEPS = 4
SLAB = 16
EDGE = 8
SIDE = 4
REACH = (11, 10, 9, 8, 7)
GROUP_ROWS = sum(REACH)
MESSAGE_ROWS = 96
VMEM = pl.BlockSpec(memory_space=pltpu.VMEM)
SMEM = pl.BlockSpec(memory_space=pltpu.SMEM)
HBM = pl.BlockSpec(memory_space=pltpu.HBM)
VMEM_LIMIT = 32 * 1024 * 1024


def columns(row):
    return jnp.broadcast_to(row, (LB, LB)).T


def class_masks(categories):
    even, odd, upper = [], [], []
    for category in categories:
        high = category > 1.5
        low = category - jnp.where(high, 2.0, 0.0)
        odd.append(jnp.where(low > 0.5, 1.0, 0.0).astype(jnp.bfloat16))
        even.append(jnp.where(low > 0.5, 0.0, 1.0).astype(jnp.bfloat16))
        upper.append(high)
    return even, odd, upper


def rates_of(categories, rates_ref):
    blocks = []
    for category in categories:
        rate = jnp.broadcast_to(rates_ref[0:1, :], category.shape)
        for c in range(1, 4):
            rate = jnp.where(category > c - 0.5, jnp.broadcast_to(rates_ref[c : c + 1, :], category.shape), rate)
        blocks.append(rate)
    return jnp.concatenate(blocks, axis=1)


def solve_lines(fields, masks, weights):
    even, odd, upper = masks
    rows = fields[0].shape[0]
    left = []
    for field in fields:
        for block in range(2):
            x = field[:, block * LB : (block + 1) * LB]
            high = x.astype(jnp.bfloat16)
            low = (x - high.astype(jnp.float32)).astype(jnp.bfloat16)
            high_pair = [high * even[block], high * odd[block]]
            low_pair = [low * even[block], low * odd[block]]
            left.append(jnp.concatenate(high_pair + low_pair + high_pair, axis=1))
    product = jnp.dot(jnp.concatenate(left, axis=0), weights, preferred_element_type=jnp.float32)
    results = []
    for index in range(len(fields)):
        blocks = []
        for block in range(2):
            part = product[(2 * index + block) * rows : (2 * index + block + 1) * rows]
            blocks.append(jnp.where(upper[block], part[:, LB:], part[:, :LB]))
        results.append(jnp.concatenate(blocks, axis=1))
    return results


def spread(field, coupling):
    rows = field.shape[0]
    return field + coupling * (pltpu.roll(field, 1, 0) + pltpu.roll(field, rows - 1, 0))


def relaxations(starts, sources, coupling, categories, weights, rates_ref, first, relaxed_to):
    masks = class_masks(categories)
    linear, state = starts[0], starts
    for m in range(STEPS):
        *state, linear = solve_lines(
            [spread(state[g], coupling) + sources(g, m) for g in range(GROUPS)] + [spread(linear, coupling)],
            masks,
            weights,
        )
        if m < STEPS - 1:
            for g in range(GROUPS):
                relaxed_to(g, m, state[g])
    ends = state
    linear = jnp.where(first > 0, jnp.zeros_like(linear), linear)
    change = ends[0] - starts[1]
    resid, onward = change, ends[1]
    for m in range(STEPS):
        resid, onward = solve_lines([spread(resid, coupling), spread(onward, coupling)], masks, weights)
    rates = rates_of(categories, rates_ref)
    decay = jnp.exp(-rates)
    ahead = onward * jnp.exp(rates)
    held = decay * linear
    return dict(
        term=resid + ahead - held,
        shift=ends[1] - ahead,
        decay=decay,
        bases=(jnp.where(first > 0, jnp.zeros_like(linear), starts[0]), change - linear),
        lasts=(ends[0] - linear, ends[1] + resid - held),
    )


def pack_kernel(
    starts_hbm, sources_hbm, coupling_hbm, classes_hbm, up_ref, down_ref, params_ref,
    starts_low, starts_high, sources_low, sources_high, coupling_row, classes_rows, sems,
):
    lines = starts_hbm.shape[1]
    low, high = pl.ds(0, SLAB), pl.ds(lines - SLAB, SLAB)
    pairs = [
        (sources_hbm.at[:, :, high, :], sources_high),
        (sources_hbm.at[:, :, low, :], sources_low),
        (starts_hbm.at[:, high, :], starts_high),
        (starts_hbm.at[:, low, :], starts_low),
        (coupling_hbm, coupling_row),
        (classes_hbm, classes_rows),
    ]
    copies = [pltpu.make_async_copy(src, dst, sems.at[i]) for i, (src, dst) in enumerate(pairs)]
    for copy in copies:
        copy.start()
    for ref in (up_ref, down_ref, params_ref):
        ref[...] = jnp.zeros_like(ref)
    for copy in copies:
        copy.wait()
    params_ref[0:1, :] = coupling_row[...]
    params_ref[1:3, :] = classes_rows[...].astype(jnp.float32)
    for g in range(GROUPS):
        at = g * GROUP_ROWS
        for index, reach in enumerate(REACH):
            if index == 0:
                up, down = starts_high[g, SLAB - reach :, :], starts_low[g, :reach, :]
            else:
                up, down = sources_high[g, index - 1, SLAB - reach :, :], sources_low[g, index - 1, :reach, :]
            up_ref[at : at + reach, :] = up
            down_ref[at : at + reach, :] = down
            at += reach
    for ref in (up_ref, down_ref):
        ref[GROUPS * GROUP_ROWS : GROUPS * GROUP_ROWS + 3, :LB] = params_ref[0:3, :]


def own_kernel(
    first_ref, starts_ref, sources_ref, params_ref, weights_ref, rates_ref,
    term_ref, shift_ref, decay_ref, base_ref, last_ref, relaxed_ref,
):
    coupling = columns(params_ref[0:1, :])
    coupling = jnp.concatenate([coupling, coupling], axis=1)
    categories = [columns(params_ref[1 + block : 2 + block, :]) for block in range(2)]

    def relaxed_to(g, m, field):
        relaxed_ref[g, m] = field

    out = relaxations(
        [starts_ref[g] for g in range(GROUPS)], lambda g, m: sources_ref[g, m], coupling, categories, weights_ref[...],
        rates_ref, first_ref[0, 0], relaxed_to,
    )
    term_ref[...] = out["term"]
    shift_ref[...] = out["shift"]
    decay_ref[...] = out["decay"]
    for g in range(GROUPS):
        base_ref[g] = out["bases"][g]
        last_ref[g] = out["lasts"][g]


def joined(inner, strip, beyond):
    lines = inner.shape[0]
    return jnp.concatenate([strip[16 - beyond : 24], inner[EDGE : lines - EDGE], strip[40 : 48 + beyond]], axis=0)


def edge_kernel(
    first_ref, starts_ref, sources_ref, params_ref, above_ref, below_ref, weights_ref, rates_ref,
    own_term_ref, own_shift_ref, own_decay_ref,
    terms_ref, factors_ref, decay_ref, base_ref, last_ref, relaxed_ref, halo_ref,
):
    lines = starts_ref.shape[1]
    lane = lax.broadcasted_iota(jnp.int32, (8, LB), 1)
    at = GROUPS * GROUP_ROWS
    own = params_ref[...]
    halo_ref[...] = jnp.zeros_like(halo_ref)
    halo_ref[0, 0:3, :LB] = above_ref[at : at + 3, :LB]
    halo_ref[0, 8:11, :LB] = below_ref[at : at + 3, :LB]
    above, below = halo_ref[0, 0:8, :LB], halo_ref[0, 8:16, :LB]
    upper = jnp.where(lane < SLAB, pltpu.roll(above, SLAB, 1), pltpu.roll(own, SLAB, 1))
    lower = jnp.where(lane < 3 * SLAB, pltpu.roll(own, 3 * SLAB, 1), pltpu.roll(below, 3 * SLAB, 1))
    strip = jnp.where(lane < 2 * SLAB, upper, lower)
    rows = 4 * SLAB
    coupling = columns(strip[0:1])[:rows]
    coupling = jnp.concatenate([coupling, coupling], axis=1)
    categories = [columns(strip[1 + block : 2 + block])[:rows] for block in range(2)]

    halo_ref[0, 0:16, :] = jnp.zeros((16, 2 * LB), jnp.float32)
    for g in range(GROUPS):
        at = g * GROUP_ROWS
        for index, reach in enumerate(REACH):
            slab = g * len(REACH) + index
            halo_ref[slab, SLAB - reach : SLAB, :] = above_ref[at : at + reach, :]
            halo_ref[slab, SLAB : SLAB + reach, :] = below_ref[at : at + reach, :]
            at += reach

    def strips(slab, low, high):
        return jnp.concatenate([halo_ref[slab, :SLAB, :], low, high, halo_ref[slab, SLAB:, :]], axis=0)

    starts = [
        strips(g * len(REACH), starts_ref[g, :SLAB, :], starts_ref[g, lines - SLAB :, :]) for g in range(GROUPS)
    ]

    def sources(g, m):
        return strips(
            g * len(REACH) + 1 + m, sources_ref[g, m, :SLAB, :], sources_ref[g, m, lines - SLAB :, :]
        )

    def relaxed_to(g, m, field):
        relaxed_ref[g, m] = field

    out = relaxations(starts, sources, coupling, categories, weights_ref[...], rates_ref, first_ref[0, 0], relaxed_to)
    section = lines + 2 * SIDE
    decay = joined(own_decay_ref[...], out["decay"], SIDE)
    for index, field in enumerate(
        (joined(own_term_ref[...], out["term"], SIDE), joined(own_shift_ref[...], out["shift"], SIDE))
    ):
        factor = decay * decay if index == 0 else jnp.zeros_like(decay)
        for block in range(2):
            at = (2 * index + block) * section
            lanes = slice(block * LB, (block + 1) * LB)
            terms_ref[at : at + section, :] = field[:, lanes]
            factors_ref[at : at + section, :] = factor[:, lanes]
    decay_ref[...] = out["decay"]
    for g in range(GROUPS):
        base_ref[g] = out["bases"][g]
        last_ref[g] = out["lasts"][g]


def scan_kernel(place_ref, terms_ref, factors_ref, entering_ref):
    factor = factors_ref[place_ref[0, 0]]
    carried = jnp.zeros_like(factor)
    for d in range(terms_ref.shape[0]):
        entering_ref[d] = carried
        carried = factor * carried + terms_ref[d]


def final_kernel(
    entering_ref, params_ref, above_ref, below_ref, weights_ref, decay_ref, base_ref, last_ref, relaxed_ref,
    edge_decay_ref, edge_base_ref, edge_last_ref, edge_relaxed_ref, states_hbm, field_ref, states_ref, sems,
):
    lines = last_ref.shape[1]
    section = lines + 2 * SIDE
    at = GROUPS * GROUP_ROWS

    def along(row):
        own = columns(params_ref[row : row + 1, :])
        above = columns(above_ref[at + row : at + row + 1, :LB])
        below = columns(below_ref[at + row : at + row + 1, :LB])
        return jnp.concatenate([above[lines - EDGE :], own, below[:EDGE]], axis=0)

    coupling = along(0)
    coupling = jnp.concatenate([coupling, coupling], axis=1)
    masks = class_masks([along(1), along(2)])

    gap = EDGE - SIDE
    field_ref[...] = jnp.zeros_like(field_ref)
    for part in range(2):
        for block in range(2):
            start = (2 * part + block) * section
            field_ref[part, gap : gap + section, block * LB : (block + 1) * LB] = entering_ref[start : start + section, :]
    entering, shift = field_ref[0], field_ref[1]
    inner = slice(EDGE, EDGE + lines)
    decay = joined(decay_ref[...], edge_decay_ref[...], EDGE)
    base = [joined(base_ref[g], edge_base_ref[g], EDGE) for g in range(GROUPS)]
    last = [joined(last_ref[g], edge_last_ref[g], 0) for g in range(GROUPS)]
    passed = decay * entering

    def send(m):
        copy = pltpu.make_async_copy(states_ref.at[:, m], states_hbm.at[:, m], sems.at[m])
        copy.start()
        return copy

    states_ref[0, 3] = passed[inner] + last[0]
    states_ref[1, 3] = (decay * passed)[inner] + last[1]
    copies = [send(3)]
    state = [entering + shift - base[0], passed + base[1]]
    weights = weights_ref[...]
    for m in range(STEPS - 1):
        state = solve_lines([spread(s, coupling) for s in state], masks, weights)
        for g in range(GROUPS):
            states_ref[g, m] = joined(relaxed_ref[g, m], edge_relaxed_ref[g, m], 0) + state[g][inner]
        copies.append(send(m))
    for copy in copies:
        copy.wait()


def shards(sources, starts, coupling, classes, inverses, coarse_rate):
    count, along = lax.axis_size("tm"), lax.axis_size("space")
    lines, line_len = starts.shape[1:]
    near_rows, sections = lines + 2 * EDGE, 4 * (lines + 2 * SIDE)
    f32 = jnp.float32
    place = lax.axis_index("tm").astype(jnp.int32).reshape(1, 1)
    first = (lax.axis_index("tm") == 0).astype(jnp.int32).reshape(1, 1)
    grant = pltpu.CompilerParams(vmem_limit_bytes=VMEM_LIMIT)

    def shape(*dims):
        return jax.ShapeDtypeStruct(dims, f32)

    message = shape(MESSAGE_ROWS, line_len)
    up, down, params = pl.pallas_call(
        pack_kernel,
        out_shape=(message, message, shape(8, lines)),
        in_specs=[HBM] * 4,
        out_specs=[VMEM] * 3,
        scratch_shapes=[
            pltpu.VMEM((GROUPS, SLAB, line_len), f32),
            pltpu.VMEM((GROUPS, SLAB, line_len), f32),
            pltpu.VMEM((GROUPS, STEPS, SLAB, line_len), f32),
            pltpu.VMEM((GROUPS, STEPS, SLAB, line_len), f32),
            pltpu.VMEM((1, lines), f32),
            pltpu.VMEM((2, lines), jnp.int32),
            pltpu.SemaphoreType.DMA((6,)),
        ],
        compiler_params=grant,
        name="pack",
    )(*[
        pltpu.with_memory_space_constraint(x, pltpu.HBM)
        for x in (starts, sources, coupling.reshape(1, lines), classes.T)
    ])

    with jax.named_scope("halo"):
        upward = [(i, i + 1) for i in range(along - 1)]
        above = lax.ppermute(up, "space", upward)
        below = lax.ppermute(down, "space", [(j, i) for i, j in upward])

    with jax.named_scope("weights"):
        transposed = inverses.transpose(0, 2, 1)
        table = jnp.concatenate(
            [
                jnp.concatenate([transposed[0], transposed[2]], axis=1),
                jnp.concatenate([transposed[1], transposed[3]], axis=1),
            ],
            axis=0,
        )
        high = lax.reduce_precision(table, 8, 7)
        weights = jnp.concatenate([high, high, table - high], axis=0).astype(jnp.bfloat16)

    def kept(rows):
        return (
            shape(rows, line_len),
            shape(GROUPS, rows, line_len),
            shape(GROUPS, rows, line_len),
            shape(GROUPS, STEPS - 1, rows, line_len),
        )

    term, shift, *own = pl.pallas_call(
        own_kernel,
        out_shape=(shape(lines, line_len), shape(lines, line_len), *kept(lines)),
        in_specs=[SMEM] + [VMEM] * 5,
        out_specs=[VMEM] * 6,
        compiler_params=grant,
        cost_estimate=pl.CostEstimate(flops=5_000_000_000, bytes_accessed=4_000_000, transcendentals=0),
        name="own",
    )(first, starts, sources, params, weights, coarse_rate)
    terms, factors, *edges = pl.pallas_call(
        edge_kernel,
        out_shape=(shape(sections, LB), shape(sections, LB), *kept(4 * SLAB)),
        in_specs=[SMEM] + [VMEM] * 10,
        out_specs=[VMEM] * 6,
        scratch_shapes=[pltpu.VMEM((GROUPS * len(REACH), 2 * SLAB, line_len), f32)],
        compiler_params=grant,
        name="edge",
    )(first, starts, sources, params, above, below, weights, coarse_rate, term, shift, own[0])

    split = (count, 1, sections * LB // count)
    with jax.named_scope("gather_terms"):
        terms = lax.all_to_all(terms.reshape(split), "tm", 0, 0)
    entering = pl.pallas_call(
        scan_kernel,
        out_shape=shape(*split),
        in_specs=[SMEM] + [VMEM] * 2,
        out_specs=VMEM,
        compiler_params=grant,
        name="scan",
    )(place, terms, factors.reshape(split))
    with jax.named_scope("return_terms"):
        entering = lax.all_to_all(entering, "tm", 0, 0)
    return pl.pallas_call(
        final_kernel,
        out_shape=shape(GROUPS, STEPS, lines, line_len),
        in_specs=[VMEM] * 13,
        out_specs=HBM,
        scratch_shapes=[
            pltpu.VMEM((2, near_rows, line_len), f32),
            pltpu.VMEM((GROUPS, STEPS, lines, line_len), f32),
            pltpu.SemaphoreType.DMA((STEPS,)),
        ],
        compiler_params=grant,
        name="final",
    )(entering.reshape(sections, LB), params, above, below, weights, *own, *edges)


def solution(mesh):
    in_specs = (
        P("tm", None, "space", None),
        P("tm", "space", None),
        P("space"),
        P("space", None),
        P(),
        P(),
    )
    out_specs = P("tm", None, "space", None)
    return jax.shard_map(shards, mesh=mesh, in_specs=in_specs, out_specs=out_specs, check_vma=False)
```

time: 477 us -> 58.4 us (0.12)
  the two profiles are of different devices: /device:TPU:152 before, /device:TPU:8 now
where the time goes in v2:
time: 58.4 us; the launch traced here: 58.1 us
  blocking collectives  40.8 us (70%)
  Pallas kernels  10.3 us (18%)
  starting transfers between devices  5.56 us (10%)
  local copies, waits for them, and re-layouts  1.2 us (2%)
    all_to_all x1, blocking collectives, shards(): terms = lax.all_to_all(terms.reshape(split), 'tm', 0, 0)  24.2 us
    all_to_all x1, blocking collectives, shards(): entering = lax.all_to_all(entering, 'tm', 0, 0)  16.6 us
    pallas_call x1, Pallas kernels, shards(): pl.pallas_call(own_kernel, out_shape=(shape(lines, line_len), shape(lines...  4.2 us
    ppermute x1, starting transfers between devices, shards(): below = lax.ppermute(down, 'space', [(j, i) for i, j in upward])  3.64 us
    pallas_call x1, Pallas kernels, shards(): pl.pallas_call(edge_kernel, out_shape=(shape(sections, LB), shape(section...  2.71 us
    pallas_call x1, Pallas kernels, shards(): pl.pallas_call(final_kernel, out_shape=shape(GROUPS, STEPS, lines, line_l...  2.23 us
    ppermute x1, starting transfers between devices, shards(): above = lax.ppermute(up, 'space', upward)  1.92 us
    unnamed x9, local copies, waits for them, and re-layouts  1.18 us
  transfers between devices with their start and end apart: 2, of which 0 were waited for; matrix products, arithmetic and copies ran while one was open for 0% of the time, Pallas kernels for 7%

profile of v2, /device:TPU:8, one launch (start us, length us, event | category | flops | bytes accessed | tf_op | source)
XLA Modules:
  0.0 58.1 jit_solution(17705547973374876518)
XLA Ops:
  0.0 0.0 copy-start.3
  0.0 1.1 %pack.1 = (f32[96,256]{1,0:T(8,128)S(1)}, f32[96,256]{1,0:T(8,128)S(1)}, f32[8,128]{1,0:T(8,128)S(1)}) custom-call(f32[2,128,256]{2,1,0:T(8,128)} %starts_ref.3, f32[2,4,128,256]{3,2,1,0:T(8,128)} %sources_ref.3, f32[1,128]{1,0:T(1,128)} %bitcast.21, s32[2,128]{1,0:T(2,128)} %bitcast.20), custom_call_target="tpu_custom_call" | custom-call | tf_op jit(solution)/shard_map/pack/pallas_call | solution.py:308
  1.1 1.9 %collective-permute-start = (f32[96,256]{1,0:T(8,128)S(1)}, f32[96,256]{1,0:T(8,128)S(1)}, u32[]{:S(2)}, u32[]{:S(2)}) collective-permute-start(f32[96,256]{1,0:T(8,128)S(1)} %get-tuple-element.21), channel_id=1, source_target_pairs={{0,1},{1,2},{2,3},{3,4},{4,5},{5,6},{6,7},{8,9},{9,10},{10,11},{11... | collective-permute-start | bytes 294920 | tf_op jit(solution)/shard_map/halo/ppermute | solution.py:331
  3.0 3.6 %collective-permute-start.1 = (f32[96,256]{1,0:T(8,128)S(1)}, f32[96,256]{1,0:T(8,128)S(1)}, u32[]{:S(2)}, u32[]{:S(2)}) collective-permute-start(f32[96,256]{1,0:T(8,128)S(1)} %get-tuple-element.22), channel_id=1, source_target_pairs={{1,0},{2,1},{3,2},{4,3},{5,4},{6,5},{7,6},{9,8},{10,9},{11,10},{12... | collective-permute-start | bytes 294920 | tf_op jit(solution)/shard_map/halo/ppermute | solution.py:332
  6.7 0.0 copy-done.3
  6.7 0.0 copy-start
  6.7 0.1 copy.7
  6.9 0.0 copy-start.1
  7.0 0.0 copy-start.2
  7.0 1.0 %copy-done = f32[2,4,128,256]{3,2,1,0:T(8,128)S(1)} copy-done((f32[2,4,128,256]{3,2,1,0:T(8,128)S(1)}, f32[2,4,128,256]{3,2,1,0:T(8,128)}, u32[]{:S(2)}) %copy-start) | copy-done | bytes 1048600
  7.9 0.1 copy-done.1
  8.0 0.0 copy-done.2
  8.0 4.2 %own.1 = (f32[128,256]{1,0:T(8,128)S(1)}, f32[128,256]{1,0:T(8,128)S(1)}, f32[128,256]{1,0:T(8,128)S(1)}, f32[2,128,256]{2,1,0:T(8,128)S(1)}, f32[2,128,256]{2,1...) custom-call(s32[1,1]{1,0:T(1,128)} %bitcast.1.first_ref, f32[2,128,256]{2,1,0:T(8,128)S(1)} %copy-done.1, ...), custom_call_target="tpu_custom_call" | custom-call | flops 5000000000 | bytes 4000000 | tf_op jit(solution)/shard_map/own/pallas_call | solution.py:354
  12.2 0.0 collective-permute-done.above_ref
  12.2 0.0 collective-permute-done.1.below_ref
  12.3 2.7 %edge.1 = (f32[544,128]{1,0:T(8,128)S(1)}, f32[544,128]{1,0:T(8,128)S(1)}, f32[64,256]{1,0:T(8,128)S(1)}, f32[2,64,256]{2,1,0:T(8,128)S(1)}, f32[2,64,256]{2,1,0:T(8,128)S(1)}, /*index=5*/f32[2,3,64,256]{3,2,1,0:T(8,128)S(1)}) custom-call(s32[1,1]{1,0:T(1,128)} %bitcast.1.first_ref, f32[2,128,256]{2,1,0:T(8,128)S(1)} %copy-done.1, ...), custom_call_target="tpu_custom_call" | custom-call | tf_op jit(solution)/shard_map/edge/pallas_call | solution.py:363
  15.0 24.2 %all_to_all.10.terms_ref = f32[32,1,2176]{2,1,0:T(1,128)S(1)} all-to-all(f32[32,1,2176]{2,1,0:T(1,128)S(1)} %bitcast.18), channel_id=1, replica_groups=mesh['tm'=32,'space'=8] {'tm'}, dimensions={0} | all-to-all | bytes 557056 | tf_op jit(solution)/shard_map/gather_terms/all_to_all | solution.py:375
  39.2 0.1 scan.1
  39.3 16.6 %all_to_all.11 = f32[32,1,2176]{2,1,0:T(1,128)S(1)} all-to-all(f32[32,1,2176]{2,1,0:T(1,128)S(1)} %scan.1), channel_id=1, replica_groups=mesh['tm'=32,'space'=8] {'tm'}, dimensions={0} | all-to-all | bytes 557056 | tf_op jit(solution)/shard_map/return_terms/all_to_all | solution.py:385
  55.9 2.2 %final.1 = f32[2,4,128,256]{3,2,1,0:T(8,128)} custom-call(f32[544,128]{1,0:T(8,128)S(1)} %bitcast.16, f32[8,128]{1,0:T(8,128)S(1)} %get-tuple-element.20.params_ref, f32[96,256]{1,0:T(8,128)S(1)} %collective-permute-done.above_ref, f32[96,256]{1,0:T(8,128)S(1)} %collective-permute-done.1.below_ref, bf16[768,256]{1,0:T(8,128)(2,1)S(1)} %pad_maximum_fusion.weights_ref, ...), custom_call_target="tpu_custom_call" | custom-call | tf_op jit(solution)/shard_map/final/pallas_call | solution.py:386
  (3 shorter events, 0.1 us)
Async XLA Ops:
  0.0 6.7 %copy-start.3 = (f32[4,128,128]{2,1,0:T(8,128)S(1)}, f32[4,128,128]{2,1,0:T(8,128)}, u32[]{:S(2)}) copy-start(f32[4,128,128]{2,1,0:T(8,128)} %param.10) | copy-start | bytes 786436
  1.1 11.1 %collective-permute-start = (f32[96,256]{1,0:T(8,128)S(1)}, f32[96,256]{1,0:T(8,128)S(1)}, u32[]{:S(2)}, u32[]{:S(2)}) collective-permute-start(f32[96,256]{1,0:T(8,128)S(1)} %get-tuple-element.21), channel_id=1, source_target_pairs={{0,1},{1,2},{2,3},{3,4},{4,5},{5,6},{6,7},{8,9},{9,10},{10,11},{11... | collective-permute-start | bytes 294920 | tf_op jit(solution)/shard_map/halo/ppermute | solution.py:331
  3.0 9.2 %collective-permute-start.1 = (f32[96,256]{1,0:T(8,128)S(1)}, f32[96,256]{1,0:T(8,128)S(1)}, u32[]{:S(2)}, u32[]{:S(2)}) collective-permute-start(f32[96,256]{1,0:T(8,128)S(1)} %get-tuple-element.22), channel_id=1, source_target_pairs={{1,0},{2,1},{3,2},{4,3},{5,4},{6,5},{7,6},{9,8},{10,9},{11,10},{12... | collective-permute-start | bytes 294920 | tf_op jit(solution)/shard_map/halo/ppermute | solution.py:332
  6.7 1.2 %copy-start = (f32[2,4,128,256]{3,2,1,0:T(8,128)S(1)}, f32[2,4,128,256]{3,2,1,0:T(8,128)}, u32[]{:S(2)}) copy-start(f32[2,4,128,256]{3,2,1,0:T(8,128)} %sources_ref.3) | copy-start | bytes 3145732
  6.9 1.1 %copy-start.1 = (f32[2,128,256]{2,1,0:T(8,128)S(1)}, f32[2,128,256]{2,1,0:T(8,128)}, u32[]{:S(2)}) copy-start(f32[2,128,256]{2,1,0:T(8,128)} %starts_ref.3) | copy-start | bytes 786436
  7.0 1.1 %copy-start.2 = (f32[4,128]{1,0:T(4,128)S(1)}, f32[4,128]{1,0:T(4,128)}, u32[]{:S(2)}) copy-start(f32[4,128]{1,0:T(4,128)} %rates_ref.3) | copy-start | bytes 6148

commit v3 on v2

--- a/solution.py
+++ b/solution.py
@@ -12,14 +12,13 @@
 STEPS = 4
 SLAB = 16
 EDGE = 8
-SIDE = 4
 REACH = (11, 10, 9, 8, 7)
 GROUP_ROWS = sum(REACH)
 MESSAGE_ROWS = 96
 VMEM = pl.BlockSpec(memory_space=pltpu.VMEM)
 SMEM = pl.BlockSpec(memory_space=pltpu.SMEM)
 HBM = pl.BlockSpec(memory_space=pltpu.HBM)
-VMEM_LIMIT = 32 * 1024 * 1024
+MEBI = 1024 * 1024
 
 
 def columns(row):
@@ -174,7 +173,7 @@
 def edge_kernel(
     first_ref, starts_ref, sources_ref, params_ref, above_ref, below_ref, weights_ref, rates_ref,
     own_term_ref, own_shift_ref, own_decay_ref,
-    terms_ref, factors_ref, decay_ref, base_ref, last_ref, relaxed_ref, halo_ref,
+    terms_ref, factors_ref, shift_ref, decay_ref, base_ref, last_ref, relaxed_ref, halo_ref,
 ):
     lines = starts_ref.shape[1]
     lane = lax.broadcasted_iota(jnp.int32, (8, LB), 1)
@@ -217,17 +216,15 @@
         relaxed_ref[g, m] = field
 
     out = relaxations(starts, sources, coupling, categories, weights_ref[...], rates_ref, first_ref[0, 0], relaxed_to)
-    section = lines + 2 * SIDE
-    decay = joined(own_decay_ref[...], out["decay"], SIDE)
-    for index, field in enumerate(
-        (joined(own_term_ref[...], out["term"], SIDE), joined(own_shift_ref[...], out["shift"], SIDE))
-    ):
-        factor = decay * decay if index == 0 else jnp.zeros_like(decay)
-        for block in range(2):
-            at = (2 * index + block) * section
-            lanes = slice(block * LB, (block + 1) * LB)
-            terms_ref[at : at + section, :] = field[:, lanes]
-            factors_ref[at : at + section, :] = factor[:, lanes]
+    section = lines + 2 * EDGE
+    decay = joined(own_decay_ref[...], out["decay"], EDGE)
+    term = joined(own_term_ref[...], out["term"], EDGE)
+    for block in range(2):
+        at = block * section
+        lanes = slice(block * LB, (block + 1) * LB)
+        terms_ref[at : at + section, :] = term[:, lanes]
+        factors_ref[at : at + section, :] = (decay * decay)[:, lanes]
+    shift_ref[...] = joined(own_shift_ref[...], out["shift"], EDGE)
     decay_ref[...] = out["decay"]
     for g in range(GROUPS):
         base_ref[g] = out["bases"][g]
@@ -243,11 +240,11 @@
 
 
 def final_kernel(
-    entering_ref, params_ref, above_ref, below_ref, weights_ref, decay_ref, base_ref, last_ref, relaxed_ref,
-    edge_decay_ref, edge_base_ref, edge_last_ref, edge_relaxed_ref, states_hbm, field_ref, states_ref, sems,
+    entering_ref, shift_ref, params_ref, above_ref, below_ref, weights_ref, decay_ref, base_ref, last_ref, relaxed_ref,
+    edge_decay_ref, edge_base_ref, edge_last_ref, edge_relaxed_ref, states_hbm, states_ref, sems,
 ):
     lines = last_ref.shape[1]
-    section = lines + 2 * SIDE
+    section = lines + 2 * EDGE
     at = GROUPS * GROUP_ROWS
 
     def along(row):
@@ -260,13 +257,8 @@
     coupling = jnp.concatenate([coupling, coupling], axis=1)
     masks = class_masks([along(1), along(2)])
 
-    gap = EDGE - SIDE
-    field_ref[...] = jnp.zeros_like(field_ref)
-    for part in range(2):
-        for block in range(2):
-            start = (2 * part + block) * section
-            field_ref[part, gap : gap + section, block * LB : (block + 1) * LB] = entering_ref[start : start + section, :]
-    entering, shift = field_ref[0], field_ref[1]
+    entering = jnp.concatenate([entering_ref[:section, :], entering_ref[section:, :]], axis=1)
+    shift = shift_ref[...]
     inner = slice(EDGE, EDGE + lines)
     decay = joined(decay_ref[...], edge_decay_ref[...], EDGE)
     base = [joined(base_ref[g], edge_base_ref[g], EDGE) for g in range(GROUPS)]
@@ -295,11 +287,14 @@
 def shards(sources, starts, coupling, classes, inverses, coarse_rate):
     count, along = lax.axis_size("tm"), lax.axis_size("space")
     lines, line_len = starts.shape[1:]
-    near_rows, sections = lines + 2 * EDGE, 4 * (lines + 2 * SIDE)
+    near_rows = lines + 2 * EDGE
+    sections = 2 * near_rows
     f32 = jnp.float32
     place = lax.axis_index("tm").astype(jnp.int32).reshape(1, 1)
     first = (lax.axis_index("tm") == 0).astype(jnp.int32).reshape(1, 1)
-    grant = pltpu.CompilerParams(vmem_limit_bytes=VMEM_LIMIT)
+
+    def grant(size):
+        return pltpu.CompilerParams(vmem_limit_bytes=size * MEBI)
 
     def shape(*dims):
         return jax.ShapeDtypeStruct(dims, f32)
@@ -319,7 +314,7 @@
             pltpu.VMEM((2, lines), jnp.int32),
             pltpu.SemaphoreType.DMA((6,)),
         ],
-        compiler_params=grant,
+        compiler_params=grant(4),
         name="pack",
     )(*[
         pltpu.with_memory_space_constraint(x, pltpu.HBM)
@@ -356,21 +351,23 @@
         out_shape=(shape(lines, line_len), shape(lines, line_len), *kept(lines)),
         in_specs=[SMEM] + [VMEM] * 5,
         out_specs=[VMEM] * 6,
-        compiler_params=grant,
+        compiler_params=grant(24),
         cost_estimate=pl.CostEstimate(flops=5_000_000_000, bytes_accessed=4_000_000, transcendentals=0),
         name="own",
     )(first, starts, sources, params, weights, coarse_rate)
-    terms, factors, *edges = pl.pallas_call(
+    terms, factors, shift, *edges = pl.pallas_call(
         edge_kernel,
-        out_shape=(shape(sections, LB), shape(sections, LB), *kept(4 * SLAB)),
+        out_shape=(shape(sections, LB), shape(sections, LB), shape(near_rows, line_len), *kept(4 * SLAB)),
         in_specs=[SMEM] + [VMEM] * 10,
-        out_specs=[VMEM] * 6,
+        out_specs=[VMEM] * 7,
         scratch_shapes=[pltpu.VMEM((GROUPS * len(REACH), 2 * SLAB, line_len), f32)],
-        compiler_params=grant,
+        compiler_params=grant(20),
         name="edge",
     )(first, starts, sources, params, above, below, weights, coarse_rate, term, shift, own[0])
 
     split = (count, 1, sections * LB // count)
+    with jax.named_scope("onward"):
+        shift = lax.ppermute(shift, "tm", [(i, i + 1) for i in range(count - 1)])
     with jax.named_scope("gather_terms"):
         terms = lax.all_to_all(terms.reshape(split), "tm", 0, 0)
     entering = pl.pallas_call(
@@ -378,7 +375,7 @@
         out_shape=shape(*split),
         in_specs=[SMEM] + [VMEM] * 2,
         out_specs=VMEM,
-        compiler_params=grant,
+        compiler_params=grant(4),
         name="scan",
     )(place, terms, factors.reshape(split))
     with jax.named_scope("return_terms"):
@@ -386,16 +383,15 @@
     return pl.pallas_call(
         final_kernel,
         out_shape=shape(GROUPS, STEPS, lines, line_len),
-        in_specs=[VMEM] * 13,
+        in_specs=[VMEM] * 14,
         out_specs=HBM,
         scratch_shapes=[
-            pltpu.VMEM((2, near_rows, line_len), f32),
             pltpu.VMEM((GROUPS, STEPS, lines, line_len), f32),
             pltpu.SemaphoreType.DMA((STEPS,)),
         ],
-        compiler_params=grant,
+        compiler_params=grant(20),
         name="final",
-    )(entering.reshape(sections, LB), params, above, below, weights, *own, *edges)
+    )(entering.reshape(sections, LB), shift, params, above, below, weights, *own, *edges)
 
 
 def solution(mesh):

time: 58.4 us -> 56.3 us (0.964)
  blocking collectives: 40.8 us -> 22 us
  waiting for transfers between devices: 0.01 us -> 7.79 us
  starting transfers between devices: 5.56 us -> 13.1 us
  local copies, waits for them, and re-layouts: 1.2 us -> 1.87 us
  Pallas kernels: 10.3 us -> 10.9 us
    all_to_all x1 -> x0, blocking collectives: 16.6 us -> none  [shards(): entering = lax.all_to_all(entering, 'tm', 0, 0)]
    all_to_all x0 -> x1, waiting for transfers between devices: none -> 4.82 us  [shards(): entering = lax.all_to_all(entering, 'tm', 0, 0)]
    all_to_all x0 -> x1, starting transfers between devices: none -> 4 us  [shards(): entering = lax.all_to_all(entering, 'tm', 0, 0)]
    ppermute x0 -> x1, starting transfers between devices: none -> 3.59 us  [shards(): shift = lax.ppermute(shift, 'tm', [(i, i + 1) for i in range(count - 1)])]
    ppermute x0 -> x1, waiting for transfers between devices: none -> 2.96 us  [shards(): shift = lax.ppermute(shift, 'tm', [(i, i + 1) for i in range(count - 1)])]
    all_to_all x1, blocking collectives: 24.2 us -> 22 us  [shards(): terms = lax.all_to_all(terms.reshape(split), 'tm', 0, 0)]
    unnamed x9 -> x21, local copies, waits for them, and re-layouts: 1.18 us -> 1.85 us
    pallas_call x1, Pallas kernels: 0.07 us -> 0.73 us  [shards(): pl.pallas_call(scan_kernel, out_shape=shape(*split), in_specs=[SMEM] + [V...]
  transfers between devices with their start and end apart: 2 -> 4, of which waited for: 0 -> 2; matrix products, arithmetic and copies ran while one was open for 0% -> 0% of each run, Pallas kernels for 7% -> 7%
where the time goes in v3:
time: 56.3 us; the launch traced here: 55.9 us
  blocking collectives  22 us (39%)
  starting transfers between devices  13.1 us (23%)
  Pallas kernels  10.9 us (19%)
  waiting for transfers between devices  7.79 us (14%)
  local copies, waits for them, and re-layouts  1.87 us (3%)
    all_to_all x1, blocking collectives, shards(): terms = lax.all_to_all(terms.reshape(split), 'tm', 0, 0)  22 us
    all_to_all x1, waiting for transfers between devices, shards(): entering = lax.all_to_all(entering, 'tm', 0, 0)  4.82 us
    pallas_call x1, Pallas kernels, shards(): pl.pallas_call(own_kernel, out_shape=(shape(lines, line_len), shape(lines...  4.17 us
    all_to_all x1, starting transfers between devices, shards(): entering = lax.all_to_all(entering, 'tm', 0, 0)  4 us
    ppermute x1, starting transfers between devices, shards(): below = lax.ppermute(down, 'space', [(j, i) for i, j in upward])  3.64 us
    ppermute x1, starting transfers between devices, shards(): shift = lax.ppermute(shift, 'tm', [(i, i + 1) for i in range(count - 1)])  3.59 us
    ppermute x1, waiting for transfers between devices, shards(): shift = lax.ppermute(shift, 'tm', [(i, i + 1) for i in range(count - 1)])  2.96 us
    pallas_call x1, Pallas kernels, shards(): pl.pallas_call(edge_kernel, out_shape=(shape(sections, LB), shape(section...  2.69 us
  transfers between devices with their start and end apart: 4, of which 2 were waited for; matrix products, arithmetic and copies ran while one was open for 0% of the time, Pallas kernels for 7%

profile of v3, /device:TPU:8, one launch (start us, length us, event | category | flops | bytes accessed | tf_op | source)
XLA Modules:
  0.0 55.9 jit_solution(7988299078145496310)
XLA Ops:
  0.0 0.0 copy-start.9
  0.0 1.1 %pack.1 = (f32[96,256]{1,0:T(8,128)S(1)}, f32[96,256]{1,0:T(8,128)S(1)}, f32[8,128]{1,0:T(8,128)S(1)}) custom-call(f32[2,128,256]{2,1,0:T(8,128)} %starts_ref.3, f32[2,4,128,256]{3,2,1,0:T(8,128)} %sources_ref.3, f32[1,128]{1,0:T(1,128)} %bitcast.21, s32[2,128]{1,0:T(2,128)} %bitcast.20), custom_call_target="tpu_custom_call" | custom-call | tf_op jit(solution)/shard_map/pack/pallas_call | solution.py:303
  1.1 1.9 %collective-permute-start = (f32[96,256]{1,0:T(8,128)S(1)}, f32[96,256]{1,0:T(8,128)S(1)}, u32[]{:S(2)}, u32[]{:S(2)}) collective-permute-start(f32[96,256]{1,0:T(8,128)S(1)} %get-tuple-element.22), channel_id=1, source_target_pairs={{0,1},{1,2},{2,3},{3,4},{4,5},{5,6},{6,7},{8,9},{9,10},{10,11},{11... | collective-permute-start | bytes 294920 | tf_op jit(solution)/shard_map/halo/ppermute | solution.py:326
  3.0 3.6 %collective-permute-start.1 = (f32[96,256]{1,0:T(8,128)S(1)}, f32[96,256]{1,0:T(8,128)S(1)}, u32[]{:S(2)}, u32[]{:S(2)}) collective-permute-start(f32[96,256]{1,0:T(8,128)S(1)} %get-tuple-element.23), channel_id=1, source_target_pairs={{1,0},{2,1},{3,2},{4,3},{5,4},{6,5},{7,6},{9,8},{10,9},{11,10},{12... | collective-permute-start | bytes 294920 | tf_op jit(solution)/shard_map/halo/ppermute | solution.py:327
  6.7 0.0 copy-done.9
  6.7 0.0 copy-start
  6.7 0.1 copy.7
  6.9 0.0 copy-start.1
  7.0 0.0 copy-start.6
  7.0 1.0 %copy-done = f32[2,4,128,256]{3,2,1,0:T(8,128)S(1)} copy-done((f32[2,4,128,256]{3,2,1,0:T(8,128)S(1)}, f32[2,4,128,256]{3,2,1,0:T(8,128)}, u32[]{:S(2)}) %copy-start) | copy-done | bytes 1048600
  7.9 0.1 copy-done.1
  8.0 0.0 copy-done.6
  8.0 4.2 %own.1 = (f32[128,256]{1,0:T(8,128)S(1)}, f32[128,256]{1,0:T(8,128)S(1)}, f32[128,256]{1,0:T(8,128)S(1)}, f32[2,128,256]{2,1,0:T(8,128)S(1)}, f32[2,128,256]{2,1...) custom-call(s32[1,1]{1,0:T(1,128)} %bitcast.1.first_ref, f32[2,128,256]{2,1,0:T(8,128)S(1)} %copy-done.1, ...), custom_call_target="tpu_custom_call" | custom-call | flops 5000000000 | bytes 4000000 | tf_op jit(solution)/shard_map/own/pallas_call | solution.py:349
  12.2 0.0 collective-permute-done.above_ref
  12.2 0.0 collective-permute-done.1.below_ref
  12.2 2.7 %edge.1 = (f32[288,128]{1,0:T(8,128)S(1)}, f32[288,128]{1,0:T(8,128)S(1)}, f32[144,256]{1,0:T(8,128)S(1)}, f32[64,256]{1,0:T(8,128)S(1)}, f32[2,64,256]{2,1,0:T(...) custom-call(s32[1,1]{1,0:T(1,128)} %bitcast.1.first_ref, f32[2,128,256]{2,1,0:T(8,128)S(1)} %copy-done.1, ...), custom_call_target="tpu_custom_call" | custom-call | tf_op jit(solution)/shard_map/edge/pallas_call | solution.py:358
  14.9 0.0 copy-start.7
  14.9 0.6 %copy-done.7 = f32[144,256]{1,0:T(8,128)} copy-done((f32[144,256]{1,0:T(8,128)}, f32[144,256]{1,0:T(8,128)S(1)}, u32[]{:S(2)}) %copy-start.7) | copy-done | bytes 147480
  15.6 0.0 copy-start.2
  15.6 0.0 copy-start.4
  15.6 22.0 %all_to_all.10.terms_ref = f32[32,1,1152]{2,1,0:T(1,128)S(1)} all-to-all(f32[32,1,1152]{2,1,0:T(1,128)S(1)} %bitcast.17), channel_id=1, replica_groups=mesh['tm'=32,'space'=8] {'tm'}, dimensions={0} | all-to-all | bytes 294912 | tf_op jit(solution)/shard_map/gather_terms/all_to_all | solution.py:372
  37.6 0.0 copy-done.2
  37.6 0.0 copy-done.4
  37.6 0.0 copy-start.8
  37.6 0.7 %scan.1 = f32[32,1,1152]{2,1,0:T(1,128)} custom-call(s32[1,1]{1,0:T(1,128)} %bitcast.place_ref, f32[32,1,1152]{2,1,0:T(1,128)S(1)} %all_to_all.10.terms_ref, f32[32,1,1152]{2,1,0:T(1,128)S(1)} %bitcast.18), custom_call_target="tpu_custom_call" | custom-call | tf_op jit(solution)/shard_map/scan/pallas_call | solution.py:373
  38.3 0.0 copy-start.3
  38.3 0.0 copy-start.5
  38.3 4.0 %all-to-all-start.1 = ((f32[32,1,1152]{2,1,0:T(1,128)}), f32[32,1,1152]{2,1,0:T(1,128)S(1)}, u32[]{:S(2)}, u32[]{:S(2)}) async-start(f32[32,1,1152]{2,1,0:T(1,128)} %scan.1), calls=%async_computation.1 | async-start | bytes 294912 | tf_op jit(solution)/shard_map/return_terms/all_to_all | solution.py:382
  42.3 0.0 copy-done.8
  42.4 3.6 %collective-permute-start.2 = (f32[144,256]{1,0:T(8,128)S(1)}, f32[144,256]{1,0:T(8,128)S(1)}, u32[]{:S(2)}, u32[]{:S(2)}) collective-permute-start(f32[144,256]{1,0:T(8,128)S(1)} %copy-done.8), channel_id=1, source_target_pairs={{0,8},{8,16},{16,24},{24,32},{32,40},{40,48},{48,56},{56,64},{64,7... | collective-permute-start | bytes 442376 | tf_op jit(solution)/shard_map/onward/ppermute | solution.py:370
  46.0 3.0 %collective-permute-done.2.shift_ref = f32[144,256]{1,0:T(8,128)S(1)} collective-permute-done((f32[144,256]{1,0:T(8,128)S(1)}, f32[144,256]{1,0:T(8,128)S(1)}, u32[]{:S(2)}, u32[]{:S(2)}) %collective-permute-start.2) | collective-permute-done | bytes 147488 | tf_op jit(solution)/shard_map/onward/ppermute | solution.py:370
  48.9 4.8 %all-to-all-done.1 = f32[32,1,1152]{2,1,0:T(1,128)S(1)} async-done(((f32[32,1,1152]{2,1,0:T(1,128)}), f32[32,1,1152]{2,1,0:T(1,128)S(1)}, u32[]{:S(2)}, u32[]{:S(2)}) %all-to-all-start.1) | async-done | bytes 147488 | tf_op jit(solution)/shard_map/return_terms/all_to_all | solution.py:382
  53.7 0.0 copy-done.3
  53.7 0.0 copy-done.5
  53.8 2.2 %final.1 = f32[2,4,128,256]{3,2,1,0:T(8,128)} custom-call(f32[288,128]{1,0:T(8,128)S(1)} %bitcast.16, f32[144,256]{1,0:T(8,128)S(1)} %collective-permute-done.2.shift_ref, f32[8,128]{1,0:T(8,128)S(1)} %get-tuple-element.21.params_ref, f32[96,256]{1,0:T(8,128)S(1)} %collective-permute-done.above_ref, f32[96,256]{1,0:T(8,128)S(1)} %collective-permute-done.1.below_ref, ...), custom_call_target="tpu_custom_call" | custom-call | tf_op jit(solution)/shard_map/final/pallas_call | solution.py:383
  (3 shorter events, 0.1 us)
Async XLA Ops:
  0.0 6.7 %copy-start.9 = (f32[4,128,128]{2,1,0:T(8,128)S(1)}, f32[4,128,128]{2,1,0:T(8,128)}, u32[]{:S(2)}) copy-start(f32[4,128,128]{2,1,0:T(8,128)} %param.10) | copy-start | bytes 786436
  1.1 11.1 %collective-permute-start = (f32[96,256]{1,0:T(8,128)S(1)}, f32[96,256]{1,0:T(8,128)S(1)}, u32[]{:S(2)}, u32[]{:S(2)}) collective-permute-start(f32[96,256]{1,0:T(8,128)S(1)} %get-tuple-element.22), channel_id=1, source_target_pairs={{0,1},{1,2},{2,3},{3,4},{4,5},{5,6},{6,7},{8,9},{9,10},{10,11},{11... | collective-permute-start | bytes 294920 | tf_op jit(solution)/shard_map/halo/ppermute | solution.py:326
  3.0 9.2 %collective-permute-start.1 = (f32[96,256]{1,0:T(8,128)S(1)}, f32[96,256]{1,0:T(8,128)S(1)}, u32[]{:S(2)}, u32[]{:S(2)}) collective-permute-start(f32[96,256]{1,0:T(8,128)S(1)} %get-tuple-element.23), channel_id=1, source_target_pairs={{1,0},{2,1},{3,2},{4,3},{5,4},{6,5},{7,6},{9,8},{10,9},{11,10},{12... | collective-permute-start | bytes 294920 | tf_op jit(solution)/shard_map/halo/ppermute | solution.py:327
  6.7 1.2 %copy-start = (f32[2,4,128,256]{3,2,1,0:T(8,128)S(1)}, f32[2,4,128,256]{3,2,1,0:T(8,128)}, u32[]{:S(2)}) copy-start(f32[2,4,128,256]{3,2,1,0:T(8,128)} %sources_ref.3) | copy-start | bytes 3145732
  6.9 1.1 %copy-start.1 = (f32[2,128,256]{2,1,0:T(8,128)S(1)}, f32[2,128,256]{2,1,0:T(8,128)}, u32[]{:S(2)}) copy-start(f32[2,128,256]{2,1,0:T(8,128)} %starts_ref.3) | copy-start | bytes 786436
  7.0 1.1 %copy-start.6 = (f32[4,128]{1,0:T(4,128)S(1)}, f32[4,128]{1,0:T(4,128)}, u32[]{:S(2)}) copy-start(f32[4,128]{1,0:T(4,128)} %rates_ref.3) | copy-start | bytes 6148
  14.9 0.7 %copy-start.7 = (f32[144,256]{1,0:T(8,128)}, f32[144,256]{1,0:T(8,128)S(1)}, u32[]{:S(2)}) copy-start(f32[144,256]{1,0:T(8,128)S(1)} %get-tuple-element.29) | copy-start | bytes 442372
  15.6 22.0 %copy-start.2 = (f32[2,64,256]{2,1,0:T(8,128)}, f32[2,64,256]{2,1,0:T(8,128)S(1)}, u32[]{:S(2)}) copy-start(f32[2,64,256]{2,1,0:T(8,128)S(1)} %get-tuple-element.34.edge_base_ref) | copy-start | bytes 393220
  15.6 22.0 %copy-start.4 = (f32[2,64,256]{2,1,0:T(8,128)}, f32[2,64,256]{2,1,0:T(8,128)S(1)}, u32[]{:S(2)}) copy-start(f32[2,64,256]{2,1,0:T(8,128)S(1)} %get-tuple-element.35.edge_last_ref) | copy-start | bytes 393220
  37.6 4.7 %copy-start.8 = (f32[144,256]{1,0:T(8,128)S(1)}, f32[144,256]{1,0:T(8,128)}, u32[]{:S(2)}) copy-start(f32[144,256]{1,0:T(8,128)} %copy-done.7) | copy-start | bytes 442372
  38.3 15.4 %copy-start.3 = (f32[2,64,256]{2,1,0:T(8,128)S(1)}, f32[2,64,256]{2,1,0:T(8,128)}, u32[]{:S(2)}) copy-start(f32[2,64,256]{2,1,0:T(8,128)} %copy-done.2) | copy-start | bytes 393220
  38.3 15.4 %copy-start.5 = (f32[2,64,256]{2,1,0:T(8,128)S(1)}, f32[2,64,256]{2,1,0:T(8,128)}, u32[]{:S(2)}) copy-start(f32[2,64,256]{2,1,0:T(8,128)} %copy-done.4) | copy-start | bytes 393220
  38.3 15.4 %all-to-all-start.1 = ((f32[32,1,1152]{2,1,0:T(1,128)}), f32[32,1,1152]{2,1,0:T(1,128)S(1)}, u32[]{:S(2)}, u32[]{:S(2)}) async-start(f32[32,1,1152]{2,1,0:T(1,128)} %scan.1), calls=%async_computation.1 | async-start | bytes 294912 | tf_op jit(solution)/shard_map/return_terms/all_to_all | solution.py:382
  42.4 6.6 %collective-permute-start.2 = (f32[144,256]{1,0:T(8,128)S(1)}, f32[144,256]{1,0:T(8,128)S(1)}, u32[]{:S(2)}, u32[]{:S(2)}) collective-permute-start(f32[144,256]{1,0:T(8,128)S(1)} %copy-done.8), channel_id=1, source_target_pairs={{0,8},{8,16},{16,24},{24,32},{32,40},{40,48},{48,56},{56,64},{64,7... | collective-permute-start | bytes 442376 | tf_op jit(solution)/shard_map/onward/ppermute | solution.py:370

commit v4 on v3

--- a/solution.py
+++ b/solution.py
@@ -46,27 +46,27 @@
     return jnp.concatenate(blocks, axis=1)
 
 
+def solve_field(field, masks, weights):
+    even, odd, upper = masks
+    rows = field.shape[0]
+    left = []
+    for block in range(2):
+        x = field[:, block * LB : (block + 1) * LB]
+        high = x.astype(jnp.bfloat16)
+        low = (x - high.astype(jnp.float32)).astype(jnp.bfloat16)
+        high_pair = [high * even[block], high * odd[block]]
+        low_pair = [low * even[block], low * odd[block]]
+        left.append(jnp.concatenate(high_pair + low_pair + high_pair, axis=1))
+    product = jnp.dot(jnp.concatenate(left, axis=0), weights, preferred_element_type=jnp.float32)
+    blocks = []
+    for block in range(2):
+        part = product[block * rows : (block + 1) * rows]
+        blocks.append(jnp.where(upper[block], part[:, LB:], part[:, :LB]))
+    return jnp.concatenate(blocks, axis=1)
+
+
 def solve_lines(fields, masks, weights):
-    even, odd, upper = masks
-    rows = fields[0].shape[0]
-    left = []
-    for field in fields:
-        for block in range(2):
-            x = field[:, block * LB : (block + 1) * LB]
-            high = x.astype(jnp.bfloat16)
-            low = (x - high.astype(jnp.float32)).astype(jnp.bfloat16)
-            high_pair = [high * even[block], high * odd[block]]
-            low_pair = [low * even[block], low * odd[block]]
-            left.append(jnp.concatenate(high_pair + low_pair + high_pair, axis=1))
-    product = jnp.dot(jnp.concatenate(left, axis=0), weights, preferred_element_type=jnp.float32)
-    results = []
-    for index in range(len(fields)):
-        blocks = []
-        for block in range(2):
-            part = product[(2 * index + block) * rows : (2 * index + block + 1) * rows]
-            blocks.append(jnp.where(upper[block], part[:, LB:], part[:, :LB]))
-        results.append(jnp.concatenate(blocks, axis=1))
-    return results
+    return [solve_field(field, masks, weights) for field in fields]
 
 
 def spread(field, coupling):
@@ -106,7 +106,7 @@
 
 
 def pack_kernel(
-    starts_hbm, sources_hbm, coupling_hbm, classes_hbm, up_ref, down_ref, params_ref,
+    starts_hbm, sources_hbm, coupling_hbm, classes_hbm, up_ref, down_ref, params_ref, starts_ref, sources_ref,
     starts_low, starts_high, sources_low, sources_high, coupling_row, classes_rows, sems,
 ):
     lines = starts_hbm.shape[1]
@@ -118,13 +118,16 @@
         (starts_hbm.at[:, low, :], starts_low),
         (coupling_hbm, coupling_row),
         (classes_hbm, classes_rows),
+        (starts_hbm, starts_ref),
+        (sources_hbm, sources_ref),
     ]
+    whole = 2
     copies = [pltpu.make_async_copy(src, dst, sems.at[i]) for i, (src, dst) in enumerate(pairs)]
     for copy in copies:
         copy.start()
     for ref in (up_ref, down_ref, params_ref):
         ref[...] = jnp.zeros_like(ref)
-    for copy in copies:
+    for copy in copies[:-whole]:
         copy.wait()
     params_ref[0:1, :] = coupling_row[...]
     params_ref[1:3, :] = classes_rows[...].astype(jnp.float32)
@@ -140,6 +143,8 @@
             at += reach
     for ref in (up_ref, down_ref):
         ref[GROUPS * GROUP_ROWS : GROUPS * GROUP_ROWS + 3, :LB] = params_ref[0:3, :]
+    for copy in copies[-whole:]:
+        copy.wait()
 
 
 def own_kernel(
@@ -300,11 +305,11 @@
         return jax.ShapeDtypeStruct(dims, f32)
 
     message = shape(MESSAGE_ROWS, line_len)
-    up, down, params = pl.pallas_call(
+    up, down, params, held_starts, held_sources = pl.pallas_call(
         pack_kernel,
-        out_shape=(message, message, shape(8, lines)),
+        out_shape=(message, message, shape(8, lines), shape(*starts.shape), shape(*sources.shape)),
         in_specs=[HBM] * 4,
-        out_specs=[VMEM] * 3,
+        out_specs=[VMEM] * 5,
         scratch_shapes=[
             pltpu.VMEM((GROUPS, SLAB, line_len), f32),
             pltpu.VMEM((GROUPS, SLAB, line_len), f32),
@@ -312,9 +317,9 @@
             pltpu.VMEM((GROUPS, STEPS, SLAB, line_len), f32),
             pltpu.VMEM((1, lines), f32),
             pltpu.VMEM((2, lines), jnp.int32),
-            pltpu.SemaphoreType.DMA((6,)),
+            pltpu.SemaphoreType.DMA((8,)),
         ],
-        compiler_params=grant(4),
+        compiler_params=grant(6),
         name="pack",
     )(*[
         pltpu.with_memory_space_constraint(x, pltpu.HBM)
@@ -354,7 +359,7 @@
         compiler_params=grant(24),
         cost_estimate=pl.CostEstimate(flops=5_000_000_000, bytes_accessed=4_000_000, transcendentals=0),
         name="own",
-    )(first, starts, sources, params, weights, coarse_rate)
+    )(first, held_starts, held_sources, params, weights, coarse_rate)
     terms, factors, shift, *edges = pl.pallas_call(
         edge_kernel,
         out_shape=(shape(sections, LB), shape(sections, LB), shape(near_rows, line_len), *kept(4 * SLAB)),
@@ -363,7 +368,7 @@
         scratch_shapes=[pltpu.VMEM((GROUPS * len(REACH), 2 * SLAB, line_len), f32)],
         compiler_params=grant(20),
         name="edge",
-    )(first, starts, sources, params, above, below, weights, coarse_rate, term, shift, own[0])
+    )(first, held_starts, held_sources, params, above, below, weights, coarse_rate, term, shift, own[0])
 
     split = (count, 1, sections * LB // count)
     with jax.named_scope("onward"):
@@ -372,7 +377,7 @@
         terms = lax.all_to_all(terms.reshape(split), "tm", 0, 0)
     entering = pl.pallas_call(
         scan_kernel,
-        out_shape=shape(*split),
+        out_shape=pltpu.VMEM(split, f32),
         in_specs=[SMEM] + [VMEM] * 2,
         out_specs=VMEM,
         compiler_params=grant(4),

time: 56.3 us -> 54.5 us (0.968)
  Pallas kernels: 10.9 us -> 9.12 us
    pallas_call x1, Pallas kernels: 4.17 us -> 2.72 us  [shards(): pl.pallas_call(own_kernel, out_shape=(shape(lines, line_len), shape(lines...]
    pallas_call x1, Pallas kernels: 2.69 us -> 2.03 us  [shards(): pl.pallas_call(edge_kernel, out_shape=(shape(sections, LB), shape(section...]
  transfers between devices with their start and end apart: 4 -> 4, of which waited for: 2 -> 2; matrix products, arithmetic and copies ran while one was open for 0% -> 0% of each run, Pallas kernels for 7% -> 5%
where the time goes in v4:
time: 54.5 us; the launch traced here: 54.2 us
  blocking collectives  22.3 us (41%)
  starting transfers between devices  13.1 us (24%)
  Pallas kernels  9.12 us (17%)
  waiting for transfers between devices  7.88 us (14%)
  local copies, waits for them, and re-layouts  1.5 us (3%)
    all_to_all x1, blocking collectives, shards(): terms = lax.all_to_all(terms.reshape(split), 'tm', 0, 0)  22.3 us
    all_to_all x1, waiting for transfers between devices, shards(): entering = lax.all_to_all(entering, 'tm', 0, 0)  4.86 us
    all_to_all x1, starting transfers between devices, shards(): entering = lax.all_to_all(entering, 'tm', 0, 0)  3.99 us
    ppermute x1, starting transfers between devices, shards(): below = lax.ppermute(down, 'space', [(j, i) for i, j in upward])  3.64 us
    ppermute x1, starting transfers between devices, shards(): shift = lax.ppermute(shift, 'tm', [(i, i + 1) for i in range(count - 1)])  3.59 us
    ppermute x1, waiting for transfers between devices, shards(): shift = lax.ppermute(shift, 'tm', [(i, i + 1) for i in range(count - 1)])  3.01 us
    pallas_call x1, Pallas kernels, shards(): pl.pallas_call(own_kernel, out_shape=(shape(lines, line_len), shape(lines...  2.72 us
    pallas_call x1, Pallas kernels, shards(): pl.pallas_call(edge_kernel, out_shape=(shape(sections, LB), shape(section...  2.03 us
  transfers between devices with their start and end apart: 4, of which 2 were waited for; matrix products, arithmetic and copies ran while one was open for 0% of the time, Pallas kernels for 5%

profile of v4, /device:TPU:8, one launch (start us, length us, event | category | flops | bytes accessed | tf_op | source)
XLA Modules:
  0.0 54.2 jit_solution(6190596650996431458)
XLA Ops:
  0.0 0.0 copy-start.9
  0.0 1.6 %pack.1 = (f32[96,256]{1,0:T(8,128)S(1)}, f32[96,256]{1,0:T(8,128)S(1)}, f32[8,128]{1,0:T(8,128)S(1)}, f32[2,128,256]{2,1,0:T(8,128)S(1)}, f32[2,4,128,256]{3,2,1,0:T(8,128)S(1)}) custom-call(f32[2,128,256]{2,1,0:T(8,128)} %starts_hbm.1, f32[2,4,128,256]{3,2,1,0:T(8,128)} %sources_hbm.1, f32[1,128]{1,0:T(1,128)} %bitcast.21, s32[2,128]{1,0:T(2,128)} %bitcast.20), custom_call_target="tpu_custom_call" | custom-call | tf_op jit(solution)/shard_map/pack/pallas_call | solution.py:308
  1.6 1.9 %collective-permute-start = (f32[96,256]{1,0:T(8,128)S(1)}, f32[96,256]{1,0:T(8,128)S(1)}, u32[]{:S(2)}, u32[]{:S(2)}) collective-permute-start(f32[96,256]{1,0:T(8,128)S(1)} %get-tuple-element.26), channel_id=1, source_target_pairs={{0,1},{1,2},{2,3},{3,4},{4,5},{5,6},{6,7},{8,9},{9,10},{10,11},{11... | collective-permute-start | bytes 294920 | tf_op jit(solution)/shard_map/halo/ppermute | solution.py:331
  3.6 3.6 %collective-permute-start.1 = (f32[96,256]{1,0:T(8,128)S(1)}, f32[96,256]{1,0:T(8,128)S(1)}, u32[]{:S(2)}, u32[]{:S(2)}) collective-permute-start(f32[96,256]{1,0:T(8,128)S(1)} %get-tuple-element.27), channel_id=1, source_target_pairs={{1,0},{2,1},{3,2},{4,3},{5,4},{6,5},{7,6},{9,8},{10,9},{11,10},{12... | collective-permute-start | bytes 294920 | tf_op jit(solution)/shard_map/halo/ppermute | solution.py:332
  7.2 0.0 copy-done.9
  7.2 0.1 copy.7
  7.5 0.0 copy-start.6
  7.5 0.7 %copy-done.6 = f32[4,128]{1,0:T(4,128)S(1)} copy-done((f32[4,128]{1,0:T(4,128)S(1)}, f32[4,128]{1,0:T(4,128)}, u32[]{:S(2)}) %copy-start.6) | copy-done | bytes 2072
  8.2 2.7 %own.1 = (f32[128,256]{1,0:T(8,128)S(1)}, f32[128,256]{1,0:T(8,128)S(1)}, f32[128,256]{1,0:T(8,128)S(1)}, f32[2,128,256]{2,1,0:T(8,128)S(1)}, f32[2,128,256]{2,1...) custom-call(s32[1,1]{1,0:T(1,128)} %bitcast.1.first_ref, f32[2,128,256]{2,1,0:T(8,128)S(1)} %get-tuple-element.23.starts_ref, ...), custom_call_target="tpu_custom_call" | custom-call | flops 5000000000 | bytes 4000000 | tf_op jit(solution)/shard_map/own/pallas_call | solution.py:354
  10.9 0.0 copy-start
  10.9 0.0 collective-permute-done.above_ref
  10.9 0.0 collective-permute-done.1.below_ref
  10.9 2.0 %edge.1 = (f32[288,128]{1,0:T(8,128)S(1)}, f32[288,128]{1,0:T(8,128)S(1)}, f32[144,256]{1,0:T(8,128)S(1)}, f32[64,256]{1,0:T(8,128)S(1)}, f32[2,64,256]{2,1,0:T(...) custom-call(s32[1,1]{1,0:T(1,128)} %bitcast.1.first_ref, ...), custom_call_target="tpu_custom_call" | custom-call | tf_op jit(solution)/shard_map/edge/pallas_call | solution.py:363
  12.9 0.0 copy-done
  13.0 0.0 copy-start.7
  13.0 0.6 %copy-done.7 = f32[144,256]{1,0:T(8,128)} copy-done((f32[144,256]{1,0:T(8,128)}, f32[144,256]{1,0:T(8,128)S(1)}, u32[]{:S(2)}) %copy-start.7) | copy-done | bytes 147480
  13.6 0.0 copy-start.2
  13.6 0.0 copy-start.4
  13.6 22.3 %all_to_all.10.terms_ref = f32[32,1,1152]{2,1,0:T(1,128)S(1)} all-to-all(f32[32,1,1152]{2,1,0:T(1,128)S(1)} %bitcast.17), channel_id=1, replica_groups=mesh['tm'=32,'space'=8] {'tm'}, dimensions={0} | all-to-all | bytes 294912 | tf_op jit(solution)/shard_map/gather_terms/all_to_all | solution.py:377
  35.9 0.0 copy-done.2
  35.9 0.0 copy-done.4
  35.9 0.0 copy-start.8
  35.9 0.0 copy-start.3
  35.9 0.0 copy-start.5
  35.9 0.7 %scan.1 = f32[32,1,1152]{2,1,0:T(1,128)} custom-call(s32[1,1]{1,0:T(1,128)} %bitcast.place_ref, f32[32,1,1152]{2,1,0:T(1,128)S(1)} %all_to_all.10.terms_ref, f32[32,1,1152]{2,1,0:T(1,128)S(1)} %bitcast.18), custom_call_target="tpu_custom_call" | custom-call | tf_op jit(solution)/shard_map/scan/pallas_call | solution.py:378
  36.7 0.0 copy-start.1
  36.7 4.0 %all-to-all-start.1 = ((f32[32,1,1152]{2,1,0:T(1,128)}), f32[32,1,1152]{2,1,0:T(1,128)S(1)}, u32[]{:S(2)}, u32[]{:S(2)}) async-start(f32[32,1,1152]{2,1,0:T(1,128)} %scan.1), calls=%async_computation.1 | async-start | bytes 294912 | tf_op jit(solution)/shard_map/return_terms/all_to_all | solution.py:387
  40.7 0.0 copy-done.8
  40.7 3.6 %collective-permute-start.2 = (f32[144,256]{1,0:T(8,128)S(1)}, f32[144,256]{1,0:T(8,128)S(1)}, u32[]{:S(2)}, u32[]{:S(2)}) collective-permute-start(f32[144,256]{1,0:T(8,128)S(1)} %copy-done.8), channel_id=1, source_target_pairs={{0,8},{8,16},{16,24},{24,32},{32,40},{40,48},{48,56},{56,64},{64,7... | collective-permute-start | bytes 442376 | tf_op jit(solution)/shard_map/onward/ppermute | solution.py:375
  44.3 3.0 %collective-permute-done.2.shift_ref = f32[144,256]{1,0:T(8,128)S(1)} collective-permute-done((f32[144,256]{1,0:T(8,128)S(1)}, f32[144,256]{1,0:T(8,128)S(1)}, u32[]{:S(2)}, u32[]{:S(2)}) %collective-permute-start.2) | collective-permute-done | bytes 147488 | tf_op jit(solution)/shard_map/onward/ppermute | solution.py:375
  47.3 4.9 %all-to-all-done.1 = f32[32,1,1152]{2,1,0:T(1,128)S(1)} async-done(((f32[32,1,1152]{2,1,0:T(1,128)}), f32[32,1,1152]{2,1,0:T(1,128)S(1)}, u32[]{:S(2)}, u32[]{:S(2)}) %all-to-all-start.1) | async-done | bytes 147488 | tf_op jit(solution)/shard_map/return_terms/all_to_all | solution.py:387
  52.1 0.0 copy-done.3
  52.1 0.0 copy-done.5
  52.1 0.0 copy-done.1
  52.1 2.0 %final.1 = f32[2,4,128,256]{3,2,1,0:T(8,128)} custom-call(f32[288,128]{1,0:T(8,128)S(1)} %bitcast.16, f32[144,256]{1,0:T(8,128)S(1)} %collective-permute-done.2.shift_ref, f32[8,128]{1,0:T(8,128)S(1)} %get-tuple-element.25.params_ref, f32[96,256]{1,0:T(8,128)S(1)} %collective-permute-done.above_ref, f32[96,256]{1,0:T(8,128)S(1)} %collective-permute-done.1.below_ref, ...), custom_call_target="tpu_custom_call" | custom-call | tf_op jit(solution)/shard_map/final/pallas_call | solution.py:388
  (3 shorter events, 0.1 us)
Async XLA Ops:
  0.0 7.2 %copy-start.9 = (f32[4,128,128]{2,1,0:T(8,128)S(1)}, f32[4,128,128]{2,1,0:T(8,128)}, u32[]{:S(2)}) copy-start(f32[4,128,128]{2,1,0:T(8,128)} %param.10) | copy-start | bytes 786436
  1.6 9.3 %collective-permute-start = (f32[96,256]{1,0:T(8,128)S(1)}, f32[96,256]{1,0:T(8,128)S(1)}, u32[]{:S(2)}, u32[]{:S(2)}) collective-permute-start(f32[96,256]{1,0:T(8,128)S(1)} %get-tuple-element.26), channel_id=1, source_target_pairs={{0,1},{1,2},{2,3},{3,4},{4,5},{5,6},{6,7},{8,9},{9,10},{10,11},{11... | collective-permute-start | bytes 294920 | tf_op jit(solution)/shard_map/halo/ppermute | solution.py:331
  3.6 7.3 %collective-permute-start.1 = (f32[96,256]{1,0:T(8,128)S(1)}, f32[96,256]{1,0:T(8,128)S(1)}, u32[]{:S(2)}, u32[]{:S(2)}) collective-permute-start(f32[96,256]{1,0:T(8,128)S(1)} %get-tuple-element.27), channel_id=1, source_target_pairs={{1,0},{2,1},{3,2},{4,3},{5,4},{6,5},{7,6},{9,8},{10,9},{11,10},{12... | collective-permute-start | bytes 294920 | tf_op jit(solution)/shard_map/halo/ppermute | solution.py:332
  7.5 0.7 %copy-start.6 = (f32[4,128]{1,0:T(4,128)S(1)}, f32[4,128]{1,0:T(4,128)}, u32[]{:S(2)}) copy-start(f32[4,128]{1,0:T(4,128)} %rates_ref.3) | copy-start | bytes 6148
  10.9 2.1 %copy-start = (f32[2,128,256]{2,1,0:T(8,128)}, f32[2,128,256]{2,1,0:T(8,128)S(1)}, u32[]{:S(2)}) copy-start(f32[2,128,256]{2,1,0:T(8,128)S(1)} %get-tuple-element.35.last_ref) | copy-start | bytes 786436
  13.0 0.7 %copy-start.7 = (f32[144,256]{1,0:T(8,128)}, f32[144,256]{1,0:T(8,128)S(1)}, u32[]{:S(2)}) copy-start(f32[144,256]{1,0:T(8,128)S(1)} %get-tuple-element.33) | copy-start | bytes 442372
  13.6 22.3 %copy-start.2 = (f32[2,64,256]{2,1,0:T(8,128)}, f32[2,64,256]{2,1,0:T(8,128)S(1)}, u32[]{:S(2)}) copy-start(f32[2,64,256]{2,1,0:T(8,128)S(1)} %get-tuple-element.38.edge_base_ref) | copy-start | bytes 393220
  13.6 22.3 %copy-start.4 = (f32[2,64,256]{2,1,0:T(8,128)}, f32[2,64,256]{2,1,0:T(8,128)S(1)}, u32[]{:S(2)}) copy-start(f32[2,64,256]{2,1,0:T(8,128)S(1)} %get-tuple-element.39.edge_last_ref) | copy-start | bytes 393220
  35.9 4.8 %copy-start.8 = (f32[144,256]{1,0:T(8,128)S(1)}, f32[144,256]{1,0:T(8,128)}, u32[]{:S(2)}) copy-start(f32[144,256]{1,0:T(8,128)} %copy-done.7) | copy-start | bytes 442372
  35.9 16.2 %copy-start.3 = (f32[2,64,256]{2,1,0:T(8,128)S(1)}, f32[2,64,256]{2,1,0:T(8,128)}, u32[]{:S(2)}) copy-start(f32[2,64,256]{2,1,0:T(8,128)} %copy-done.2) | copy-start | bytes 393220
  35.9 16.2 %copy-start.5 = (f32[2,64,256]{2,1,0:T(8,128)S(1)}, f32[2,64,256]{2,1,0:T(8,128)}, u32[]{:S(2)}) copy-start(f32[2,64,256]{2,1,0:T(8,128)} %copy-done.4) | copy-start | bytes 393220
  36.7 15.5 %copy-start.1 = (f32[2,128,256]{2,1,0:T(8,128)S(1)}, f32[2,128,256]{2,1,0:T(8,128)}, u32[]{:S(2)}) copy-start(f32[2,128,256]{2,1,0:T(8,128)} %copy-done) | copy-start | bytes 786436
  36.7 15.5 %all-to-all-start.1 = ((f32[32,1,1152]{2,1,0:T(1,128)}), f32[32,1,1152]{2,1,0:T(1,128)S(1)}, u32[]{:S(2)}, u32[]{:S(2)}) async-start(f32[32,1,1152]{2,1,0:T(1,128)} %scan.1), calls=%async_computation.1 | async-start | bytes 294912 | tf_op jit(solution)/shard_map/return_terms/all_to_all | solution.py:387
  40.7 6.6 %collective-permute-start.2 = (f32[144,256]{1,0:T(8,128)S(1)}, f32[144,256]{1,0:T(8,128)S(1)}, u32[]{:S(2)}, u32[]{:S(2)}) collective-permute-start(f32[144,256]{1,0:T(8,128)S(1)} %copy-done.8), channel_id=1, source_target_pairs={{0,8},{8,16},{16,24},{24,32},{32,40},{40,48},{48,56},{56,64},{64,7... | collective-permute-start | bytes 442376 | tf_op jit(solution)/shard_map/onward/ppermute | solution.py:375

commit v5 on v4

--- a/solution.py
+++ b/solution.py
@@ -106,8 +106,9 @@
 
 
 def pack_kernel(
-    starts_hbm, sources_hbm, coupling_hbm, classes_hbm, up_ref, down_ref, params_ref, starts_ref, sources_ref,
-    starts_low, starts_high, sources_low, sources_high, coupling_row, classes_rows, sems,
+    starts_hbm, sources_hbm, coupling_hbm, classes_hbm, rates_hbm,
+    up_ref, down_ref, params_ref, rates_ref, starts_ref, starts_low, starts_high, sources_low, sources_high,
+    coupling_row, classes_rows, sems,
 ):
     lines = starts_hbm.shape[1]
     low, high = pl.ds(0, SLAB), pl.ds(lines - SLAB, SLAB)
@@ -119,7 +120,7 @@
         (coupling_hbm, coupling_row),
         (classes_hbm, classes_rows),
         (starts_hbm, starts_ref),
-        (sources_hbm, sources_ref),
+        (rates_hbm, rates_ref),
     ]
     whole = 2
     copies = [pltpu.make_async_copy(src, dst, sems.at[i]) for i, (src, dst) in enumerate(pairs)]
@@ -148,19 +149,36 @@
 
 
 def own_kernel(
-    first_ref, starts_ref, sources_ref, params_ref, weights_ref, rates_ref,
-    term_ref, shift_ref, decay_ref, base_ref, last_ref, relaxed_ref,
+    first_ref, sources_hbm, starts_ref, params_ref, weights_ref, rates_ref,
+    term_ref, shift_ref, decay_ref, base_ref, last_ref, lines_ref, relaxed_hbm,
+    sources_ref, relaxed_ref, in_sems, out_sems,
 ):
-    coupling = columns(params_ref[0:1, :])
+    arriving = [
+        pltpu.make_async_copy(sources_hbm.at[:, m], sources_ref.at[:, m], in_sems.at[m]) for m in range(STEPS)
+    ]
+    for copy in arriving:
+        copy.start()
+    coupling, *categories = [columns(params_ref[row : row + 1, :]) for row in range(3)]
+    for row, values in enumerate([coupling, *categories]):
+        lines_ref[row] = values
     coupling = jnp.concatenate([coupling, coupling], axis=1)
-    categories = [columns(params_ref[1 + block : 2 + block, :]) for block in range(2)]
+
+    leaving = []
+
+    def sources(g, m):
+        if g == 0:
+            arriving[m].wait()
+        return sources_ref[g, m]
 
     def relaxed_to(g, m, field):
         relaxed_ref[g, m] = field
+        if g == GROUPS - 1:
+            leaving.append(pltpu.make_async_copy(relaxed_ref.at[:, m], relaxed_hbm.at[:, m], out_sems.at[m]))
+            leaving[-1].start()
 
     out = relaxations(
-        [starts_ref[g] for g in range(GROUPS)], lambda g, m: sources_ref[g, m], coupling, categories, weights_ref[...],
-        rates_ref, first_ref[0, 0], relaxed_to,
+        [starts_ref[g] for g in range(GROUPS)], sources, coupling, categories, weights_ref[...], rates_ref,
+        first_ref[0, 0], relaxed_to,
     )
     term_ref[...] = out["term"]
     shift_ref[...] = out["shift"]
@@ -168,19 +186,25 @@
     for g in range(GROUPS):
         base_ref[g] = out["bases"][g]
         last_ref[g] = out["lasts"][g]
-
-
-def joined(inner, strip, beyond):
-    lines = inner.shape[0]
-    return jnp.concatenate([strip[16 - beyond : 24], inner[EDGE : lines - EDGE], strip[40 : 48 + beyond]], axis=0)
+    for copy in leaving:
+        copy.wait()
+
+
+def ends_of(strip, beyond):
+    return jnp.concatenate([strip[16 - beyond : 24], strip[40 : 48 + beyond]], axis=0)
+
+
+def joined(inner, ends):
+    lines, half = inner.shape[0], ends.shape[0] // 2
+    return jnp.concatenate([ends[:half], inner[EDGE : lines - EDGE], ends[half:]], axis=0)
 
 
 def edge_kernel(
-    first_ref, starts_ref, sources_ref, params_ref, above_ref, below_ref, weights_ref, rates_ref,
-    own_term_ref, own_shift_ref, own_decay_ref,
-    terms_ref, factors_ref, shift_ref, decay_ref, base_ref, last_ref, relaxed_ref, halo_ref,
+    first_ref, starts_low, starts_high, sources_low, sources_high, params_ref, above_ref, below_ref, weights_ref,
+    rates_ref, own_term_ref, own_shift_ref, own_decay_ref,
+    terms_ref, factors_ref, shift_ref, decay_ref, base_ref, last_ref, lines_ref, relaxed_ref, halo_ref,
 ):
-    lines = starts_ref.shape[1]
+    lines = params_ref.shape[1]
     lane = lax.broadcasted_iota(jnp.int32, (8, LB), 1)
     at = GROUPS * GROUP_ROWS
     own = params_ref[...]
@@ -192,9 +216,10 @@
     lower = jnp.where(lane < 3 * SLAB, pltpu.roll(own, 3 * SLAB, 1), pltpu.roll(below, 3 * SLAB, 1))
     strip = jnp.where(lane < 2 * SLAB, upper, lower)
     rows = 4 * SLAB
-    coupling = columns(strip[0:1])[:rows]
+    coupling, *categories = [columns(strip[row : row + 1])[:rows] for row in range(3)]
+    for row, values in enumerate([coupling, *categories]):
+        lines_ref[row] = ends_of(values, EDGE)
     coupling = jnp.concatenate([coupling, coupling], axis=1)
-    categories = [columns(strip[1 + block : 2 + block])[:rows] for block in range(2)]
 
     halo_ref[0, 0:16, :] = jnp.zeros((16, 2 * LB), jnp.float32)
     for g in range(GROUPS):
@@ -208,35 +233,33 @@
     def strips(slab, low, high):
         return jnp.concatenate([halo_ref[slab, :SLAB, :], low, high, halo_ref[slab, SLAB:, :]], axis=0)
 
-    starts = [
-        strips(g * len(REACH), starts_ref[g, :SLAB, :], starts_ref[g, lines - SLAB :, :]) for g in range(GROUPS)
-    ]
+    starts = [strips(g * len(REACH), starts_low[g], starts_high[g]) for g in range(GROUPS)]
 
     def sources(g, m):
-        return strips(
-            g * len(REACH) + 1 + m, sources_ref[g, m, :SLAB, :], sources_ref[g, m, lines - SLAB :, :]
-        )
+        return strips(g * len(REACH) + 1 + m, sources_low[g, m], sources_high[g, m])
 
     def relaxed_to(g, m, field):
-        relaxed_ref[g, m] = field
+        relaxed_ref[g, m] = ends_of(field, 0)
 
     out = relaxations(starts, sources, coupling, categories, weights_ref[...], rates_ref, first_ref[0, 0], relaxed_to)
     section = lines + 2 * EDGE
-    decay = joined(own_decay_ref[...], out["decay"], EDGE)
-    term = joined(own_term_ref[...], out["term"], EDGE)
+    end_decay = ends_of(out["decay"], EDGE)
+    decay = joined(own_decay_ref[...], end_decay)
+    term = joined(own_term_ref[...], ends_of(out["term"], EDGE))
     for block in range(2):
         at = block * section
         lanes = slice(block * LB, (block + 1) * LB)
         terms_ref[at : at + section, :] = term[:, lanes]
         factors_ref[at : at + section, :] = (decay * decay)[:, lanes]
-    shift_ref[...] = joined(own_shift_ref[...], out["shift"], EDGE)
-    decay_ref[...] = out["decay"]
+    shift_ref[...] = joined(own_shift_ref[...], ends_of(out["shift"], EDGE))
+    decay_ref[...] = end_decay
     for g in range(GROUPS):
-        base_ref[g] = out["bases"][g]
-        last_ref[g] = out["lasts"][g]
-
-
-def scan_kernel(place_ref, terms_ref, factors_ref, entering_ref):
+        base_ref[g] = ends_of(out["bases"][g], EDGE)
+        last_ref[g] = ends_of(out["lasts"][g], 0)
+
+
+def scan_kernel(place_ref, terms_ref, factors_ref, shift_ref, entering_ref):
+    del shift_ref
     factor = factors_ref[place_ref[0, 0]]
     carried = jnp.zeros_like(factor)
     for d in range(terms_ref.shape[0]):
@@ -245,29 +268,24 @@
 
 
 def final_kernel(
-    entering_ref, shift_ref, params_ref, above_ref, below_ref, weights_ref, decay_ref, base_ref, last_ref, relaxed_ref,
-    edge_decay_ref, edge_base_ref, edge_last_ref, edge_relaxed_ref, states_hbm, states_ref, sems,
+    entering_ref, shift_ref, weights_ref, decay_ref, base_ref, last_ref, lines_ref, relaxed_hbm,
+    edge_decay_ref, edge_base_ref, edge_last_ref, edge_lines_ref, edge_relaxed_ref,
+    states_hbm, states_ref, relaxed_ref, sems, in_sem,
 ):
     lines = last_ref.shape[1]
     section = lines + 2 * EDGE
-    at = GROUPS * GROUP_ROWS
-
-    def along(row):
-        own = columns(params_ref[row : row + 1, :])
-        above = columns(above_ref[at + row : at + row + 1, :LB])
-        below = columns(below_ref[at + row : at + row + 1, :LB])
-        return jnp.concatenate([above[lines - EDGE :], own, below[:EDGE]], axis=0)
-
-    coupling = along(0)
+    arriving = pltpu.make_async_copy(relaxed_hbm, relaxed_ref, in_sem)
+    arriving.start()
+    coupling, *categories = [joined(lines_ref[row], edge_lines_ref[row]) for row in range(3)]
     coupling = jnp.concatenate([coupling, coupling], axis=1)
-    masks = class_masks([along(1), along(2)])
+    masks = class_masks(categories)
 
     entering = jnp.concatenate([entering_ref[:section, :], entering_ref[section:, :]], axis=1)
     shift = shift_ref[...]
     inner = slice(EDGE, EDGE + lines)
-    decay = joined(decay_ref[...], edge_decay_ref[...], EDGE)
-    base = [joined(base_ref[g], edge_base_ref[g], EDGE) for g in range(GROUPS)]
-    last = [joined(last_ref[g], edge_last_ref[g], 0) for g in range(GROUPS)]
+    decay = joined(decay_ref[...], edge_decay_ref[...])
+    base = [joined(base_ref[g], edge_base_ref[g]) for g in range(GROUPS)]
+    last = [joined(last_ref[g], edge_last_ref[g]) for g in range(GROUPS)]
     passed = decay * entering
 
     def send(m):
@@ -282,8 +300,10 @@
     weights = weights_ref[...]
     for m in range(STEPS - 1):
         state = solve_lines([spread(s, coupling) for s in state], masks, weights)
+        if m == 0:
+            arriving.wait()
         for g in range(GROUPS):
-            states_ref[g, m] = joined(relaxed_ref[g, m], edge_relaxed_ref[g, m], 0) + state[g][inner]
+            states_ref[g, m] = joined(relaxed_ref[g, m], edge_relaxed_ref[g, m]) + state[g][inner]
         copies.append(send(m))
     for copy in copies:
         copy.wait()
@@ -301,20 +321,29 @@
     def grant(size):
         return pltpu.CompilerParams(vmem_limit_bytes=size * MEBI)
 
+    def in_hbm(x):
+        return pltpu.with_memory_space_constraint(x, pltpu.HBM)
+
     def shape(*dims):
         return jax.ShapeDtypeStruct(dims, f32)
 
     message = shape(MESSAGE_ROWS, line_len)
-    up, down, params, held_starts, held_sources = pl.pallas_call(
+    up, down, params, rates, held_starts, *slabs = pl.pallas_call(
         pack_kernel,
-        out_shape=(message, message, shape(8, lines), shape(*starts.shape), shape(*sources.shape)),
-        in_specs=[HBM] * 4,
-        out_specs=[VMEM] * 5,
+        out_shape=(
+            message,
+            message,
+            shape(8, lines),
+            shape(*coarse_rate.shape),
+            shape(*starts.shape),
+            shape(GROUPS, SLAB, line_len),
+            shape(GROUPS, SLAB, line_len),
+            shape(GROUPS, STEPS, SLAB, line_len),
+            shape(GROUPS, STEPS, SLAB, line_len),
+        ),
+        in_specs=[HBM] * 5,
+        out_specs=[VMEM] * 9,
         scratch_shapes=[
-            pltpu.VMEM((GROUPS, SLAB, line_len), f32),
-            pltpu.VMEM((GROUPS, SLAB, line_len), f32),
-            pltpu.VMEM((GROUPS, STEPS, SLAB, line_len), f32),
-            pltpu.VMEM((GROUPS, STEPS, SLAB, line_len), f32),
             pltpu.VMEM((1, lines), f32),
             pltpu.VMEM((2, lines), jnp.int32),
             pltpu.SemaphoreType.DMA((8,)),
@@ -322,8 +351,8 @@
         compiler_params=grant(6),
         name="pack",
     )(*[
-        pltpu.with_memory_space_constraint(x, pltpu.HBM)
-        for x in (starts, sources, coupling.reshape(1, lines), classes.T)
+        in_hbm(x)
+        for x in (starts, sources, coupling.reshape(1, lines), classes.T, coarse_rate)
     ])
 
     with jax.named_scope("halo"):
@@ -343,32 +372,50 @@
         high = lax.reduce_precision(table, 8, 7)
         weights = jnp.concatenate([high, high, table - high], axis=0).astype(jnp.bfloat16)
 
-    def kept(rows):
+    def kept(rows, wide_rows):
         return (
-            shape(rows, line_len),
+            shape(wide_rows, line_len),
+            shape(GROUPS, wide_rows, line_len),
             shape(GROUPS, rows, line_len),
-            shape(GROUPS, rows, line_len),
+            shape(3, wide_rows, LB),
             shape(GROUPS, STEPS - 1, rows, line_len),
         )
 
+    held = pltpu.VMEM((GROUPS, STEPS - 1, lines, line_len), f32)
     term, shift, *own = pl.pallas_call(
         own_kernel,
-        out_shape=(shape(lines, line_len), shape(lines, line_len), *kept(lines)),
-        in_specs=[SMEM] + [VMEM] * 5,
-        out_specs=[VMEM] * 6,
+        out_shape=(
+            shape(lines, line_len),
+            shape(lines, line_len),
+            *kept(lines, lines)[:-1],
+            pltpu.HBM((GROUPS, STEPS - 1, lines, line_len), f32),
+        ),
+        in_specs=[SMEM, HBM] + [VMEM] * 4,
+        out_specs=[VMEM] * 6 + [HBM],
+        scratch_shapes=[
+            pltpu.VMEM((GROUPS, STEPS, lines, line_len), f32),
+            held,
+            pltpu.SemaphoreType.DMA((STEPS,)),
+            pltpu.SemaphoreType.DMA((STEPS - 1,)),
+        ],
         compiler_params=grant(24),
         cost_estimate=pl.CostEstimate(flops=5_000_000_000, bytes_accessed=4_000_000, transcendentals=0),
         name="own",
-    )(first, held_starts, held_sources, params, weights, coarse_rate)
+    )(first, in_hbm(sources), held_starts, params, weights, rates)
     terms, factors, shift, *edges = pl.pallas_call(
         edge_kernel,
-        out_shape=(shape(sections, LB), shape(sections, LB), shape(near_rows, line_len), *kept(4 * SLAB)),
-        in_specs=[SMEM] + [VMEM] * 10,
-        out_specs=[VMEM] * 7,
+        out_shape=(
+            shape(sections, LB),
+            shape(sections, LB),
+            shape(near_rows, line_len),
+            *kept(2 * EDGE, 4 * EDGE),
+        ),
+        in_specs=[SMEM] + [VMEM] * 12,
+        out_specs=[VMEM] * 8,
         scratch_shapes=[pltpu.VMEM((GROUPS * len(REACH), 2 * SLAB, line_len), f32)],
         compiler_params=grant(20),
         name="edge",
-    )(first, held_starts, held_sources, params, above, below, weights, coarse_rate, term, shift, own[0])
+    )(first, *slabs, params, above, below, weights, rates, term, shift, own[0])
 
     split = (count, 1, sections * LB // count)
     with jax.named_scope("onward"):
@@ -377,26 +424,28 @@
         terms = lax.all_to_all(terms.reshape(split), "tm", 0, 0)
     entering = pl.pallas_call(
         scan_kernel,
-        out_shape=pltpu.VMEM(split, f32),
-        in_specs=[SMEM] + [VMEM] * 2,
+        out_shape=shape(*split),
+        in_specs=[SMEM] + [VMEM] * 3,
         out_specs=VMEM,
         compiler_params=grant(4),
         name="scan",
-    )(place, terms, factors.reshape(split))
+    )(place, terms, factors.reshape(split), shift)
     with jax.named_scope("return_terms"):
         entering = lax.all_to_all(entering, "tm", 0, 0)
     return pl.pallas_call(
         final_kernel,
         out_shape=shape(GROUPS, STEPS, lines, line_len),
-        in_specs=[VMEM] * 14,
+        in_specs=[VMEM] * 7 + [HBM] + [VMEM] * 5,
         out_specs=HBM,
         scratch_shapes=[
             pltpu.VMEM((GROUPS, STEPS, lines, line_len), f32),
+            held,
             pltpu.SemaphoreType.DMA((STEPS,)),
+            pltpu.SemaphoreType.DMA,
         ],
         compiler_params=grant(20),
         name="final",
-    )(entering.reshape(sections, LB), shift, params, above, below, weights, *own, *edges)
+    )(entering.reshape(sections, LB), shift, weights, *own[:-1], in_hbm(own[-1]), *edges)
 
 
 def solution(mesh):

time: 54.5 us -> 57.3 us (1.051)
  starting transfers between devices: 13.1 us -> 20.6 us
  blocking collectives: 22.3 us -> 16.8 us
  Pallas kernels: 9.12 us -> 11.5 us
  local copies, waits for them, and re-layouts: 1.5 us -> 0.15 us
    all_to_all x1, starting transfers between devices: 3.99 us -> 11.3 us  [shards(): terms = lax.all_to_all(terms.reshape(split), 'tm', 0, 0)]
    all_to_all x1, blocking collectives: 22.3 us -> 16.8 us  [shards(): entering = lax.all_to_all(entering, 'tm', 0, 0)]
    pallas_call x1, Pallas kernels: 2.72 us -> 4.49 us  [shards(): pl.pallas_call(own_kernel, out_shape=(shape(lines, line_len), shape(lines...]
    unnamed x21 -> x3, local copies, waits for them, and re-layouts: 1.48 us -> 0.13 us
    pallas_call x1, Pallas kernels: 2.01 us -> 2.93 us  [shards(): pl.pallas_call(final_kernel, out_shape=shape(GROUPS, STEPS, lines, line_l...]
    pallas_call x1, Pallas kernels: 2.03 us -> 2.71 us  [shards(): pl.pallas_call(edge_kernel, out_shape=(shape(sections, LB), shape(section...]
    pallas_call x1, Pallas kernels: 0.74 us -> 0.07 us  [shards(): pl.pallas_call(scan_kernel, out_shape=shape(*split), in_specs=[SMEM] + [V...]
    all_to_all x1, waiting for transfers between devices: 4.86 us -> 4.2 us  [shards(): terms = lax.all_to_all(terms.reshape(split), 'tm', 0, 0)]
  transfers between devices with their start and end apart: 4 -> 4, of which waited for: 2 -> 2; matrix products, arithmetic and copies ran while one was open for 0% -> 0% of each run, Pallas kernels for 5% -> 8%
where the time goes in v5:
time: 57.3 us; the launch traced here: 57 us
  starting transfers between devices  20.6 us (36%)
  blocking collectives  16.8 us (29%)
  Pallas kernels  11.5 us (20%)
  waiting for transfers between devices  7.79 us (14%)
    all_to_all x1, blocking collectives, shards(): entering = lax.all_to_all(entering, 'tm', 0, 0)  16.8 us
    all_to_all x1, starting transfers between devices, shards(): terms = lax.all_to_all(terms.reshape(split), 'tm', 0, 0)  11.3 us
    pallas_call x1, Pallas kernels, shards(): pl.pallas_call(own_kernel, out_shape=(shape(lines, line_len), shape(lines...  4.49 us
    all_to_all x1, waiting for transfers between devices, shards(): terms = lax.all_to_all(terms.reshape(split), 'tm', 0, 0)  4.2 us
    ppermute x1, starting transfers between devices, shards(): shift = lax.ppermute(shift, 'tm', [(i, i + 1) for i in range(count - 1)])  3.7 us
    ppermute x1, starting transfers between devices, shards(): below = lax.ppermute(down, 'space', [(j, i) for i, j in upward])  3.64 us
    ppermute x1, waiting for transfers between devices, shards(): shift = lax.ppermute(shift, 'tm', [(i, i + 1) for i in range(count - 1)])  3.59 us
    pallas_call x1, Pallas kernels, shards(): pl.pallas_call(final_kernel, out_shape=shape(GROUPS, STEPS, lines, line_l...  2.93 us
  transfers between devices with their start and end apart: 4, of which 2 were waited for; matrix products, arithmetic and copies ran while one was open for 0% of the time, Pallas kernels for 8%

profile of v5, /device:TPU:8, one launch (start us, length us, event | category | flops | bytes accessed | tf_op | source)
XLA Modules:
  0.0 57.0 jit_solution(14675002083139042975)
XLA Ops:
  0.0 0.0 copy-start
  0.0 1.3 %pack.1 = (f32[96,256]{1,0:T(8,128)S(1)}, f32[96,256]{1,0:T(8,128)S(1)}, f32[8,128]{1,0:T(8,128)S(1)}, f32[4,128]{1,0:T(4,128)S(1)}, f32[2,128,256]{2,1,0:T(8,12...) custom-call(f32[2,128,256]{2,1,0:T(8,128)} %starts_hbm.1, ...), custom_call_target="tpu_custom_call" | custom-call | tf_op jit(solution)/shard_map/pack/pallas_call | solution.py:331
  1.3 1.9 %collective-permute-start = (f32[96,256]{1,0:T(8,128)S(1)}, f32[96,256]{1,0:T(8,128)S(1)}, u32[]{:S(2)}, u32[]{:S(2)}) collective-permute-start(f32[96,256]{1,0:T(8,128)S(1)} %get-tuple-element.34), channel_id=1, source_target_pairs={{0,1},{1,2},{2,3},{3,4},{4,5},{5,6},{6,7},{8,9},{9,10},{10,11},{11... | collective-permute-start | bytes 294920 | tf_op jit(solution)/shard_map/halo/ppermute | solution.py:360
  3.2 3.6 %collective-permute-start.1 = (f32[96,256]{1,0:T(8,128)S(1)}, f32[96,256]{1,0:T(8,128)S(1)}, u32[]{:S(2)}, u32[]{:S(2)}) collective-permute-start(f32[96,256]{1,0:T(8,128)S(1)} %get-tuple-element.35), channel_id=1, source_target_pairs={{1,0},{2,1},{3,2},{4,3},{5,4},{6,5},{7,6},{9,8},{10,9},{11,10},{12... | collective-permute-start | bytes 294920 | tf_op jit(solution)/shard_map/halo/ppermute | solution.py:361
  6.9 0.0 copy-done
  6.9 0.1 copy.7
  7.1 4.5 %own.1 = (f32[128,256]{1,0:T(8,128)S(1)}, f32[128,256]{1,0:T(8,128)S(1)}, f32[128,256]{1,0:T(8,128)S(1)}, f32[2,128,256]{2,1,0:T(8,128)S(1)}, f32[2,128,256]{2,1...) custom-call(s32[1,1]{1,0:T(1,128)} %bitcast.1.first_ref, f32[2,4,128,256]{3,2,1,0:T(8,128)} %sources_hbm.3, ...), custom_call_target="tpu_custom_call" | custom-call | flops 5000000000 | bytes 4000000 | tf_op jit(solution)/shard_map/own/pallas_call | solution.py:385
  11.6 0.0 collective-permute-done.above_ref
  11.6 0.0 collective-permute-done.1.below_ref
  11.6 2.7 %edge.1 = (f32[288,128]{1,0:T(8,128)}, f32[288,128]{1,0:T(8,128)S(1)}, f32[144,256]{1,0:T(8,128)S(1)}, f32[32,256]{1,0:T(8,128)S(1)}, f32[2,32,256]{2,1,0:T(8,12...) custom-call(s32[1,1]{1,0:T(1,128)} %bitcast.1.first_ref, ...), custom_call_target="tpu_custom_call" | custom-call | tf_op jit(solution)/shard_map/edge/pallas_call | solution.py:405
  14.3 11.3 %all-to-all-start = ((f32[32,1,1152]{2,1,0:T(1,128)}), f32[32,1,1152]{2,1,0:T(1,128)S(1)}, u32[]{:S(2)}, u32[]{:S(2)}) async-start(f32[32,1,1152]{2,1,0:T(1,128)} %bitcast.9), calls=%async_computation | async-start | bytes 294912 | tf_op jit(solution)/shard_map/gather_terms/all_to_all | solution.py:424
  25.7 3.7 %collective-permute-start.2 = (f32[144,256]{1,0:T(8,128)S(1)}, f32[144,256]{1,0:T(8,128)S(1)}, u32[]{:S(2)}, u32[]{:S(2)}) collective-permute-start(f32[144,256]{1,0:T(8,128)S(1)} %get-tuple-element.43), channel_id=1, source_target_pairs={{0,8},{8,16},{16,24},{24,32},{32,40},{40,48},{48,56},{56,64},{64,7... | collective-permute-start | bytes 442376 | tf_op jit(solution)/shard_map/onward/ppermute | solution.py:422
  29.4 3.6 %collective-permute-done.2.shift_ref = f32[144,256]{1,0:T(8,128)S(1)} collective-permute-done((f32[144,256]{1,0:T(8,128)S(1)}, f32[144,256]{1,0:T(8,128)S(1)}, u32[]{:S(2)}, u32[]{:S(2)}) %collective-permute-start.2) | collective-permute-done | bytes 147488 | tf_op jit(solution)/shard_map/onward/ppermute | solution.py:422
  32.9 4.2 %all-to-all-done.terms_ref = f32[32,1,1152]{2,1,0:T(1,128)S(1)} async-done(((f32[32,1,1152]{2,1,0:T(1,128)}), f32[32,1,1152]{2,1,0:T(1,128)S(1)}, u32[]{:S(2)}, u32[]{:S(2)}) %all-to-all-start) | async-done | bytes 147488 | tf_op jit(solution)/shard_map/gather_terms/all_to_all | solution.py:424
  37.1 0.1 scan.1
  37.2 16.8 %all_to_all.10 = f32[32,1,1152]{2,1,0:T(1,128)S(1)} all-to-all(f32[32,1,1152]{2,1,0:T(1,128)S(1)} %scan.1), channel_id=1, replica_groups=mesh['tm'=32,'space'=8] {'tm'}, dimensions={0} | all-to-all | bytes 294912 | tf_op jit(solution)/shard_map/return_terms/all_to_all | solution.py:434
  54.1 2.9 %final.1 = f32[2,4,128,256]{3,2,1,0:T(8,128)} custom-call(f32[288,128]{1,0:T(8,128)S(1)} %bitcast.16, f32[144,256]{1,0:T(8,128)S(1)} %collective-permute-done.2.shift_ref, bf16[768,256]{1,0:T(8,128)(2,1)S(1)} %pad_maximum_fusion.weights_ref, f32[128,256]{1,0:T(8,128)S(1)} %get-tuple-element.40.own_decay_ref.decay_ref, ...), custom_call_target="tpu_custom_call" | custom-call | tf_op jit(solution)/shard_map/final/pallas_call | solution.py:435
  (3 shorter events, 0.1 us)
Async XLA Ops:
  0.0 6.9 %copy-start = (f32[4,128,128]{2,1,0:T(8,128)S(1)}, f32[4,128,128]{2,1,0:T(8,128)}, u32[]{:S(2)}) copy-start(f32[4,128,128]{2,1,0:T(8,128)} %param.10) | copy-start | bytes 786436
  1.3 10.3 %collective-permute-start = (f32[96,256]{1,0:T(8,128)S(1)}, f32[96,256]{1,0:T(8,128)S(1)}, u32[]{:S(2)}, u32[]{:S(2)}) collective-permute-start(f32[96,256]{1,0:T(8,128)S(1)} %get-tuple-element.34), channel_id=1, source_target_pairs={{0,1},{1,2},{2,3},{3,4},{4,5},{5,6},{6,7},{8,9},{9,10},{10,11},{11... | collective-permute-start | bytes 294920 | tf_op jit(solution)/shard_map/halo/ppermute | solution.py:360
  3.2 8.4 %collective-permute-start.1 = (f32[96,256]{1,0:T(8,128)S(1)}, f32[96,256]{1,0:T(8,128)S(1)}, u32[]{:S(2)}, u32[]{:S(2)}) collective-permute-start(f32[96,256]{1,0:T(8,128)S(1)} %get-tuple-element.35), channel_id=1, source_target_pairs={{1,0},{2,1},{3,2},{4,3},{5,4},{6,5},{7,6},{9,8},{10,9},{11,10},{12... | collective-permute-start | bytes 294920 | tf_op jit(solution)/shard_map/halo/ppermute | solution.py:361
  14.3 22.8 %all-to-all-start = ((f32[32,1,1152]{2,1,0:T(1,128)}), f32[32,1,1152]{2,1,0:T(1,128)S(1)}, u32[]{:S(2)}, u32[]{:S(2)}) async-start(f32[32,1,1152]{2,1,0:T(1,128)} %bitcast.9), calls=%async_computation | async-start | bytes 294912 | tf_op jit(solution)/shard_map/gather_terms/all_to_all | solution.py:424
  25.7 7.3 %collective-permute-start.2 = (f32[144,256]{1,0:T(8,128)S(1)}, f32[144,256]{1,0:T(8,128)S(1)}, u32[]{:S(2)}, u32[]{:S(2)}) collective-permute-start(f32[144,256]{1,0:T(8,128)S(1)} %get-tuple-element.43), channel_id=1, source_target_pairs={{0,8},{8,16},{16,24},{24,32},{32,40},{40,48},{48,56},{56,64},{64,7... | collective-permute-start | bytes 442376 | tf_op jit(solution)/shard_map/onward/ppermute | solution.py:422

commit v6 on v4

--- a/solution.py
+++ b/solution.py
@@ -57,6 +57,7 @@
         high_pair = [high * even[block], high * odd[block]]
         low_pair = [low * even[block], low * odd[block]]
         left.append(jnp.concatenate(high_pair + low_pair + high_pair, axis=1))
+    weights = jnp.concatenate([weights[: 2 * LB], weights], axis=0)
     product = jnp.dot(jnp.concatenate(left, axis=0), weights, preferred_element_type=jnp.float32)
     blocks = []
     for block in range(2):
@@ -101,12 +102,13 @@
         shift=ends[1] - ahead,
         decay=decay,
         bases=(jnp.where(first > 0, jnp.zeros_like(linear), starts[0]), change - linear),
-        lasts=(ends[0] - linear, ends[1] + resid - held),
+        last=ends[1] + resid - held,
     )
 
 
 def pack_kernel(
-    starts_hbm, sources_hbm, coupling_hbm, classes_hbm, up_ref, down_ref, params_ref, starts_ref, sources_ref,
+    starts_hbm, sources_hbm, coupling_hbm, classes_hbm, rates_hbm,
+    up_ref, down_ref, params_ref, starts_ref, sources_ref, rates_ref,
     starts_low, starts_high, sources_low, sources_high, coupling_row, classes_rows, sems,
 ):
     lines = starts_hbm.shape[1]
@@ -120,8 +122,9 @@
         (classes_hbm, classes_rows),
         (starts_hbm, starts_ref),
         (sources_hbm, sources_ref),
+        (rates_hbm, rates_ref),
     ]
-    whole = 2
+    whole = 3
     copies = [pltpu.make_async_copy(src, dst, sems.at[i]) for i, (src, dst) in enumerate(pairs)]
     for copy in copies:
         copy.start()
@@ -151,9 +154,8 @@
     first_ref, starts_ref, sources_ref, params_ref, weights_ref, rates_ref,
     term_ref, shift_ref, decay_ref, base_ref, last_ref, relaxed_ref,
 ):
-    coupling = columns(params_ref[0:1, :])
+    coupling, *categories = [columns(params_ref[row : row + 1, :]) for row in range(3)]
     coupling = jnp.concatenate([coupling, coupling], axis=1)
-    categories = [columns(params_ref[1 + block : 2 + block, :]) for block in range(2)]
 
     def relaxed_to(g, m, field):
         relaxed_ref[g, m] = field
@@ -165,14 +167,17 @@
     term_ref[...] = out["term"]
     shift_ref[...] = out["shift"]
     decay_ref[...] = out["decay"]
-    for g in range(GROUPS):
-        base_ref[g] = out["bases"][g]
-        last_ref[g] = out["lasts"][g]
-
-
-def joined(inner, strip, beyond):
-    lines = inner.shape[0]
-    return jnp.concatenate([strip[16 - beyond : 24], inner[EDGE : lines - EDGE], strip[40 : 48 + beyond]], axis=0)
+    base_ref[...] = out["bases"][1]
+    last_ref[...] = out["last"]
+
+
+def ends_of(strip, beyond):
+    return jnp.concatenate([strip[16 - beyond : 24], strip[40 : 48 + beyond]], axis=0)
+
+
+def joined(inner, ends):
+    lines, half = inner.shape[0], ends.shape[0] // 2
+    return jnp.concatenate([ends[:half], inner[EDGE : lines - EDGE], ends[half:]], axis=0)
 
 
 def edge_kernel(
@@ -192,9 +197,8 @@
     lower = jnp.where(lane < 3 * SLAB, pltpu.roll(own, 3 * SLAB, 1), pltpu.roll(below, 3 * SLAB, 1))
     strip = jnp.where(lane < 2 * SLAB, upper, lower)
     rows = 4 * SLAB
-    coupling = columns(strip[0:1])[:rows]
+    coupling, *categories = [columns(strip[row : row + 1])[:rows] for row in range(3)]
     coupling = jnp.concatenate([coupling, coupling], axis=1)
-    categories = [columns(strip[1 + block : 2 + block])[:rows] for block in range(2)]
 
     halo_ref[0, 0:16, :] = jnp.zeros((16, 2 * LB), jnp.float32)
     for g in range(GROUPS):
@@ -218,22 +222,23 @@
         )
 
     def relaxed_to(g, m, field):
-        relaxed_ref[g, m] = field
+        relaxed_ref[g, m] = ends_of(field, 0)
 
     out = relaxations(starts, sources, coupling, categories, weights_ref[...], rates_ref, first_ref[0, 0], relaxed_to)
     section = lines + 2 * EDGE
-    decay = joined(own_decay_ref[...], out["decay"], EDGE)
-    term = joined(own_term_ref[...], out["term"], EDGE)
+    end_decay = ends_of(out["decay"], EDGE)
+    decay = joined(own_decay_ref[...], end_decay)
+    term = joined(own_term_ref[...], ends_of(out["term"], EDGE))
     for block in range(2):
         at = block * section
         lanes = slice(block * LB, (block + 1) * LB)
         terms_ref[at : at + section, :] = term[:, lanes]
         factors_ref[at : at + section, :] = (decay * decay)[:, lanes]
-    shift_ref[...] = joined(own_shift_ref[...], out["shift"], EDGE)
-    decay_ref[...] = out["decay"]
+    shift_ref[...] = joined(own_shift_ref[...], ends_of(out["shift"], EDGE))
+    decay_ref[...] = end_decay
     for g in range(GROUPS):
-        base_ref[g] = out["bases"][g]
-        last_ref[g] = out["lasts"][g]
+        base_ref[g] = ends_of(out["bases"][g], EDGE)
+    last_ref[...] = ends_of(out["last"], 0)
 
 
 def scan_kernel(place_ref, terms_ref, factors_ref, entering_ref):
@@ -245,10 +250,10 @@
 
 
 def final_kernel(
-    entering_ref, shift_ref, params_ref, above_ref, below_ref, weights_ref, decay_ref, base_ref, last_ref, relaxed_ref,
-    edge_decay_ref, edge_base_ref, edge_last_ref, edge_relaxed_ref, states_hbm, states_ref, sems,
+    first_ref, entering_ref, shift_ref, params_ref, above_ref, below_ref, weights_ref, starts_ref,
+    decay_ref, base_ref, last_ref, relaxed_ref, edge_decay_ref, edge_base_ref, edge_last_ref, edge_relaxed_ref, states_hbm, states_ref, sems,
 ):
-    lines = last_ref.shape[1]
+    lines = last_ref.shape[0]
     section = lines + 2 * EDGE
     at = GROUPS * GROUP_ROWS
 
@@ -258,16 +263,17 @@
         below = columns(below_ref[at + row : at + row + 1, :LB])
         return jnp.concatenate([above[lines - EDGE :], own, below[:EDGE]], axis=0)
 
-    coupling = along(0)
+    coupling, *categories = [along(row) for row in range(3)]
     coupling = jnp.concatenate([coupling, coupling], axis=1)
-    masks = class_masks([along(1), along(2)])
+    masks = class_masks(categories)
 
     entering = jnp.concatenate([entering_ref[:section, :], entering_ref[section:, :]], axis=1)
     shift = shift_ref[...]
     inner = slice(EDGE, EDGE + lines)
-    decay = joined(decay_ref[...], edge_decay_ref[...], EDGE)
-    base = [joined(base_ref[g], edge_base_ref[g], EDGE) for g in range(GROUPS)]
-    last = [joined(last_ref[g], edge_last_ref[g], 0) for g in range(GROUPS)]
+    decay = joined(decay_ref[...], edge_decay_ref[...])
+    start = jnp.where(first_ref[0, 0] > 0, 0.0, 1.0) * starts_ref[0]
+    base = [joined(start, edge_base_ref[0]), joined(base_ref[...], edge_base_ref[1])]
+    last = [base[1][inner] + starts_ref[1], joined(last_ref[...], edge_last_ref[...])]
     passed = decay * entering
 
     def send(m):
@@ -283,7 +289,7 @@
     for m in range(STEPS - 1):
         state = solve_lines([spread(s, coupling) for s in state], masks, weights)
         for g in range(GROUPS):
-            states_ref[g, m] = joined(relaxed_ref[g, m], edge_relaxed_ref[g, m], 0) + state[g][inner]
+            states_ref[g, m] = joined(relaxed_ref[g, m], edge_relaxed_ref[g, m]) + state[g][inner]
         copies.append(send(m))
     for copy in copies:
         copy.wait()
@@ -305,11 +311,11 @@
         return jax.ShapeDtypeStruct(dims, f32)
 
     message = shape(MESSAGE_ROWS, line_len)
-    up, down, params, held_starts, held_sources = pl.pallas_call(
+    up, down, params, held_starts, held_sources, rates = pl.pallas_call(
         pack_kernel,
-        out_shape=(message, message, shape(8, lines), shape(*starts.shape), shape(*sources.shape)),
-        in_specs=[HBM] * 4,
-        out_specs=[VMEM] * 5,
+        out_shape=(message, message, shape(8, lines), *[shape(*x.shape) for x in (starts, sources, coarse_rate)]),
+        in_specs=[HBM] * 5,
+        out_specs=[VMEM] * 6,
         scratch_shapes=[
             pltpu.VMEM((GROUPS, SLAB, line_len), f32),
             pltpu.VMEM((GROUPS, SLAB, line_len), f32),
@@ -317,13 +323,13 @@
             pltpu.VMEM((GROUPS, STEPS, SLAB, line_len), f32),
             pltpu.VMEM((1, lines), f32),
             pltpu.VMEM((2, lines), jnp.int32),
-            pltpu.SemaphoreType.DMA((8,)),
+            pltpu.SemaphoreType.DMA((9,)),
         ],
         compiler_params=grant(6),
         name="pack",
     )(*[
         pltpu.with_memory_space_constraint(x, pltpu.HBM)
-        for x in (starts, sources, coupling.reshape(1, lines), classes.T)
+        for x in (starts, sources, coupling.reshape(1, lines), classes.T, coarse_rate)
     ])
 
     with jax.named_scope("halo"):
@@ -341,34 +347,37 @@
             axis=0,
         )
         high = lax.reduce_precision(table, 8, 7)
-        weights = jnp.concatenate([high, high, table - high], axis=0).astype(jnp.bfloat16)
-
-    def kept(rows):
-        return (
-            shape(rows, line_len),
-            shape(GROUPS, rows, line_len),
-            shape(GROUPS, rows, line_len),
-            shape(GROUPS, STEPS - 1, rows, line_len),
-        )
+        weights = jnp.concatenate([high, table - high], axis=0).astype(jnp.bfloat16)
+
+    def relaxed(rows):
+        return shape(GROUPS, STEPS - 1, rows, line_len)
 
     term, shift, *own = pl.pallas_call(
         own_kernel,
-        out_shape=(shape(lines, line_len), shape(lines, line_len), *kept(lines)),
+        out_shape=(*[shape(lines, line_len)] * 5, relaxed(lines)),
         in_specs=[SMEM] + [VMEM] * 5,
         out_specs=[VMEM] * 6,
         compiler_params=grant(24),
         cost_estimate=pl.CostEstimate(flops=5_000_000_000, bytes_accessed=4_000_000, transcendentals=0),
         name="own",
-    )(first, held_starts, held_sources, params, weights, coarse_rate)
+    )(first, held_starts, held_sources, params, weights, rates)
     terms, factors, shift, *edges = pl.pallas_call(
         edge_kernel,
-        out_shape=(shape(sections, LB), shape(sections, LB), shape(near_rows, line_len), *kept(4 * SLAB)),
+        out_shape=(
+            shape(sections, LB),
+            shape(sections, LB),
+            shape(near_rows, line_len),
+            shape(4 * EDGE, line_len),
+            shape(GROUPS, 4 * EDGE, line_len),
+            shape(2 * EDGE, line_len),
+            relaxed(2 * EDGE),
+        ),
         in_specs=[SMEM] + [VMEM] * 10,
         out_specs=[VMEM] * 7,
         scratch_shapes=[pltpu.VMEM((GROUPS * len(REACH), 2 * SLAB, line_len), f32)],
         compiler_params=grant(20),
         name="edge",
-    )(first, held_starts, held_sources, params, above, below, weights, coarse_rate, term, shift, own[0])
+    )(first, held_starts, held_sources, params, above, below, weights, rates, term, shift, own[0])
 
     split = (count, 1, sections * LB // count)
     with jax.named_scope("onward"):
@@ -377,7 +386,7 @@
         terms = lax.all_to_all(terms.reshape(split), "tm", 0, 0)
     entering = pl.pallas_call(
         scan_kernel,
-        out_shape=pltpu.VMEM(split, f32),
+        out_shape=shape(*split),
         in_specs=[SMEM] + [VMEM] * 2,
         out_specs=VMEM,
         compiler_params=grant(4),
@@ -388,7 +397,7 @@
     return pl.pallas_call(
         final_kernel,
         out_shape=shape(GROUPS, STEPS, lines, line_len),
-        in_specs=[VMEM] * 14,
+        in_specs=[SMEM] + [VMEM] * 15,
         out_specs=HBM,
         scratch_shapes=[
             pltpu.VMEM((GROUPS, STEPS, lines, line_len), f32),
@@ -396,7 +405,7 @@
         ],
         compiler_params=grant(20),
         name="final",
-    )(entering.reshape(sections, LB), shift, params, above, below, weights, *own, *edges)
+    )(first, entering.reshape(sections, LB), shift, params, above, below, weights, held_starts, *own, *edges)
 
 
 def solution(mesh):

time: 54.5 us -> 53.6 us (0.983)
  local copies, waits for them, and re-layouts: 1.5 us -> 0.15 us
  blocking collectives: 22.3 us -> 23.1 us
    unnamed x21 -> x3, local copies, waits for them, and re-layouts: 1.48 us -> 0.13 us
    all_to_all x1, blocking collectives: 22.3 us -> 23.1 us  [shards(): terms = lax.all_to_all(terms.reshape(split), 'tm', 0, 0)]
where the time goes in v6:
time: 53.6 us; the launch traced here: 53.3 us
  blocking collectives  23.1 us (43%)
  starting transfers between devices  13 us (24%)
  Pallas kernels  9.13 us (17%)
  waiting for transfers between devices  7.75 us (14%)
    all_to_all x1, blocking collectives, shards(): terms = lax.all_to_all(terms.reshape(split), 'tm', 0, 0)  23.1 us
    all_to_all x1, waiting for transfers between devices, shards(): entering = lax.all_to_all(entering, 'tm', 0, 0)  4.69 us
    all_to_all x1, starting transfers between devices, shards(): entering = lax.all_to_all(entering, 'tm', 0, 0)  3.86 us
    ppermute x1, starting transfers between devices, shards(): below = lax.ppermute(down, 'space', [(j, i) for i, j in upward])  3.64 us
    ppermute x1, starting transfers between devices, shards(): shift = lax.ppermute(shift, 'tm', [(i, i + 1) for i in range(count - 1)])  3.59 us
    ppermute x1, waiting for transfers between devices, shards(): shift = lax.ppermute(shift, 'tm', [(i, i + 1) for i in range(count - 1)])  3.05 us
    pallas_call x1, Pallas kernels, shards(): pl.pallas_call(own_kernel, out_shape=(*[shape(lines, line_len)] * 5, rela...  2.72 us
    pallas_call x1, Pallas kernels, shards(): pl.pallas_call(edge_kernel, out_shape=(shape(sections, LB), shape(section...  2.04 us
  transfers between devices with their start and end apart: 4, of which 2 were waited for; matrix products, arithmetic and copies ran while one was open for 0% of the time, Pallas kernels for 5%

profile of v6, /device:TPU:8, one launch (start us, length us, event | category | flops | bytes accessed | tf_op | source)
XLA Modules:
  0.0 53.3 jit_solution(9638890348878429262)
XLA Ops:
  0.0 0.0 copy-start
  0.0 1.6 %pack.1 = (f32[96,256]{1,0:T(8,128)S(1)}, f32[96,256]{1,0:T(8,128)S(1)}, f32[8,128]{1,0:T(8,128)S(1)}, f32[2,128,256]{2,1,0:T(8,128)S(1)}, f32[2,4,128,256]{3,2,1,0:T(8,128)S(1)}, /*index=5*/f32[4,128]{1,0:T(4,128)S(1)}) custom-call(f32[2,128,256]{2,1,0:T(8,128)} %starts_hbm.1, f32[2,4,128,256]{3,2,1,0:T(8,128)} %sources_hbm.1, f32[1,128]{1,0:T(1,128)} %bitcast.21, ...), custom_call_target="tpu_custom_call" | custom-call | tf_op jit(solution)/shard_map/pack/pallas_call | solution.py:314
  1.6 1.9 %collective-permute-start = (f32[96,256]{1,0:T(8,128)S(1)}, f32[96,256]{1,0:T(8,128)S(1)}, u32[]{:S(2)}, u32[]{:S(2)}) collective-permute-start(f32[96,256]{1,0:T(8,128)S(1)} %get-tuple-element.27), channel_id=1, source_target_pairs={{0,1},{1,2},{2,3},{3,4},{4,5},{5,6},{6,7},{8,9},{9,10},{10,11},{11... | collective-permute-start | bytes 294920 | tf_op jit(solution)/shard_map/halo/ppermute | solution.py:337
  3.6 3.6 %collective-permute-start.1 = (f32[96,256]{1,0:T(8,128)S(1)}, f32[96,256]{1,0:T(8,128)S(1)}, u32[]{:S(2)}, u32[]{:S(2)}) collective-permute-start(f32[96,256]{1,0:T(8,128)S(1)} %get-tuple-element.28), channel_id=1, source_target_pairs={{1,0},{2,1},{3,2},{4,3},{5,4},{6,5},{7,6},{9,8},{10,9},{11,10},{12... | collective-permute-start | bytes 294920 | tf_op jit(solution)/shard_map/halo/ppermute | solution.py:338
  7.2 0.0 copy-done
  7.2 0.1 copy.7
  7.5 2.7 %own.1 = (f32[128,256]{1,0:T(8,128)S(1)}, f32[128,256]{1,0:T(8,128)S(1)}, f32[128,256]{1,0:T(8,128)S(1)}, f32[128,256]{1,0:T(8,128)S(1)}, f32[128,256]{1,0:T(8,128)S(1)}, /*index=5*/f32[2,3,128,256]{3,2,1,0:T(8,128)S(1)}) custom-call(s32[1,1]{1,0:T(1,128)} %bitcast.first_ref, f32[2,128,256]{2,1,0:T(8,128)S(1)} %get-tuple-element.24.starts_ref, ...), custom_call_target="tpu_custom_call" | custom-call | flops 5000000000 | bytes 4000000 | tf_op jit(solution)/shard_map/own/pallas_call | solution.py:355
  10.2 0.0 collective-permute-done.above_ref
  10.2 0.0 collective-permute-done.1.below_ref
  10.2 2.0 %edge.1 = (f32[288,128]{1,0:T(8,128)S(1)}, f32[288,128]{1,0:T(8,128)S(1)}, f32[144,256]{1,0:T(8,128)S(1)}, f32[32,256]{1,0:T(8,128)S(1)}, f32[2,32,256]{2,1,0:T(...) custom-call(s32[1,1]{1,0:T(1,128)} %bitcast.first_ref, ...), custom_call_target="tpu_custom_call" | custom-call | tf_op jit(solution)/shard_map/edge/pallas_call | solution.py:364
  12.3 23.1 %all_to_all.10.terms_ref = f32[32,1,1152]{2,1,0:T(1,128)S(1)} all-to-all(f32[32,1,1152]{2,1,0:T(1,128)S(1)} %bitcast.17), channel_id=1, replica_groups=mesh['tm'=32,'space'=8] {'tm'}, dimensions={0} | all-to-all | bytes 294912 | tf_op jit(solution)/shard_map/gather_terms/all_to_all | solution.py:386
  35.3 0.7 %scan.1 = f32[32,1,1152]{2,1,0:T(1,128)} custom-call(s32[1,1]{1,0:T(1,128)} %bitcast.1.place_ref, f32[32,1,1152]{2,1,0:T(1,128)S(1)} %all_to_all.10.terms_ref, f32[32,1,1152]{2,1,0:T(1,128)S(1)} %bitcast.18), custom_call_target="tpu_custom_call" | custom-call | tf_op jit(solution)/shard_map/scan/pallas_call | solution.py:387
  36.1 3.9 %all-to-all-start.1 = ((f32[32,1,1152]{2,1,0:T(1,128)}), f32[32,1,1152]{2,1,0:T(1,128)S(1)}, u32[]{:S(2)}, u32[]{:S(2)}) async-start(f32[32,1,1152]{2,1,0:T(1,128)} %scan.1), calls=%async_computation.1 | async-start | bytes 294912 | tf_op jit(solution)/shard_map/return_terms/all_to_all | solution.py:396
  39.9 3.6 %collective-permute-start.2 = (f32[144,256]{1,0:T(8,128)S(1)}, f32[144,256]{1,0:T(8,128)S(1)}, u32[]{:S(2)}, u32[]{:S(2)}) collective-permute-start(f32[144,256]{1,0:T(8,128)S(1)} %get-tuple-element.35), channel_id=1, source_target_pairs={{0,8},{8,16},{16,24},{24,32},{32,40},{40,48},{48,56},{56,64},{64,7... | collective-permute-start | bytes 442376 | tf_op jit(solution)/shard_map/onward/ppermute | solution.py:384
  43.5 3.0 %collective-permute-done.2.shift_ref = f32[144,256]{1,0:T(8,128)S(1)} collective-permute-done((f32[144,256]{1,0:T(8,128)S(1)}, f32[144,256]{1,0:T(8,128)S(1)}, u32[]{:S(2)}, u32[]{:S(2)}) %collective-permute-start.2) | collective-permute-done | bytes 147488 | tf_op jit(solution)/shard_map/onward/ppermute | solution.py:384
  46.6 4.7 %all-to-all-done.1 = f32[32,1,1152]{2,1,0:T(1,128)S(1)} async-done(((f32[32,1,1152]{2,1,0:T(1,128)}), f32[32,1,1152]{2,1,0:T(1,128)S(1)}, u32[]{:S(2)}, u32[]{:S(2)}) %all-to-all-start.1) | async-done | bytes 147488 | tf_op jit(solution)/shard_map/return_terms/all_to_all | solution.py:396
  51.3 2.0 %final.1 = f32[2,4,128,256]{3,2,1,0:T(8,128)} custom-call(s32[1,1]{1,0:T(1,128)} %bitcast.first_ref, f32[288,128]{1,0:T(8,128)S(1)} %bitcast.16, f32[144,256]{1,0:T(8,128)S(1)} %collective-permute-done.2.shift_ref, f32[8,128]{1,0:T(8,128)S(1)} %get-tuple-element.26.params_ref, f32[96,256]{1,0:T(8,128)S(1)} %collective-permute-done.above_ref, ...), custom_call_target="tpu_custom_call" | custom-call | tf_op jit(solution)/shard_map/final/pallas_call | solution.py:397
  (3 shorter events, 0.1 us)
Async XLA Ops:
  0.0 7.2 %copy-start = (f32[4,128,128]{2,1,0:T(8,128)S(1)}, f32[4,128,128]{2,1,0:T(8,128)}, u32[]{:S(2)}) copy-start(f32[4,128,128]{2,1,0:T(8,128)} %param.10) | copy-start | bytes 786436
  1.6 8.6 %collective-permute-start = (f32[96,256]{1,0:T(8,128)S(1)}, f32[96,256]{1,0:T(8,128)S(1)}, u32[]{:S(2)}, u32[]{:S(2)}) collective-permute-start(f32[96,256]{1,0:T(8,128)S(1)} %get-tuple-element.27), channel_id=1, source_target_pairs={{0,1},{1,2},{2,3},{3,4},{4,5},{5,6},{6,7},{8,9},{9,10},{10,11},{11... | collective-permute-start | bytes 294920 | tf_op jit(solution)/shard_map/halo/ppermute | solution.py:337
  3.6 6.6 %collective-permute-start.1 = (f32[96,256]{1,0:T(8,128)S(1)}, f32[96,256]{1,0:T(8,128)S(1)}, u32[]{:S(2)}, u32[]{:S(2)}) collective-permute-start(f32[96,256]{1,0:T(8,128)S(1)} %get-tuple-element.28), channel_id=1, source_target_pairs={{1,0},{2,1},{3,2},{4,3},{5,4},{6,5},{7,6},{9,8},{10,9},{11,10},{12... | collective-permute-start | bytes 294920 | tf_op jit(solution)/shard_map/halo/ppermute | solution.py:338
  36.1 15.2 %all-to-all-start.1 = ((f32[32,1,1152]{2,1,0:T(1,128)}), f32[32,1,1152]{2,1,0:T(1,128)S(1)}, u32[]{:S(2)}, u32[]{:S(2)}) async-start(f32[32,1,1152]{2,1,0:T(1,128)} %scan.1), calls=%async_computation.1 | async-start | bytes 294912 | tf_op jit(solution)/shard_map/return_terms/all_to_all | solution.py:396
  39.9 6.6 %collective-permute-start.2 = (f32[144,256]{1,0:T(8,128)S(1)}, f32[144,256]{1,0:T(8,128)S(1)}, u32[]{:S(2)}, u32[]{:S(2)}) collective-permute-start(f32[144,256]{1,0:T(8,128)S(1)} %get-tuple-element.35), channel_id=1, source_target_pairs={{0,8},{8,16},{16,24},{24,32},{32,40},{40,48},{48,56},{56,64},{64,7... | collective-permute-start | bytes 442376 | tf_op jit(solution)/shard_map/onward/ppermute | solution.py:384

commit v7 on v6

--- a/solution.py
+++ b/solution.py
@@ -107,9 +107,9 @@
 
 
 def pack_kernel(
-    starts_hbm, sources_hbm, coupling_hbm, classes_hbm, rates_hbm,
-    up_ref, down_ref, params_ref, starts_ref, sources_ref, rates_ref,
-    starts_low, starts_high, sources_low, sources_high, coupling_row, classes_rows, sems,
+    starts_hbm, sources_hbm, coupling_hbm, classes_hbm, rates_hbm, inverses_hbm,
+    up_ref, down_ref, params_ref, starts_ref, sources_ref, rates_ref, weights_ref,
+    starts_low, starts_high, sources_low, sources_high, coupling_row, classes_rows, inverses_ref, sems,
 ):
     lines = starts_hbm.shape[1]
     low, high = pl.ds(0, SLAB), pl.ds(lines - SLAB, SLAB)
@@ -120,6 +120,7 @@
         (starts_hbm.at[:, low, :], starts_low),
         (coupling_hbm, coupling_row),
         (classes_hbm, classes_rows),
+        (inverses_hbm, inverses_ref),
         (starts_hbm, starts_ref),
         (sources_hbm, sources_ref),
         (rates_hbm, rates_ref),
@@ -146,6 +147,13 @@
             at += reach
     for ref in (up_ref, down_ref):
         ref[GROUPS * GROUP_ROWS : GROUPS * GROUP_ROWS + 3, :LB] = params_ref[0:3, :]
+    for c in range(4):
+        transposed = inverses_ref[c].T
+        rounded = transposed.astype(jnp.bfloat16)
+        rest = (transposed - rounded.astype(jnp.float32)).astype(jnp.bfloat16)
+        row, lane = c % 2 * LB, c // 2 * LB
+        weights_ref[row : row + LB, lane : lane + LB] = rounded
+        weights_ref[2 * LB + row : 3 * LB + row, lane : lane + LB] = rest
     for copy in copies[-whole:]:
         copy.wait()
 
@@ -249,12 +257,8 @@
         carried = factor * carried + terms_ref[d]
 
 
-def final_kernel(
-    first_ref, entering_ref, shift_ref, params_ref, above_ref, below_ref, weights_ref, starts_ref,
-    decay_ref, base_ref, last_ref, relaxed_ref, edge_decay_ref, edge_base_ref, edge_last_ref, edge_relaxed_ref, states_hbm, states_ref, sems,
-):
-    lines = last_ref.shape[0]
-    section = lines + 2 * EDGE
+def lines_kernel(params_ref, above_ref, below_ref, coupling_ref, masks_ref, upper_ref):
+    lines = params_ref.shape[1]
     at = GROUPS * GROUP_ROWS
 
     def along(row):
@@ -263,9 +267,26 @@
         below = columns(below_ref[at + row : at + row + 1, :LB])
         return jnp.concatenate([above[lines - EDGE :], own, below[:EDGE]], axis=0)
 
-    coupling, *categories = [along(row) for row in range(3)]
-    coupling = jnp.concatenate([coupling, coupling], axis=1)
-    masks = class_masks(categories)
+    coupling_ref[...] = along(0)
+    even, odd, upper = class_masks([along(1), along(2)])
+    for block in range(2):
+        masks_ref[0, block] = even[block]
+        masks_ref[1, block] = odd[block]
+        upper_ref[block] = jnp.where(upper[block], 1.0, 0.0)
+
+
+def final_kernel(
+    first_ref, entering_ref, shift_ref, coupling_ref, masks_ref, upper_ref, weights_ref, starts_ref,
+    decay_ref, base_ref, last_ref, relaxed_ref, edge_decay_ref, edge_base_ref, edge_last_ref, edge_relaxed_ref, states_hbm, states_ref, sems,
+):
+    lines = last_ref.shape[0]
+    section = lines + 2 * EDGE
+    coupling = jnp.concatenate([coupling_ref[...], coupling_ref[...]], axis=1)
+    masks = (
+        [masks_ref[0, block] for block in range(2)],
+        [masks_ref[1, block] for block in range(2)],
+        [upper_ref[block] > 0.5 for block in range(2)],
+    )
 
     entering = jnp.concatenate([entering_ref[:section, :], entering_ref[section:, :]], axis=1)
     shift = shift_ref[...]
@@ -311,11 +332,17 @@
         return jax.ShapeDtypeStruct(dims, f32)
 
     message = shape(MESSAGE_ROWS, line_len)
-    up, down, params, held_starts, held_sources, rates = pl.pallas_call(
+    up, down, params, held_starts, held_sources, rates, weights = pl.pallas_call(
         pack_kernel,
-        out_shape=(message, message, shape(8, lines), *[shape(*x.shape) for x in (starts, sources, coarse_rate)]),
-        in_specs=[HBM] * 5,
-        out_specs=[VMEM] * 6,
+        out_shape=(
+            message,
+            message,
+            shape(8, lines),
+            *[shape(*x.shape) for x in (starts, sources, coarse_rate)],
+            jax.ShapeDtypeStruct((4 * LB, 2 * LB), jnp.bfloat16),
+        ),
+        in_specs=[HBM] * 6,
+        out_specs=[VMEM] * 7,
         scratch_shapes=[
             pltpu.VMEM((GROUPS, SLAB, line_len), f32),
             pltpu.VMEM((GROUPS, SLAB, line_len), f32),
@@ -323,31 +350,20 @@
             pltpu.VMEM((GROUPS, STEPS, SLAB, line_len), f32),
             pltpu.VMEM((1, lines), f32),
             pltpu.VMEM((2, lines), jnp.int32),
-            pltpu.SemaphoreType.DMA((9,)),
+            pltpu.VMEM(inverses.shape, f32),
+            pltpu.SemaphoreType.DMA((10,)),
         ],
         compiler_params=grant(6),
         name="pack",
     )(*[
         pltpu.with_memory_space_constraint(x, pltpu.HBM)
-        for x in (starts, sources, coupling.reshape(1, lines), classes.T, coarse_rate)
+        for x in (starts, sources, coupling.reshape(1, lines), classes.T, coarse_rate, inverses)
     ])
 
     with jax.named_scope("halo"):
         upward = [(i, i + 1) for i in range(along - 1)]
         above = lax.ppermute(up, "space", upward)
         below = lax.ppermute(down, "space", [(j, i) for i, j in upward])
-
-    with jax.named_scope("weights"):
-        transposed = inverses.transpose(0, 2, 1)
-        table = jnp.concatenate(
-            [
-                jnp.concatenate([transposed[0], transposed[2]], axis=1),
-                jnp.concatenate([transposed[1], transposed[3]], axis=1),
-            ],
-            axis=0,
-        )
-        high = lax.reduce_precision(table, 8, 7)
-        weights = jnp.concatenate([high, table - high], axis=0).astype(jnp.bfloat16)
 
     def relaxed(rows):
         return shape(GROUPS, STEPS - 1, rows, line_len)
@@ -394,6 +410,19 @@
     )(place, terms, factors.reshape(split))
     with jax.named_scope("return_terms"):
         entering = lax.all_to_all(entering, "tm", 0, 0)
+    spread_lines = pl.pallas_call(
+        lines_kernel,
+        out_shape=(
+            shape(near_rows, LB),
+            jax.ShapeDtypeStruct((2, 2, near_rows, LB), jnp.bfloat16),
+            shape(2, near_rows, LB),
+        ),
+        in_specs=[VMEM] * 3,
+        out_specs=[VMEM] * 3,
+        compiler_params=grant(4),
+        cost_estimate=pl.CostEstimate(flops=1_000_000_000, bytes_accessed=1_000_000, transcendentals=0),
+        name="lines",
+    )(params, above, below)
     return pl.pallas_call(
         final_kernel,
         out_shape=shape(GROUPS, STEPS, lines, line_len),
@@ -405,7 +434,7 @@
         ],
         compiler_params=grant(20),
         name="final",
-    )(first, entering.reshape(sections, LB), shift, params, above, below, weights, held_starts, *own, *edges)
+    )(first, entering.reshape(sections, LB), shift, *spread_lines, weights, held_starts, *own, *edges)
 
 
 def solution(mesh):

time: 53.6 us -> 53.5 us (level)
    ppermute x1, waiting for transfers between devices: 3.05 us -> 3.65 us  [shards(): shift = lax.ppermute(shift, 'tm', [(i, i + 1) for i in range(count - 1)])]
    all_to_all x1, waiting for transfers between devices: 4.69 us -> 4.12 us  [shards(): entering = lax.all_to_all(entering, 'tm', 0, 0)]
  transfers between devices with their start and end apart: 4 -> 4, of which waited for: 2 -> 2; matrix products, arithmetic and copies ran while one was open for 0% -> 0% of each run, Pallas kernels for 5% -> 6%
where the time goes in v7:
time: 53.5 us; the launch traced here: 53.2 us
  blocking collectives  22.9 us (43%)
  starting transfers between devices  13.2 us (25%)
  Pallas kernels  9.29 us (17%)
  waiting for transfers between devices  7.78 us (15%)
    all_to_all x1, blocking collectives, shards(): terms = lax.all_to_all(terms.reshape(split), 'tm', 0, 0)  22.9 us
    all_to_all x1, waiting for transfers between devices, shards(): entering = lax.all_to_all(entering, 'tm', 0, 0)  4.12 us
    all_to_all x1, starting transfers between devices, shards(): entering = lax.all_to_all(entering, 'tm', 0, 0)  3.93 us
    ppermute x1, starting transfers between devices, shards(): shift = lax.ppermute(shift, 'tm', [(i, i + 1) for i in range(count - 1)])  3.7 us
    ppermute x1, waiting for transfers between devices, shards(): shift = lax.ppermute(shift, 'tm', [(i, i + 1) for i in range(count - 1)])  3.65 us
    ppermute x1, starting transfers between devices, shards(): below = lax.ppermute(down, 'space', [(j, i) for i, j in upward])  3.64 us
    pallas_call x1, Pallas kernels, shards(): pl.pallas_call(own_kernel, out_shape=(*[shape(lines, line_len)] * 5, rela...  2.72 us
    pallas_call x1, Pallas kernels, shards(): pl.pallas_call(edge_kernel, out_shape=(shape(sections, LB), shape(section...  2.04 us
  transfers between devices with their start and end apart: 4, of which 2 were waited for; matrix products, arithmetic and copies ran while one was open for 0% of the time, Pallas kernels for 6%

profile of v7, /device:TPU:8, one launch (start us, length us, event | category | flops | bytes accessed | tf_op | source)
XLA Modules:
  0.0 53.2 jit_solution(3963288544193274676)
XLA Ops:
  0.0 1.7 %pack.1 = (f32[96,256]{1,0:T(8,128)S(1)}, f32[96,256]{1,0:T(8,128)S(1)}, f32[8,128]{1,0:T(8,128)S(1)}, f32[2,128,256]{2,1,0:T(8,128)S(1)}, f32[2,4,128,256]{3,2,...) custom-call(f32[2,128,256]{2,1,0:T(8,128)} %starts_hbm.1, f32[2,4,128,256]{3,2,1,0:T(8,128)} %sources_hbm.1, ...), custom_call_target="tpu_custom_call" | custom-call | tf_op jit(solution)/shard_map/pack/pallas_call | solution.py:335
  1.7 1.9 %collective-permute-start = (f32[96,256]{1,0:T(8,128)S(1)}, f32[96,256]{1,0:T(8,128)S(1)}, u32[]{:S(2)}, u32[]{:S(2)}) collective-permute-start(f32[96,256]{1,0:T(8,128)S(1)} %get-tuple-element.31), channel_id=1, source_target_pairs={{0,1},{1,2},{2,3},{3,4},{4,5},{5,6},{6,7},{8,9},{9,10},{10,11},{11... | collective-permute-start | bytes 294920 | tf_op jit(solution)/shard_map/halo/ppermute | solution.py:365
  3.6 3.6 %collective-permute-start.1 = (f32[96,256]{1,0:T(8,128)S(1)}, f32[96,256]{1,0:T(8,128)S(1)}, u32[]{:S(2)}, u32[]{:S(2)}) collective-permute-start(f32[96,256]{1,0:T(8,128)S(1)} %get-tuple-element.32), channel_id=1, source_target_pairs={{1,0},{2,1},{3,2},{4,3},{5,4},{6,5},{7,6},{9,8},{10,9},{11,10},{12... | collective-permute-start | bytes 294920 | tf_op jit(solution)/shard_map/halo/ppermute | solution.py:366
  7.3 2.7 %own.1 = (f32[128,256]{1,0:T(8,128)S(1)}, f32[128,256]{1,0:T(8,128)S(1)}, f32[128,256]{1,0:T(8,128)S(1)}, f32[128,256]{1,0:T(8,128)S(1)}, f32[128,256]{1,0:T(8,128)S(1)}, /*index=5*/f32[2,3,128,256]{3,2,1,0:T(8,128)S(1)}) custom-call(s32[1,1]{1,0:T(1,128)} %bitcast.first_ref, f32[2,128,256]{2,1,0:T(8,128)S(1)} %get-tuple-element.28.starts_ref, ...), custom_call_target="tpu_custom_call" | custom-call | flops 5000000000 | bytes 4000000 | tf_op jit(solution)/shard_map/own/pallas_call | solution.py:371
  10.0 0.0 collective-permute-done.above_ref
  10.0 0.0 collective-permute-done.1.below_ref
  10.0 2.0 %edge.1 = (f32[288,128]{1,0:T(8,128)S(1)}, f32[288,128]{1,0:T(8,128)S(1)}, f32[144,256]{1,0:T(8,128)S(1)}, f32[32,256]{1,0:T(8,128)S(1)}, f32[2,32,256]{2,1,0:T(...) custom-call(s32[1,1]{1,0:T(1,128)} %bitcast.first_ref, ...), custom_call_target="tpu_custom_call" | custom-call | tf_op jit(solution)/shard_map/edge/pallas_call | solution.py:380
  12.1 22.9 %all_to_all.10.terms_ref = f32[32,1,1152]{2,1,0:T(1,128)S(1)} all-to-all(f32[32,1,1152]{2,1,0:T(1,128)S(1)} %bitcast.8), channel_id=1, replica_groups=mesh['tm'=32,'space'=8] {'tm'}, dimensions={0} | all-to-all | bytes 294912 | tf_op jit(solution)/shard_map/gather_terms/all_to_all | solution.py:402
  35.0 0.7 %scan.1 = f32[32,1,1152]{2,1,0:T(1,128)} custom-call(s32[1,1]{1,0:T(1,128)} %bitcast.1.place_ref, f32[32,1,1152]{2,1,0:T(1,128)S(1)} %all_to_all.10.terms_ref, f32[32,1,1152]{2,1,0:T(1,128)S(1)} %bitcast.9), custom_call_target="tpu_custom_call" | custom-call | tf_op jit(solution)/shard_map/scan/pallas_call | solution.py:403
  35.7 3.9 %all-to-all-start.1 = ((f32[32,1,1152]{2,1,0:T(1,128)}), f32[32,1,1152]{2,1,0:T(1,128)S(1)}, u32[]{:S(2)}, u32[]{:S(2)}) async-start(f32[32,1,1152]{2,1,0:T(1,128)} %scan.1), calls=%async_computation.1 | async-start | bytes 294912 | tf_op jit(solution)/shard_map/return_terms/all_to_all | solution.py:412
  39.6 3.7 %collective-permute-start.2 = (f32[144,256]{1,0:T(8,128)S(1)}, f32[144,256]{1,0:T(8,128)S(1)}, u32[]{:S(2)}, u32[]{:S(2)}) collective-permute-start(f32[144,256]{1,0:T(8,128)S(1)} %get-tuple-element.40), channel_id=1, source_target_pairs={{0,8},{8,16},{16,24},{24,32},{32,40},{40,48},{48,56},{56,64},{64,7... | collective-permute-start | bytes 442376 | tf_op jit(solution)/shard_map/onward/ppermute | solution.py:400
  43.3 0.2 lines.1
  43.6 3.7 %collective-permute-done.2.shift_ref = f32[144,256]{1,0:T(8,128)S(1)} collective-permute-done((f32[144,256]{1,0:T(8,128)S(1)}, f32[144,256]{1,0:T(8,128)S(1)}, u32[]{:S(2)}, u32[]{:S(2)}) %collective-permute-start.2) | collective-permute-done | bytes 147488 | tf_op jit(solution)/shard_map/onward/ppermute | solution.py:400
  47.2 4.1 %all-to-all-done.1 = f32[32,1,1152]{2,1,0:T(1,128)S(1)} async-done(((f32[32,1,1152]{2,1,0:T(1,128)}), f32[32,1,1152]{2,1,0:T(1,128)S(1)}, u32[]{:S(2)}, u32[]{:S(2)}) %all-to-all-start.1) | async-done | bytes 147488 | tf_op jit(solution)/shard_map/return_terms/all_to_all | solution.py:412
  51.3 1.9 %final.1 = f32[2,4,128,256]{3,2,1,0:T(8,128)} custom-call(s32[1,1]{1,0:T(1,128)} %bitcast.first_ref, f32[288,128]{1,0:T(8,128)S(1)} %bitcast.7, f32[144,256]{1,0:T(8,128)S(1)} %collective-permute-done.2.shift_ref, f32[144,128]{1,0:T(8,128)S(1)} %get-tuple-element.41.coupling_ref, bf16[2,2,144,128]{3,2,1,0:T(8,128)(2,1)S(1)} %get-tuple-element.42.masks_ref, ...), custom_call_target="tpu_custom_call" | custom-call | tf_op jit(solution)/shard_map/final/pallas_call | solution.py:426
Async XLA Ops:
  1.7 8.3 %collective-permute-start = (f32[96,256]{1,0:T(8,128)S(1)}, f32[96,256]{1,0:T(8,128)S(1)}, u32[]{:S(2)}, u32[]{:S(2)}) collective-permute-start(f32[96,256]{1,0:T(8,128)S(1)} %get-tuple-element.31), channel_id=1, source_target_pairs={{0,1},{1,2},{2,3},{3,4},{4,5},{5,6},{6,7},{8,9},{9,10},{10,11},{11... | collective-permute-start | bytes 294920 | tf_op jit(solution)/shard_map/halo/ppermute | solution.py:365
  3.6 6.4 %collective-permute-start.1 = (f32[96,256]{1,0:T(8,128)S(1)}, f32[96,256]{1,0:T(8,128)S(1)}, u32[]{:S(2)}, u32[]{:S(2)}) collective-permute-start(f32[96,256]{1,0:T(8,128)S(1)} %get-tuple-element.32), channel_id=1, source_target_pairs={{1,0},{2,1},{3,2},{4,3},{5,4},{6,5},{7,6},{9,8},{10,9},{11,10},{12... | collective-permute-start | bytes 294920 | tf_op jit(solution)/shard_map/halo/ppermute | solution.py:366
  35.7 15.6 %all-to-all-start.1 = ((f32[32,1,1152]{2,1,0:T(1,128)}), f32[32,1,1152]{2,1,0:T(1,128)S(1)}, u32[]{:S(2)}, u32[]{:S(2)}) async-start(f32[32,1,1152]{2,1,0:T(1,128)} %scan.1), calls=%async_computation.1 | async-start | bytes 294912 | tf_op jit(solution)/shard_map/return_terms/all_to_all | solution.py:412
  39.6 7.6 %collective-permute-start.2 = (f32[144,256]{1,0:T(8,128)S(1)}, f32[144,256]{1,0:T(8,128)S(1)}, u32[]{:S(2)}, u32[]{:S(2)}) collective-permute-start(f32[144,256]{1,0:T(8,128)S(1)} %get-tuple-element.40), channel_id=1, source_target_pairs={{0,8},{8,16},{16,24},{24,32},{32,40},{40,48},{48,56},{56,64},{64,7... | collective-permute-start | bytes 442376 | tf_op jit(solution)/shard_map/onward/ppermute | solution.py:400

commit v8 on v7

--- a/solution.py
+++ b/solution.py
@@ -49,20 +49,21 @@
 def solve_field(field, masks, weights):
     even, odd, upper = masks
     rows = field.shape[0]
-    left = []
+    highs, lows = [], []
     for block in range(2):
         x = field[:, block * LB : (block + 1) * LB]
         high = x.astype(jnp.bfloat16)
         low = (x - high.astype(jnp.float32)).astype(jnp.bfloat16)
-        high_pair = [high * even[block], high * odd[block]]
-        low_pair = [low * even[block], low * odd[block]]
-        left.append(jnp.concatenate(high_pair + low_pair + high_pair, axis=1))
-    weights = jnp.concatenate([weights[: 2 * LB], weights], axis=0)
-    product = jnp.dot(jnp.concatenate(left, axis=0), weights, preferred_element_type=jnp.float32)
+        highs.append(jnp.concatenate([high * even[block], high * odd[block]], axis=1))
+        lows.append(jnp.concatenate([low * even[block], low * odd[block]], axis=1))
+    highs, lows = jnp.concatenate(highs, axis=0), jnp.concatenate(lows, axis=0)
+    pairs = ((highs, weights[: 2 * LB]), (lows, weights[: 2 * LB]), (highs, weights[2 * LB :]))
+    products = [jnp.dot(left, right, preferred_element_type=jnp.float32) for left, right in pairs]
     blocks = []
     for block in range(2):
-        part = product[block * rows : (block + 1) * rows]
-        blocks.append(jnp.where(upper[block], part[:, LB:], part[:, :LB]))
+        parts = [product[block * rows : (block + 1) * rows] for product in products]
+        first, second, third = [jnp.where(upper[block], part[:, LB:], part[:, :LB]) for part in parts]
+        blocks.append(first + second + third)
     return jnp.concatenate(blocks, axis=1)
 
 
@@ -109,44 +110,26 @@
 def pack_kernel(
     starts_hbm, sources_hbm, coupling_hbm, classes_hbm, rates_hbm, inverses_hbm,
     up_ref, down_ref, params_ref, starts_ref, sources_ref, rates_ref, weights_ref,
-    starts_low, starts_high, sources_low, sources_high, coupling_row, classes_rows, inverses_ref, sems,
+    coupling_row, classes_rows, inverses_ref, sems,
 ):
     lines = starts_hbm.shape[1]
-    low, high = pl.ds(0, SLAB), pl.ds(lines - SLAB, SLAB)
     pairs = [
-        (sources_hbm.at[:, :, high, :], sources_high),
-        (sources_hbm.at[:, :, low, :], sources_low),
-        (starts_hbm.at[:, high, :], starts_high),
-        (starts_hbm.at[:, low, :], starts_low),
+        (inverses_hbm, inverses_ref),
         (coupling_hbm, coupling_row),
         (classes_hbm, classes_rows),
-        (inverses_hbm, inverses_ref),
-        (starts_hbm, starts_ref),
-        (sources_hbm, sources_ref),
+        *[(starts_hbm.at[g], starts_ref.at[g]) for g in range(GROUPS)],
+        *[(sources_hbm.at[g, m], sources_ref.at[g, m]) for g in range(GROUPS) for m in range(STEPS)],
         (rates_hbm, rates_ref),
     ]
-    whole = 3
     copies = [pltpu.make_async_copy(src, dst, sems.at[i]) for i, (src, dst) in enumerate(pairs)]
     for copy in copies:
         copy.start()
     for ref in (up_ref, down_ref, params_ref):
         ref[...] = jnp.zeros_like(ref)
-    for copy in copies[:-whole]:
+    for copy in copies[:3]:
         copy.wait()
     params_ref[0:1, :] = coupling_row[...]
     params_ref[1:3, :] = classes_rows[...].astype(jnp.float32)
-    for g in range(GROUPS):
-        at = g * GROUP_ROWS
-        for index, reach in enumerate(REACH):
-            if index == 0:
-                up, down = starts_high[g, SLAB - reach :, :], starts_low[g, :reach, :]
-            else:
-                up, down = sources_high[g, index - 1, SLAB - reach :, :], sources_low[g, index - 1, :reach, :]
-            up_ref[at : at + reach, :] = up
-            down_ref[at : at + reach, :] = down
-            at += reach
-    for ref in (up_ref, down_ref):
-        ref[GROUPS * GROUP_ROWS : GROUPS * GROUP_ROWS + 3, :LB] = params_ref[0:3, :]
     for c in range(4):
         transposed = inverses_ref[c].T
         rounded = transposed.astype(jnp.bfloat16)
@@ -154,8 +137,20 @@
         row, lane = c % 2 * LB, c // 2 * LB
         weights_ref[row : row + LB, lane : lane + LB] = rounded
         weights_ref[2 * LB + row : 3 * LB + row, lane : lane + LB] = rest
-    for copy in copies[-whole:]:
+    for copy in copies[3:]:
         copy.wait()
+    for g in range(GROUPS):
+        at = g * GROUP_ROWS
+        for index, reach in enumerate(REACH):
+            if index == 0:
+                own = starts_ref.at[g]
+            else:
+                own = sources_ref.at[g, index - 1]
+            up_ref[at : at + reach, :] = own[lines - reach :, :]
+            down_ref[at : at + reach, :] = own[:reach, :]
+            at += reach
+    for ref in (up_ref, down_ref):
+        ref[GROUPS * GROUP_ROWS : GROUPS * GROUP_ROWS + 3, :LB] = params_ref[0:3, :]
 
 
 def own_kernel(
@@ -297,21 +292,21 @@
     last = [base[1][inner] + starts_ref[1], joined(last_ref[...], edge_last_ref[...])]
     passed = decay * entering
 
-    def send(m):
-        copy = pltpu.make_async_copy(states_ref.at[:, m], states_hbm.at[:, m], sems.at[m])
+    def send(g, m):
+        copy = pltpu.make_async_copy(states_ref.at[g, m], states_hbm.at[g, m], sems.at[g, m])
         copy.start()
         return copy
 
     states_ref[0, 3] = passed[inner] + last[0]
     states_ref[1, 3] = (decay * passed)[inner] + last[1]
-    copies = [send(3)]
+    copies = [send(g, 3) for g in range(GROUPS)]
     state = [entering + shift - base[0], passed + base[1]]
     weights = weights_ref[...]
     for m in range(STEPS - 1):
         state = solve_lines([spread(s, coupling) for s in state], masks, weights)
         for g in range(GROUPS):
             states_ref[g, m] = joined(relaxed_ref[g, m], edge_relaxed_ref[g, m]) + state[g][inner]
-        copies.append(send(m))
+            copies.append(send(g, m))
     for copy in copies:
         copy.wait()
 
@@ -344,14 +339,10 @@
         in_specs=[HBM] * 6,
         out_specs=[VMEM] * 7,
         scratch_shapes=[
-            pltpu.VMEM((GROUPS, SLAB, line_len), f32),
-            pltpu.VMEM((GROUPS, SLAB, line_len), f32),
-            pltpu.VMEM((GROUPS, STEPS, SLAB, line_len), f32),
-            pltpu.VMEM((GROUPS, STEPS, SLAB, line_len), f32),
             pltpu.VMEM((1, lines), f32),
             pltpu.VMEM((2, lines), jnp.int32),
             pltpu.VMEM(inverses.shape, f32),
-            pltpu.SemaphoreType.DMA((10,)),
+            pltpu.SemaphoreType.DMA((4 + GROUPS * (1 + STEPS),)),
         ],
         compiler_params=grant(6),
         name="pack",
@@ -430,7 +421,7 @@
         out_specs=HBM,
         scratch_shapes=[
             pltpu.VMEM((GROUPS, STEPS, lines, line_len), f32),
-            pltpu.SemaphoreType.DMA((STEPS,)),
+            pltpu.SemaphoreType.DMA((GROUPS, STEPS)),
         ],
         compiler_params=grant(20),
         name="final",

time: 53.5 us -> 52.6 us (0.983)
  Pallas kernels: 9.29 us -> 8.44 us
  transfers between devices with their start and end apart: 4 -> 4, of which waited for: 2 -> 2; matrix products, arithmetic and copies ran while one was open for 0% -> 0% of each run, Pallas kernels for 6% -> 5%
where the time goes in v8:
time: 52.6 us; the launch traced here: 52.3 us
  blocking collectives  22.8 us (43%)
  starting transfers between devices  13 us (25%)
  Pallas kernels  8.44 us (16%)
  waiting for transfers between devices  7.96 us (15%)
    all_to_all x1, blocking collectives, shards(): terms = lax.all_to_all(terms.reshape(split), 'tm', 0, 0)  22.8 us
    all_to_all x1, waiting for transfers between devices, shards(): entering = lax.all_to_all(entering, 'tm', 0, 0)  4.15 us
    all_to_all x1, starting transfers between devices, shards(): entering = lax.all_to_all(entering, 'tm', 0, 0)  3.86 us
    ppermute x1, waiting for transfers between devices, shards(): shift = lax.ppermute(shift, 'tm', [(i, i + 1) for i in range(count - 1)])  3.8 us
    ppermute x1, starting transfers between devices, shards(): below = lax.ppermute(down, 'space', [(j, i) for i, j in upward])  3.64 us
    ppermute x1, starting transfers between devices, shards(): shift = lax.ppermute(shift, 'tm', [(i, i + 1) for i in range(count - 1)])  3.59 us
    pallas_call x1, Pallas kernels, shards(): pl.pallas_call(own_kernel, out_shape=(*[shape(lines, line_len)] * 5, rela...  2.51 us
    ppermute x1, starting transfers between devices, shards(): above = lax.ppermute(up, 'space', upward)  1.92 us
  transfers between devices with their start and end apart: 4, of which 2 were waited for; matrix products, arithmetic and copies ran while one was open for 0% of the time, Pallas kernels for 5%

profile of v8, /device:TPU:8, one launch (start us, length us, event | category | flops | bytes accessed | tf_op | source)
XLA Modules:
  0.0 52.3 jit_solution(13391510108860381037)
XLA Ops:
  0.0 1.6 %pack.1 = (f32[96,256]{1,0:T(8,128)S(1)}, f32[96,256]{1,0:T(8,128)S(1)}, f32[8,128]{1,0:T(8,128)S(1)}, f32[2,128,256]{2,1,0:T(8,128)S(1)}, f32[2,4,128,256]{3,2,...) custom-call(f32[2,128,256]{2,1,0:T(8,128)} %starts_hbm.1, f32[2,4,128,256]{3,2,1,0:T(8,128)} %sources_hbm.1, ...), custom_call_target="tpu_custom_call" | custom-call | tf_op jit(solution)/shard_map/pack/pallas_call | solution.py:330
  1.6 1.9 %collective-permute-start = (f32[96,256]{1,0:T(8,128)S(1)}, f32[96,256]{1,0:T(8,128)S(1)}, u32[]{:S(2)}, u32[]{:S(2)}) collective-permute-start(f32[96,256]{1,0:T(8,128)S(1)} %get-tuple-element.31), channel_id=1, source_target_pairs={{0,1},{1,2},{2,3},{3,4},{4,5},{5,6},{6,7},{8,9},{9,10},{10,11},{11... | collective-permute-start | bytes 294920 | tf_op jit(solution)/shard_map/halo/ppermute | solution.py:356
  3.5 3.6 %collective-permute-start.1 = (f32[96,256]{1,0:T(8,128)S(1)}, f32[96,256]{1,0:T(8,128)S(1)}, u32[]{:S(2)}, u32[]{:S(2)}) collective-permute-start(f32[96,256]{1,0:T(8,128)S(1)} %get-tuple-element.32), channel_id=1, source_target_pairs={{1,0},{2,1},{3,2},{4,3},{5,4},{6,5},{7,6},{9,8},{10,9},{11,10},{12... | collective-permute-start | bytes 294920 | tf_op jit(solution)/shard_map/halo/ppermute | solution.py:357
  7.2 2.5 %own.1 = (f32[128,256]{1,0:T(8,128)S(1)}, f32[128,256]{1,0:T(8,128)S(1)}, f32[128,256]{1,0:T(8,128)S(1)}, f32[128,256]{1,0:T(8,128)S(1)}, f32[128,256]{1,0:T(8,128)S(1)}, /*index=5*/f32[2,3,128,256]{3,2,1,0:T(8,128)S(1)}) custom-call(s32[1,1]{1,0:T(1,128)} %bitcast.first_ref, f32[2,128,256]{2,1,0:T(8,128)S(1)} %get-tuple-element.28.starts_ref, ...), custom_call_target="tpu_custom_call" | custom-call | flops 5000000000 | bytes 4000000 | tf_op jit(solution)/shard_map/own/pallas_call | solution.py:362
  9.7 0.0 collective-permute-done.above_ref
  9.7 0.0 collective-permute-done.1.below_ref
  9.7 1.8 %edge.1 = (f32[288,128]{1,0:T(8,128)S(1)}, f32[288,128]{1,0:T(8,128)S(1)}, f32[144,256]{1,0:T(8,128)S(1)}, f32[32,256]{1,0:T(8,128)S(1)}, f32[2,32,256]{2,1,0:T(...) custom-call(s32[1,1]{1,0:T(1,128)} %bitcast.first_ref, ...), custom_call_target="tpu_custom_call" | custom-call | tf_op jit(solution)/shard_map/edge/pallas_call | solution.py:371
  11.5 22.8 %all_to_all.10.terms_ref = f32[32,1,1152]{2,1,0:T(1,128)S(1)} all-to-all(f32[32,1,1152]{2,1,0:T(1,128)S(1)} %bitcast.8), channel_id=1, replica_groups=mesh['tm'=32,'space'=8] {'tm'}, dimensions={0} | all-to-all | bytes 294912 | tf_op jit(solution)/shard_map/gather_terms/all_to_all | solution.py:393
  34.3 0.7 %scan.1 = f32[32,1,1152]{2,1,0:T(1,128)} custom-call(s32[1,1]{1,0:T(1,128)} %bitcast.1.place_ref, f32[32,1,1152]{2,1,0:T(1,128)S(1)} %all_to_all.10.terms_ref, f32[32,1,1152]{2,1,0:T(1,128)S(1)} %bitcast.9), custom_call_target="tpu_custom_call" | custom-call | tf_op jit(solution)/shard_map/scan/pallas_call | solution.py:394
  35.1 3.9 %all-to-all-start.1 = ((f32[32,1,1152]{2,1,0:T(1,128)}), f32[32,1,1152]{2,1,0:T(1,128)S(1)}, u32[]{:S(2)}, u32[]{:S(2)}) async-start(f32[32,1,1152]{2,1,0:T(1,128)} %scan.1), calls=%async_computation.1 | async-start | bytes 294912 | tf_op jit(solution)/shard_map/return_terms/all_to_all | solution.py:403
  38.9 3.6 %collective-permute-start.2 = (f32[144,256]{1,0:T(8,128)S(1)}, f32[144,256]{1,0:T(8,128)S(1)}, u32[]{:S(2)}, u32[]{:S(2)}) collective-permute-start(f32[144,256]{1,0:T(8,128)S(1)} %get-tuple-element.40), channel_id=1, source_target_pairs={{0,8},{8,16},{16,24},{24,32},{32,40},{40,48},{48,56},{56,64},{64,7... | collective-permute-start | bytes 442376 | tf_op jit(solution)/shard_map/onward/ppermute | solution.py:391
  42.5 0.2 lines.1
  42.7 3.8 %collective-permute-done.2.shift_ref = f32[144,256]{1,0:T(8,128)S(1)} collective-permute-done((f32[144,256]{1,0:T(8,128)S(1)}, f32[144,256]{1,0:T(8,128)S(1)}, u32[]{:S(2)}, u32[]{:S(2)}) %collective-permute-start.2) | collective-permute-done | bytes 147488 | tf_op jit(solution)/shard_map/onward/ppermute | solution.py:391
  46.5 4.2 %all-to-all-done.1 = f32[32,1,1152]{2,1,0:T(1,128)S(1)} async-done(((f32[32,1,1152]{2,1,0:T(1,128)}), f32[32,1,1152]{2,1,0:T(1,128)S(1)}, u32[]{:S(2)}, u32[]{:S(2)}) %all-to-all-start.1) | async-done | bytes 147488 | tf_op jit(solution)/shard_map/return_terms/all_to_all | solution.py:403
  50.7 1.6 %final.1 = f32[2,4,128,256]{3,2,1,0:T(8,128)} custom-call(s32[1,1]{1,0:T(1,128)} %bitcast.first_ref, f32[288,128]{1,0:T(8,128)S(1)} %bitcast.7, f32[144,256]{1,0:T(8,128)S(1)} %collective-permute-done.2.shift_ref, f32[144,128]{1,0:T(8,128)S(1)} %get-tuple-element.41.coupling_ref, bf16[2,2,144,128]{3,2,1,0:T(8,128)(2,1)S(1)} %get-tuple-element.42.masks_ref, ...), custom_call_target="tpu_custom_call" | custom-call | tf_op jit(solution)/shard_map/final/pallas_call | solution.py:417
Async XLA Ops:
  1.6 8.1 %collective-permute-start = (f32[96,256]{1,0:T(8,128)S(1)}, f32[96,256]{1,0:T(8,128)S(1)}, u32[]{:S(2)}, u32[]{:S(2)}) collective-permute-start(f32[96,256]{1,0:T(8,128)S(1)} %get-tuple-element.31), channel_id=1, source_target_pairs={{0,1},{1,2},{2,3},{3,4},{4,5},{5,6},{6,7},{8,9},{9,10},{10,11},{11... | collective-permute-start | bytes 294920 | tf_op jit(solution)/shard_map/halo/ppermute | solution.py:356
  3.5 6.2 %collective-permute-start.1 = (f32[96,256]{1,0:T(8,128)S(1)}, f32[96,256]{1,0:T(8,128)S(1)}, u32[]{:S(2)}, u32[]{:S(2)}) collective-permute-start(f32[96,256]{1,0:T(8,128)S(1)} %get-tuple-element.32), channel_id=1, source_target_pairs={{1,0},{2,1},{3,2},{4,3},{5,4},{6,5},{7,6},{9,8},{10,9},{11,10},{12... | collective-permute-start | bytes 294920 | tf_op jit(solution)/shard_map/halo/ppermute | solution.py:357
  35.1 15.6 %all-to-all-start.1 = ((f32[32,1,1152]{2,1,0:T(1,128)}), f32[32,1,1152]{2,1,0:T(1,128)S(1)}, u32[]{:S(2)}, u32[]{:S(2)}) async-start(f32[32,1,1152]{2,1,0:T(1,128)} %scan.1), calls=%async_computation.1 | async-start | bytes 294912 | tf_op jit(solution)/shard_map/return_terms/all_to_all | solution.py:403
  38.9 7.6 %collective-permute-start.2 = (f32[144,256]{1,0:T(8,128)S(1)}, f32[144,256]{1,0:T(8,128)S(1)}, u32[]{:S(2)}, u32[]{:S(2)}) collective-permute-start(f32[144,256]{1,0:T(8,128)S(1)} %get-tuple-element.40), channel_id=1, source_target_pairs={{0,8},{8,16},{16,24},{24,32},{32,40},{40,48},{48,56},{56,64},{64,7... | collective-permute-start | bytes 442376 | tf_op jit(solution)/shard_map/onward/ppermute | solution.py:391

commit v9 on v8

--- a/solution.py
+++ b/solution.py
@@ -23,6 +23,10 @@
 
 def columns(row):
     return jnp.broadcast_to(row, (LB, LB)).T
+
+
+def unless(flag_ref):
+    return jnp.where(flag_ref[0, 0] > 0, 0.0, 1.0)
 
 
 def class_masks(categories):
@@ -184,7 +188,7 @@
 
 
 def edge_kernel(
-    first_ref, starts_ref, sources_ref, params_ref, above_ref, below_ref, weights_ref, rates_ref,
+    first_ref, top_ref, bottom_ref, starts_ref, sources_ref, params_ref, above_ref, below_ref, weights_ref, rates_ref,
     own_term_ref, own_shift_ref, own_decay_ref,
     terms_ref, factors_ref, shift_ref, decay_ref, base_ref, last_ref, relaxed_ref, halo_ref,
 ):
@@ -192,9 +196,10 @@
     lane = lax.broadcasted_iota(jnp.int32, (8, LB), 1)
     at = GROUPS * GROUP_ROWS
     own = params_ref[...]
+    keep_above, keep_below = unless(top_ref), unless(bottom_ref)
     halo_ref[...] = jnp.zeros_like(halo_ref)
-    halo_ref[0, 0:3, :LB] = above_ref[at : at + 3, :LB]
-    halo_ref[0, 8:11, :LB] = below_ref[at : at + 3, :LB]
+    halo_ref[0, 0:3, :LB] = keep_above * above_ref[at : at + 3, :LB]
+    halo_ref[0, 8:11, :LB] = keep_below * below_ref[at : at + 3, :LB]
     above, below = halo_ref[0, 0:8, :LB], halo_ref[0, 8:16, :LB]
     upper = jnp.where(lane < SLAB, pltpu.roll(above, SLAB, 1), pltpu.roll(own, SLAB, 1))
     lower = jnp.where(lane < 3 * SLAB, pltpu.roll(own, 3 * SLAB, 1), pltpu.roll(below, 3 * SLAB, 1))
@@ -208,8 +213,8 @@
         at = g * GROUP_ROWS
         for index, reach in enumerate(REACH):
             slab = g * len(REACH) + index
-            halo_ref[slab, SLAB - reach : SLAB, :] = above_ref[at : at + reach, :]
-            halo_ref[slab, SLAB : SLAB + reach, :] = below_ref[at : at + reach, :]
+            halo_ref[slab, SLAB - reach : SLAB, :] = keep_above * above_ref[at : at + reach, :]
+            halo_ref[slab, SLAB : SLAB + reach, :] = keep_below * below_ref[at : at + reach, :]
             at += reach
 
     def strips(slab, low, high):
@@ -252,14 +257,14 @@
         carried = factor * carried + terms_ref[d]
 
 
-def lines_kernel(params_ref, above_ref, below_ref, coupling_ref, masks_ref, upper_ref):
+def lines_kernel(top_ref, bottom_ref, params_ref, above_ref, below_ref, coupling_ref, masks_ref, upper_ref):
     lines = params_ref.shape[1]
     at = GROUPS * GROUP_ROWS
 
     def along(row):
         own = columns(params_ref[row : row + 1, :])
-        above = columns(above_ref[at + row : at + row + 1, :LB])
-        below = columns(below_ref[at + row : at + row + 1, :LB])
+        above = columns(unless(top_ref) * above_ref[at + row : at + row + 1, :LB])
+        below = columns(unless(bottom_ref) * below_ref[at + row : at + row + 1, :LB])
         return jnp.concatenate([above[lines - EDGE :], own, below[:EDGE]], axis=0)
 
     coupling_ref[...] = along(0)
@@ -284,10 +289,11 @@
     )
 
     entering = jnp.concatenate([entering_ref[:section, :], entering_ref[section:, :]], axis=1)
-    shift = shift_ref[...]
+    keep = unless(first_ref)
+    shift = keep * shift_ref[...]
     inner = slice(EDGE, EDGE + lines)
     decay = joined(decay_ref[...], edge_decay_ref[...])
-    start = jnp.where(first_ref[0, 0] > 0, 0.0, 1.0) * starts_ref[0]
+    start = keep * starts_ref[0]
     base = [joined(start, edge_base_ref[0]), joined(base_ref[...], edge_base_ref[1])]
     last = [base[1][inner] + starts_ref[1], joined(last_ref[...], edge_last_ref[...])]
     passed = decay * entering
@@ -318,7 +324,10 @@
     sections = 2 * near_rows
     f32 = jnp.float32
     place = lax.axis_index("tm").astype(jnp.int32).reshape(1, 1)
-    first = (lax.axis_index("tm") == 0).astype(jnp.int32).reshape(1, 1)
+    row = lax.axis_index("space")
+    first, top, bottom = [
+        flag.astype(jnp.int32).reshape(1, 1) for flag in (lax.axis_index("tm") == 0, row == 0, row == along - 1)
+    ]
 
     def grant(size):
         return pltpu.CompilerParams(vmem_limit_bytes=size * MEBI)
@@ -352,7 +361,7 @@
     ])
 
     with jax.named_scope("halo"):
-        upward = [(i, i + 1) for i in range(along - 1)]
+        upward = [(i, (i + 1) % along) for i in range(along)]
         above = lax.ppermute(up, "space", upward)
         below = lax.ppermute(down, "space", [(j, i) for i, j in upward])
 
@@ -379,16 +388,16 @@
             shape(2 * EDGE, line_len),
             relaxed(2 * EDGE),
         ),
-        in_specs=[SMEM] + [VMEM] * 10,
+        in_specs=[SMEM] * 3 + [VMEM] * 10,
         out_specs=[VMEM] * 7,
         scratch_shapes=[pltpu.VMEM((GROUPS * len(REACH), 2 * SLAB, line_len), f32)],
         compiler_params=grant(20),
         name="edge",
-    )(first, held_starts, held_sources, params, above, below, weights, rates, term, shift, own[0])
+    )(first, top, bottom, held_starts, held_sources, params, above, below, weights, rates, term, shift, own[0])
 
     split = (count, 1, sections * LB // count)
     with jax.named_scope("onward"):
-        shift = lax.ppermute(shift, "tm", [(i, i + 1) for i in range(count - 1)])
+        shift = lax.ppermute(shift, "tm", [(i, (i + 1) % count) for i in range(count)])
     with jax.named_scope("gather_terms"):
         terms = lax.all_to_all(terms.reshape(split), "tm", 0, 0)
     entering = pl.pallas_call(
@@ -408,12 +417,12 @@
             jax.ShapeDtypeStruct((2, 2, near_rows, LB), jnp.bfloat16),
             shape(2, near_rows, LB),
         ),
-        in_specs=[VMEM] * 3,
+        in_specs=[SMEM] * 2 + [VMEM] * 3,
         out_specs=[VMEM] * 3,
         compiler_params=grant(4),
         cost_estimate=pl.CostEstimate(flops=1_000_000_000, bytes_accessed=1_000_000, transcendentals=0),
         name="lines",
-    )(params, above, below)
+    )(top, bottom, params, above, below)
     return pl.pallas_call(
         final_kernel,
         out_shape=shape(GROUPS, STEPS, lines, line_len),

time: 52.6 us -> 49.5 us (0.941)
  starting transfers between devices: 13 us -> 7.5 us
  waiting for transfers between devices: 7.96 us -> 10.3 us
    ppermute x1, waiting for transfers between devices: 3.8 us -> 10.3 us  [shards(): lax.ppermute(shift, 'tm', [(i, (i + 1) % count) for i in range(count)])]
    all_to_all x1, waiting for transfers between devices: 4.15 us -> 0.01 us  [shards(): entering = lax.all_to_all(entering, 'tm', 0, 0)]
    ppermute x1, starting transfers between devices: 3.64 us -> 1.73 us  [shards(): below = lax.ppermute(down, 'space', [(j, i) for i, j in upward])]
    ppermute x1, starting transfers between devices: 1.92 us -> 0.02 us  [shards(): above = lax.ppermute(up, 'space', upward)]
    ppermute x1, starting transfers between devices: 3.59 us -> 1.75 us  [shards(): lax.ppermute(shift, 'tm', [(i, (i + 1) % count) for i in range(count)])]
  transfers between devices with their start and end apart: 4 -> 4, of which waited for: 2 -> 1; matrix products, arithmetic and copies ran while one was open for 0% -> 0% of each run, Pallas kernels for 5% -> 6%
where the time goes in v9:
time: 49.5 us; the launch traced here: 49.2 us
  blocking collectives  22.8 us (46%)
  waiting for transfers between devices  10.3 us (21%)
  Pallas kernels  8.42 us (17%)
  starting transfers between devices  7.5 us (15%)
    all_to_all x1, blocking collectives, shards(): terms = lax.all_to_all(terms.reshape(split), 'tm', 0, 0)  22.8 us
    ppermute x1, waiting for transfers between devices, shards(): lax.ppermute(shift, 'tm', [(i, (i + 1) % count) for i in range(count)])  10.3 us
    all_to_all x1, starting transfers between devices, shards(): entering = lax.all_to_all(entering, 'tm', 0, 0)  3.99 us
    pallas_call x1, Pallas kernels, shards(): pl.pallas_call(own_kernel, out_shape=(*[shape(lines, line_len)] * 5, rela...  2.51 us
    pallas_call x1, Pallas kernels, shards(): pl.pallas_call(edge_kernel, out_shape=(shape(sections, LB), shape(section...  1.77 us
    ppermute x1, starting transfers between devices, shards(): lax.ppermute(shift, 'tm', [(i, (i + 1) % count) for i in range(count)])  1.75 us
    ppermute x1, starting transfers between devices, shards(): below = lax.ppermute(down, 'space', [(j, i) for i, j in upward])  1.73 us
    pallas_call x1, Pallas kernels, shards(): pl.pallas_call(final_kernel, out_shape=shape(GROUPS, STEPS, lines, line_l...  1.64 us
  transfers between devices with their start and end apart: 4, of which 1 were waited for; matrix products, arithmetic and copies ran while one was open for 0% of the time, Pallas kernels for 6%

profile of v9, /device:TPU:8, one launch (start us, length us, event | category | flops | bytes accessed | tf_op | source)
XLA Modules:
  0.0 49.2 jit_solution(1309538514160440685)
XLA Ops:
  0.0 1.6 %pack.1 = (f32[96,256]{1,0:T(8,128)S(1)}, f32[96,256]{1,0:T(8,128)S(1)}, f32[8,128]{1,0:T(8,128)S(1)}, f32[2,128,256]{2,1,0:T(8,128)S(1)}, f32[2,4,128,256]{3,2,...) custom-call(f32[2,128,256]{2,1,0:T(8,128)} %starts_hbm.1, f32[2,4,128,256]{3,2,1,0:T(8,128)} %sources_hbm.1, ...), custom_call_target="tpu_custom_call" | custom-call | tf_op jit(solution)/shard_map/pack/pallas_call | solution.py:339
  1.6 0.0 collective-permute-start
  1.6 1.7 %collective-permute-start.1 = (f32[96,256]{1,0:T(8,128)S(1)}, f32[96,256]{1,0:T(8,128)S(1)}, u32[]{:S(2)}, u32[]{:S(2)}) collective-permute-start(f32[96,256]{1,0:T(8,128)S(1)} %get-tuple-element.32), channel_id=1, source_target_pairs={{1,0},{2,1},{3,2},{4,3},{5,4},{6,5},{7,6},{0,7},{9,8},{10,9},{11,1... | collective-permute-start | bytes 294920 | tf_op jit(solution)/shard_map/halo/ppermute | solution.py:366
  3.3 2.5 %own.1 = (f32[128,256]{1,0:T(8,128)S(1)}, f32[128,256]{1,0:T(8,128)S(1)}, f32[128,256]{1,0:T(8,128)S(1)}, f32[128,256]{1,0:T(8,128)S(1)}, f32[128,256]{1,0:T(8,128)S(1)}, /*index=5*/f32[2,3,128,256]{3,2,1,0:T(8,128)S(1)}) custom-call(s32[1,1]{1,0:T(1,128)} %bitcast.first_ref, f32[2,128,256]{2,1,0:T(8,128)S(1)} %get-tuple-element.28.starts_ref, ...), custom_call_target="tpu_custom_call" | custom-call | flops 5000000000 | bytes 4000000 | tf_op jit(solution)/shard_map/own/pallas_call | solution.py:371
  5.9 0.0 collective-permute-done.above_ref
  5.9 0.0 collective-permute-done.1.below_ref
  5.9 1.8 %edge.1 = (f32[288,128]{1,0:T(8,128)S(1)}, f32[288,128]{1,0:T(8,128)S(1)}, f32[144,256]{1,0:T(8,128)S(1)}, f32[32,256]{1,0:T(8,128)S(1)}, f32[2,32,256]{2,1,0:T(...) custom-call(s32[1,1]{1,0:T(1,128)} %bitcast.first_ref, s32[1,1]{1,0:T(1,128)} %bitcast.2.top_ref, ...), custom_call_target="tpu_custom_call" | custom-call | tf_op jit(solution)/shard_map/edge/pallas_call | solution.py:380
  7.7 0.0 copy-start
  7.7 22.8 %all_to_all.10.terms_ref = f32[32,1,1152]{2,1,0:T(1,128)S(1)} all-to-all(f32[32,1,1152]{2,1,0:T(1,128)S(1)} %bitcast.10), channel_id=1, replica_groups=mesh['tm'=32,'space'=8] {'tm'}, dimensions={0} | all-to-all | bytes 294912 | tf_op jit(solution)/shard_map/gather_terms/all_to_all | solution.py:402
  30.5 0.0 copy-done
  30.5 0.7 %scan.1 = f32[32,1,1152]{2,1,0:T(1,128)} custom-call(s32[1,1]{1,0:T(1,128)} %bitcast.1.place_ref, f32[32,1,1152]{2,1,0:T(1,128)S(1)} %all_to_all.10.terms_ref, f32[32,1,1152]{2,1,0:T(1,128)S(1)} %bitcast.11), custom_call_target="tpu_custom_call" | custom-call | tf_op jit(solution)/shard_map/scan/pallas_call | solution.py:403
  31.2 0.0 copy-start.1
  31.2 4.0 %all-to-all-start.1 = ((f32[32,1,1152]{2,1,0:T(1,128)}), f32[32,1,1152]{2,1,0:T(1,128)S(1)}, u32[]{:S(2)}, u32[]{:S(2)}) async-start(f32[32,1,1152]{2,1,0:T(1,128)} %scan.1), calls=%async_computation.1 | async-start | bytes 294912 | tf_op jit(solution)/shard_map/return_terms/all_to_all | solution.py:412
  35.2 0.0 copy-done.1
  35.3 1.8 %collective-permute-start.2 = (f32[144,256]{1,0:T(8,128)S(1)}, f32[144,256]{1,0:T(8,128)S(1)}, u32[]{:S(2)}, u32[]{:S(2)}) collective-permute-start(f32[144,256]{1,0:T(8,128)S(1)} %copy-done.1), channel_id=1, source_target_pairs={{0,8},{8,16},{16,24},{24,32},{32,40},{40,48},{48,56},{56,64},{64,7... | collective-permute-start | bytes 442376 | tf_op jit(solution)/shard_map/onward/ppermute | solution.py:400
  37.0 0.2 lines.1
  37.2 10.3 %collective-permute-done.2.shift_ref = f32[144,256]{1,0:T(8,128)S(1)} collective-permute-done((f32[144,256]{1,0:T(8,128)S(1)}, f32[144,256]{1,0:T(8,128)S(1)}, u32[]{:S(2)}, u32[]{:S(2)}) %collective-permute-start.2) | collective-permute-done | bytes 147488 | tf_op jit(solution)/shard_map/onward/ppermute | solution.py:400
  47.5 0.0 all-to-all-done.1
  47.5 1.6 %final.1 = f32[2,4,128,256]{3,2,1,0:T(8,128)} custom-call(s32[1,1]{1,0:T(1,128)} %bitcast.first_ref, f32[288,128]{1,0:T(8,128)S(1)} %bitcast.9, f32[144,256]{1,0:T(8,128)S(1)} %collective-permute-done.2.shift_ref, f32[144,128]{1,0:T(8,128)S(1)} %get-tuple-element.41.coupling_ref, bf16[2,2,144,128]{3,2,1,0:T(8,128)(2,1)S(1)} %get-tuple-element.42.masks_ref, ...), custom_call_target="tpu_custom_call" | custom-call | tf_op jit(solution)/shard_map/final/pallas_call | solution.py:426
Async XLA Ops:
  1.6 4.3 %collective-permute-start = (f32[96,256]{1,0:T(8,128)S(1)}, f32[96,256]{1,0:T(8,128)S(1)}, u32[]{:S(2)}, u32[]{:S(2)}) collective-permute-start(f32[96,256]{1,0:T(8,128)S(1)} %get-tuple-element.31), channel_id=1, source_target_pairs={{0,1},{1,2},{2,3},{3,4},{4,5},{5,6},{6,7},{7,0},{8,9},{9,10},{10,1... | collective-permute-start | bytes 294920 | tf_op jit(solution)/shard_map/halo/ppermute | solution.py:365
  1.6 4.3 %collective-permute-start.1 = (f32[96,256]{1,0:T(8,128)S(1)}, f32[96,256]{1,0:T(8,128)S(1)}, u32[]{:S(2)}, u32[]{:S(2)}) collective-permute-start(f32[96,256]{1,0:T(8,128)S(1)} %get-tuple-element.32), channel_id=1, source_target_pairs={{1,0},{2,1},{3,2},{4,3},{5,4},{6,5},{7,6},{0,7},{9,8},{10,9},{11,1... | collective-permute-start | bytes 294920 | tf_op jit(solution)/shard_map/halo/ppermute | solution.py:366
  7.7 22.9 %copy-start = (f32[144,256]{1,0:T(8,128)}, f32[144,256]{1,0:T(8,128)S(1)}, u32[]{:S(2)}) copy-start(f32[144,256]{1,0:T(8,128)S(1)} %get-tuple-element.40) | copy-start | bytes 442372
  31.2 4.0 %copy-start.1 = (f32[144,256]{1,0:T(8,128)S(1)}, f32[144,256]{1,0:T(8,128)}, u32[]{:S(2)}) copy-start(f32[144,256]{1,0:T(8,128)} %copy-done) | copy-start | bytes 442372
  31.2 16.3 %all-to-all-start.1 = ((f32[32,1,1152]{2,1,0:T(1,128)}), f32[32,1,1152]{2,1,0:T(1,128)S(1)}, u32[]{:S(2)}, u32[]{:S(2)}) async-start(f32[32,1,1152]{2,1,0:T(1,128)} %scan.1), calls=%async_computation.1 | async-start | bytes 294912 | tf_op jit(solution)/shard_map/return_terms/all_to_all | solution.py:412
  35.3 12.3 %collective-permute-start.2 = (f32[144,256]{1,0:T(8,128)S(1)}, f32[144,256]{1,0:T(8,128)S(1)}, u32[]{:S(2)}, u32[]{:S(2)}) collective-permute-start(f32[144,256]{1,0:T(8,128)S(1)} %copy-done.1), channel_id=1, source_target_pairs={{0,8},{8,16},{16,24},{24,32},{32,40},{40,48},{48,56},{56,64},{64,7... | collective-permute-start | bytes 442376 | tf_op jit(solution)/shard_map/onward/ppermute | solution.py:400

commit v10 on v9

--- a/solution.py
+++ b/solution.py
@@ -105,7 +105,6 @@
     return dict(
         term=resid + ahead - held,
         shift=ends[1] - ahead,
-        decay=decay,
         bases=(jnp.where(first > 0, jnp.zeros_like(linear), starts[0]), change - linear),
         last=ends[1] + resid - held,
     )
@@ -159,7 +158,7 @@
 
 def own_kernel(
     first_ref, starts_ref, sources_ref, params_ref, weights_ref, rates_ref,
-    term_ref, shift_ref, decay_ref, base_ref, last_ref, relaxed_ref,
+    term_ref, shift_ref, base_ref, last_ref, relaxed_ref,
 ):
     coupling, *categories = [columns(params_ref[row : row + 1, :]) for row in range(3)]
     coupling = jnp.concatenate([coupling, coupling], axis=1)
@@ -173,7 +172,6 @@
     )
     term_ref[...] = out["term"]
     shift_ref[...] = out["shift"]
-    decay_ref[...] = out["decay"]
     base_ref[...] = out["bases"][1]
     last_ref[...] = out["last"]
 
@@ -189,8 +187,8 @@
 
 def edge_kernel(
     first_ref, top_ref, bottom_ref, starts_ref, sources_ref, params_ref, above_ref, below_ref, weights_ref, rates_ref,
-    own_term_ref, own_shift_ref, own_decay_ref,
-    terms_ref, factors_ref, shift_ref, decay_ref, base_ref, last_ref, relaxed_ref, halo_ref,
+    own_term_ref, own_shift_ref,
+    terms_ref, shift_ref, base_ref, last_ref, relaxed_ref, halo_ref,
 ):
     lines = starts_ref.shape[1]
     lane = lax.broadcasted_iota(jnp.int32, (8, LB), 1)
@@ -234,22 +232,19 @@
 
     out = relaxations(starts, sources, coupling, categories, weights_ref[...], rates_ref, first_ref[0, 0], relaxed_to)
     section = lines + 2 * EDGE
-    end_decay = ends_of(out["decay"], EDGE)
-    decay = joined(own_decay_ref[...], end_decay)
     term = joined(own_term_ref[...], ends_of(out["term"], EDGE))
     for block in range(2):
         at = block * section
         lanes = slice(block * LB, (block + 1) * LB)
         terms_ref[at : at + section, :] = term[:, lanes]
-        factors_ref[at : at + section, :] = (decay * decay)[:, lanes]
     shift_ref[...] = joined(own_shift_ref[...], ends_of(out["shift"], EDGE))
-    decay_ref[...] = end_decay
     for g in range(GROUPS):
         base_ref[g] = ends_of(out["bases"][g], EDGE)
     last_ref[...] = ends_of(out["last"], 0)
 
 
-def scan_kernel(place_ref, terms_ref, factors_ref, entering_ref):
+def scan_kernel(place_ref, terms_ref, factors_ref, shift_ref, entering_ref):
+    del shift_ref
     factor = factors_ref[place_ref[0, 0]]
     carried = jnp.zeros_like(factor)
     for d in range(terms_ref.shape[0]):
@@ -257,7 +252,10 @@
         carried = factor * carried + terms_ref[d]
 
 
-def lines_kernel(top_ref, bottom_ref, params_ref, above_ref, below_ref, coupling_ref, masks_ref, upper_ref):
+def lines_kernel(
+    top_ref, bottom_ref, params_ref, above_ref, below_ref, rates_ref,
+    coupling_ref, masks_ref, upper_ref, decay_ref, factors_ref,
+):
     lines = params_ref.shape[1]
     at = GROUPS * GROUP_ROWS
 
@@ -268,16 +266,22 @@
         return jnp.concatenate([above[lines - EDGE :], own, below[:EDGE]], axis=0)
 
     coupling_ref[...] = along(0)
-    even, odd, upper = class_masks([along(1), along(2)])
+    categories = [along(1), along(2)]
+    even, odd, upper = class_masks(categories)
+    decay = jnp.exp(-rates_of(categories, rates_ref))
+    decay_ref[...] = decay
     for block in range(2):
+        section = lines + 2 * EDGE
+        lanes = slice(block * LB, (block + 1) * LB)
+        factors_ref[block * section : (block + 1) * section, :] = (decay * decay)[:, lanes]
         masks_ref[0, block] = even[block]
         masks_ref[1, block] = odd[block]
         upper_ref[block] = jnp.where(upper[block], 1.0, 0.0)
 
 
 def final_kernel(
-    first_ref, entering_ref, shift_ref, coupling_ref, masks_ref, upper_ref, weights_ref, starts_ref,
-    decay_ref, base_ref, last_ref, relaxed_ref, edge_decay_ref, edge_base_ref, edge_last_ref, edge_relaxed_ref, states_hbm, states_ref, sems,
+    first_ref, entering_ref, shift_ref, coupling_ref, masks_ref, upper_ref, decay_ref, weights_ref, starts_ref,
+    base_ref, last_ref, relaxed_ref, edge_base_ref, edge_last_ref, edge_relaxed_ref, states_hbm, states_ref, sems,
 ):
     lines = last_ref.shape[0]
     section = lines + 2 * EDGE
@@ -292,7 +296,7 @@
     keep = unless(first_ref)
     shift = keep * shift_ref[...]
     inner = slice(EDGE, EDGE + lines)
-    decay = joined(decay_ref[...], edge_decay_ref[...])
+    decay = decay_ref[...]
     start = keep * starts_ref[0]
     base = [joined(start, edge_base_ref[0]), joined(base_ref[...], edge_base_ref[1])]
     last = [base[1][inner] + starts_ref[1], joined(last_ref[...], edge_last_ref[...])]
@@ -370,63 +374,63 @@
 
     term, shift, *own = pl.pallas_call(
         own_kernel,
-        out_shape=(*[shape(lines, line_len)] * 5, relaxed(lines)),
+        out_shape=(*[shape(lines, line_len)] * 4, relaxed(lines)),
         in_specs=[SMEM] + [VMEM] * 5,
-        out_specs=[VMEM] * 6,
+        out_specs=[VMEM] * 5,
         compiler_params=grant(24),
         cost_estimate=pl.CostEstimate(flops=5_000_000_000, bytes_accessed=4_000_000, transcendentals=0),
         name="own",
     )(first, held_starts, held_sources, params, weights, rates)
-    terms, factors, shift, *edges = pl.pallas_call(
+    terms, shift, *edges = pl.pallas_call(
         edge_kernel,
         out_shape=(
             shape(sections, LB),
-            shape(sections, LB),
             shape(near_rows, line_len),
-            shape(4 * EDGE, line_len),
             shape(GROUPS, 4 * EDGE, line_len),
             shape(2 * EDGE, line_len),
             relaxed(2 * EDGE),
         ),
-        in_specs=[SMEM] * 3 + [VMEM] * 10,
-        out_specs=[VMEM] * 7,
+        in_specs=[SMEM] * 3 + [VMEM] * 9,
+        out_specs=[VMEM] * 5,
         scratch_shapes=[pltpu.VMEM((GROUPS * len(REACH), 2 * SLAB, line_len), f32)],
         compiler_params=grant(20),
         name="edge",
-    )(first, top, bottom, held_starts, held_sources, params, above, below, weights, rates, term, shift, own[0])
+    )(first, top, bottom, held_starts, held_sources, params, above, below, weights, rates, term, shift)
 
     split = (count, 1, sections * LB // count)
     with jax.named_scope("onward"):
         shift = lax.ppermute(shift, "tm", [(i, (i + 1) % count) for i in range(count)])
     with jax.named_scope("gather_terms"):
         terms = lax.all_to_all(terms.reshape(split), "tm", 0, 0)
-    entering = pl.pallas_call(
-        scan_kernel,
-        out_shape=shape(*split),
-        in_specs=[SMEM] + [VMEM] * 2,
-        out_specs=VMEM,
-        compiler_params=grant(4),
-        name="scan",
-    )(place, terms, factors.reshape(split))
-    with jax.named_scope("return_terms"):
-        entering = lax.all_to_all(entering, "tm", 0, 0)
-    spread_lines = pl.pallas_call(
+    *spread_lines, factors = pl.pallas_call(
         lines_kernel,
         out_shape=(
             shape(near_rows, LB),
             jax.ShapeDtypeStruct((2, 2, near_rows, LB), jnp.bfloat16),
             shape(2, near_rows, LB),
+            shape(near_rows, line_len),
+            shape(sections, LB),
         ),
-        in_specs=[SMEM] * 2 + [VMEM] * 3,
-        out_specs=[VMEM] * 3,
+        in_specs=[SMEM] * 2 + [VMEM] * 4,
+        out_specs=[VMEM] * 5,
         compiler_params=grant(4),
         cost_estimate=pl.CostEstimate(flops=1_000_000_000, bytes_accessed=1_000_000, transcendentals=0),
         name="lines",
-    )(top, bottom, params, above, below)
+    )(top, bottom, params, above, below, rates)
+    entering = pl.pallas_call(
+        scan_kernel,
+        out_shape=shape(*split),
+        in_specs=[SMEM] + [VMEM] * 3,
+        out_specs=VMEM,
+        compiler_params=grant(4),
+        name="scan",
+    )(place, terms, factors.reshape(split), shift)
+    with jax.named_scope("return_terms"):
+        entering = lax.all_to_all(entering, "tm", 0, 0)
     return pl.pallas_call(
         final_kernel,
         out_shape=shape(GROUPS, STEPS, lines, line_len),
-        in_specs=[SMEM] + [VMEM] * 15,
+        in_specs=[SMEM] + [VMEM] * 14,
         out_specs=HBM,
         scratch_shapes=[
             pltpu.VMEM((GROUPS, STEPS, lines, line_len), f32),

time: 49.5 us -> 50.4 us (1.018)
  starting transfers between devices: 7.5 us -> 14.9 us
  blocking collectives: 22.8 us -> 15.8 us
  waiting for transfers between devices: 10.3 us -> 10.9 us
    all_to_all x1, starting transfers between devices: 3.99 us -> 11.3 us  [shards(): terms = lax.all_to_all(terms.reshape(split), 'tm', 0, 0)]
    all_to_all x1, blocking collectives: 22.8 us -> 15.8 us  [shards(): entering = lax.all_to_all(entering, 'tm', 0, 0)]
    pallas_call x2, Pallas kernels: 4.28 us -> 4.94 us  [the longest x1 2.5 us: shards(): pl.pallas_call(own_kernel, out_shape=(*[shape(lines, line_len)] * 4, rela...]
    pallas_call x1, Pallas kernels: 0.73 us -> 0.07 us  [shards(): pl.pallas_call(scan_kernel, out_shape=shape(*split), in_specs=[SMEM] + [V...]
    ppermute x1, waiting for transfers between devices: 10.3 us -> 10.9 us  [shards(): lax.ppermute(shift, 'tm', [(i, (i + 1) % count) for i in range(count)])]
  transfers between devices with their start and end apart: 4 -> 4, of which waited for: 1 -> 1; matrix products, arithmetic and copies ran while one was open for 0% -> 0% of each run, Pallas kernels for 6% -> 5%
where the time goes in v10:
time: 50.4 us; the launch traced here: 50.2 us
  blocking collectives  15.8 us (31%)
  starting transfers between devices  14.9 us (30%)
  waiting for transfers between devices  10.9 us (22%)
  Pallas kernels  8.43 us (17%)
    all_to_all x1, blocking collectives, shards(): entering = lax.all_to_all(entering, 'tm', 0, 0)  15.8 us
    all_to_all x1, starting transfers between devices, shards(): terms = lax.all_to_all(terms.reshape(split), 'tm', 0, 0)  11.3 us
    ppermute x1, waiting for transfers between devices, shards(): lax.ppermute(shift, 'tm', [(i, (i + 1) % count) for i in range(count)])  10.9 us
    pallas_call x1, Pallas kernels, shards(): pl.pallas_call(own_kernel, out_shape=(*[shape(lines, line_len)] * 4, rela...  2.5 us
    pallas_call x1, Pallas kernels, shards(): pl.pallas_call(edge_kernel, out_shape=(shape(sections, LB), shape(near_ro...  2.44 us
    ppermute x1, starting transfers between devices, shards(): lax.ppermute(shift, 'tm', [(i, (i + 1) % count) for i in range(count)])  1.87 us
    ppermute x1, starting transfers between devices, shards(): below = lax.ppermute(down, 'space', [(j, i) for i, j in upward])  1.73 us
    pallas_call x1, Pallas kernels, shards(): pl.pallas_call(final_kernel, out_shape=shape(GROUPS, STEPS, lines, line_l...  1.63 us
  transfers between devices with their start and end apart: 4, of which 1 were waited for; matrix products, arithmetic and copies ran while one was open for 0% of the time, Pallas kernels for 5%

profile of v10, /device:TPU:8, one launch (start us, length us, event | category | flops | bytes accessed | tf_op | source)
XLA Modules:
  0.0 50.2 jit_solution(15212971329247304963)
XLA Ops:
  0.0 1.6 %pack.1 = (f32[96,256]{1,0:T(8,128)S(1)}, f32[96,256]{1,0:T(8,128)S(1)}, f32[8,128]{1,0:T(8,128)S(1)}, f32[2,128,256]{2,1,0:T(8,128)S(1)}, f32[2,4,128,256]{3,2,...) custom-call(f32[2,128,256]{2,1,0:T(8,128)} %starts_hbm.1, f32[2,4,128,256]{3,2,1,0:T(8,128)} %sources_hbm.1, ...), custom_call_target="tpu_custom_call" | custom-call | tf_op jit(solution)/shard_map/pack/pallas_call | solution.py:343
  1.6 0.0 collective-permute-start
  1.6 1.7 %collective-permute-start.1 = (f32[96,256]{1,0:T(8,128)S(1)}, f32[96,256]{1,0:T(8,128)S(1)}, u32[]{:S(2)}, u32[]{:S(2)}) collective-permute-start(f32[96,256]{1,0:T(8,128)S(1)} %get-tuple-element.31), channel_id=1, source_target_pairs={{1,0},{2,1},{3,2},{4,3},{5,4},{6,5},{7,6},{0,7},{9,8},{10,9},{11,1... | collective-permute-start | bytes 294920 | tf_op jit(solution)/shard_map/halo/ppermute | solution.py:370
  3.3 2.5 %own.1 = (f32[128,256]{1,0:T(8,128)S(1)}, f32[128,256]{1,0:T(8,128)S(1)}, f32[128,256]{1,0:T(8,128)S(1)}, f32[128,256]{1,0:T(8,128)S(1)}, f32[2,3,128,256]{3,2,1,0:T(8,128)S(1)}) custom-call(s32[1,1]{1,0:T(1,128)} %bitcast.first_ref, f32[2,128,256]{2,1,0:T(8,128)S(1)} %get-tuple-element.27.starts_ref, f32[2,4,128,256]{3,2,1,0:T(8,128)S(1)} %get-tuple-element.28.sources_ref, ...), custom_call_target="tpu_custom_call" | custom-call | flops 5000000000 | bytes 4000000 | tf_op jit(solution)/shard_map/own/pallas_call | solution.py:375
  5.8 0.0 collective-permute-done.above_ref
  5.9 0.0 collective-permute-done.1.below_ref
  5.9 2.4 %edge.1 = (f32[288,128]{1,0:T(8,128)}, f32[144,256]{1,0:T(8,128)S(1)}, f32[2,32,256]{2,1,0:T(8,128)S(1)}, f32[16,256]{1,0:T(8,128)S(1)}, f32[2,3,16,256]{3,2,1,0:T(8,128)S(1)}) custom-call(s32[1,1]{1,0:T(1,128)} %bitcast.first_ref, s32[1,1]{1,0:T(1,128)} %bitcast.2.top_ref, s32[1,1]{1,0:T(1,128)} %bitcast.3.bottom_ref, ...), custom_call_target="tpu_custom_call" | custom-call | tf_op jit(solution)/shard_map/edge/pallas_call | solution.py:384
  8.3 11.3 %all-to-all-start = ((f32[32,1,1152]{2,1,0:T(1,128)}), f32[32,1,1152]{2,1,0:T(1,128)S(1)}, u32[]{:S(2)}, u32[]{:S(2)}) async-start(f32[32,1,1152]{2,1,0:T(1,128)} %bitcast.6), calls=%async_computation | async-start | bytes 294912 | tf_op jit(solution)/shard_map/gather_terms/all_to_all | solution.py:404
  19.6 1.9 %collective-permute-start.2 = (f32[144,256]{1,0:T(8,128)S(1)}, f32[144,256]{1,0:T(8,128)S(1)}, u32[]{:S(2)}, u32[]{:S(2)}) collective-permute-start(f32[144,256]{1,0:T(8,128)S(1)} %get-tuple-element.38), channel_id=1, source_target_pairs={{0,8},{8,16},{16,24},{24,32},{32,40},{40,48},{48,56},{56,64},{64,7... | collective-permute-start | bytes 442376 | tf_op jit(solution)/shard_map/onward/ppermute | solution.py:402
  21.5 0.2 lines.1
  21.7 10.9 %collective-permute-done.2.shift_ref = f32[144,256]{1,0:T(8,128)S(1)} collective-permute-done((f32[144,256]{1,0:T(8,128)S(1)}, f32[144,256]{1,0:T(8,128)S(1)}, u32[]{:S(2)}, u32[]{:S(2)}) %collective-permute-start.2) | collective-permute-done | bytes 147488 | tf_op jit(solution)/shard_map/onward/ppermute | solution.py:402
  32.6 0.0 all-to-all-done.terms_ref
  32.6 0.1 scan.1
  32.7 15.8 %all_to_all.10 = f32[32,1,1152]{2,1,0:T(1,128)S(1)} all-to-all(f32[32,1,1152]{2,1,0:T(1,128)S(1)} %scan.1), channel_id=1, replica_groups=mesh['tm'=32,'space'=8] {'tm'}, dimensions={0} | all-to-all | bytes 294912 | tf_op jit(solution)/shard_map/return_terms/all_to_all | solution.py:429
  48.5 1.6 %final.1 = f32[2,4,128,256]{3,2,1,0:T(8,128)} custom-call(s32[1,1]{1,0:T(1,128)} %bitcast.first_ref, f32[288,128]{1,0:T(8,128)S(1)} %bitcast.9, f32[144,256]{1,0:T(8,128)S(1)} %collective-permute-done.2.shift_ref, f32[144,128]{1,0:T(8,128)S(1)} %get-tuple-element.39.coupling_ref, bf16[2,2,144,128]{3,2,1,0:T(8,128)(2,1)S(1)} %get-tuple-element.40.masks_ref, ...), custom_call_target="tpu_custom_call" | custom-call | tf_op jit(solution)/shard_map/final/pallas_call | solution.py:430
Async XLA Ops:
  1.6 4.3 %collective-permute-start = (f32[96,256]{1,0:T(8,128)S(1)}, f32[96,256]{1,0:T(8,128)S(1)}, u32[]{:S(2)}, u32[]{:S(2)}) collective-permute-start(f32[96,256]{1,0:T(8,128)S(1)} %get-tuple-element.30), channel_id=1, source_target_pairs={{0,1},{1,2},{2,3},{3,4},{4,5},{5,6},{6,7},{7,0},{8,9},{9,10},{10,1... | collective-permute-start | bytes 294920 | tf_op jit(solution)/shard_map/halo/ppermute | solution.py:369
  1.6 4.3 %collective-permute-start.1 = (f32[96,256]{1,0:T(8,128)S(1)}, f32[96,256]{1,0:T(8,128)S(1)}, u32[]{:S(2)}, u32[]{:S(2)}) collective-permute-start(f32[96,256]{1,0:T(8,128)S(1)} %get-tuple-element.31), channel_id=1, source_target_pairs={{1,0},{2,1},{3,2},{4,3},{5,4},{6,5},{7,6},{0,7},{9,8},{10,9},{11,1... | collective-permute-start | bytes 294920 | tf_op jit(solution)/shard_map/halo/ppermute | solution.py:370
  8.3 24.3 %all-to-all-start = ((f32[32,1,1152]{2,1,0:T(1,128)}), f32[32,1,1152]{2,1,0:T(1,128)S(1)}, u32[]{:S(2)}, u32[]{:S(2)}) async-start(f32[32,1,1152]{2,1,0:T(1,128)} %bitcast.6), calls=%async_computation | async-start | bytes 294912 | tf_op jit(solution)/shard_map/gather_terms/all_to_all | solution.py:404
  19.6 13.0 %collective-permute-start.2 = (f32[144,256]{1,0:T(8,128)S(1)}, f32[144,256]{1,0:T(8,128)S(1)}, u32[]{:S(2)}, u32[]{:S(2)}) collective-permute-start(f32[144,256]{1,0:T(8,128)S(1)} %get-tuple-element.38), channel_id=1, source_target_pairs={{0,8},{8,16},{16,24},{24,32},{32,40},{40,48},{48,56},{56,64},{64,7... | collective-permute-start | bytes 442376 | tf_op jit(solution)/shard_map/onward/ppermute | solution.py:402
